TPU v7x, 128 devices: a whole 4x4x4 slice. The times are simulated.
128 devices in a mesh: dom: 16 (over z, x), sub: 8 (over y, core).
Axes of the slice: x: 4, y: 4, z: 4, core: 2. Of those that a mesh axis runs over, the one named last changes fastest.
Arguments:
- tile_blocks: bfloat16 [2048, 18, 192, 192], P(('dom', 'sub')), may hold values from -0.109375 to 0.109375
- neighbours: int32 [2048, 18], P(('dom', 'sub')), may hold values from 0 to 47
- send_groups: int32 [4096], P(('dom', 'sub')), may hold values from 0 to 15
- block_x: float32 [393216, 64], P(('dom', 'sub')), may hold values from -6 to 6
- block_p: float32 [393216, 64], P(('dom', 'sub')), may hold values from -6 to 6
Outputs:
- basis: float32 [393216, 192], P(('dom', 'sub'))
- basis_image: float32 [393216, 192], P(('dom', 'sub'))
- projected: float32 [192, 192], replicated
Inputs may be any that keep to these rules, and one draw needn't show every extreme that they name: `neighbours`: each entry indexes the owner's extended group list of 48 entries. `send_groups`: local group indices, 16 for the previous device then 16 for the next, per device.
All inputs are finite; a program needn't handle non-finite values.
Results may differ from a plain program's by a relative error of at most 0.0003.
The roundings to bfloat16 on the way count: a program that leaves them out, or rounds other values in their place, can miss the bound.
Values may be sent and summed in bfloat16 or wider, within the bound.
No kernel may reach another device: no remote copies, remote signals or barrier semaphores. Data moves between devices by JAX's collectives and lax.ppermute only.
A program may use at most 128 MiB of HBM per device.

v0:
```python
import jax
import jax.numpy as jnp
from jax import lax
from jax.sharding import PartitionSpec as P


def extended_2(cells, sides, width):
    for axis, dim in sides:
        count = lax.axis_size(axis)
        ends = count - 1
        head = lax.slice_in_dim(cells, 0, width, axis=dim)
        tail = lax.slice_in_dim(cells, cells.shape[dim] - width, cells.shape[dim], axis=dim)
        cells = jnp.concatenate(
            [
                lax.ppermute(tail, axis, [(i, (i + 1) % count) for i in range(ends)]),
                cells,
                lax.ppermute(head, axis, [((i + 1) % count, i) for i in range(ends)]),
            ],
            axis=dim,
        )
    return cells


def gather_rims(local, send_groups):
    count = local.shape[0]
    return jnp.concatenate([local[send_groups[:count]], local[send_groups[count:]]], 0)


def widen(rims, local):
    count = local.shape[0]
    return jnp.concatenate([rims[:count], local, rims[3 * count :]], 0)


def apply_tiles(tile_blocks, neighbours, extended):
    picked = extended[neighbours]
    return jnp.einsum("gkij,gkjc->gic", tile_blocks, picked, preferred_element_type=jnp.float32)


def shards(tile_blocks, neighbours, send_groups, block_x, block_p):
    highest = lax.Precision.HIGHEST
    count = tile_blocks.shape[0]
    degrees = tile_blocks.shape[2]
    columns = block_x.shape[1]
    local_rows = count * degrees
    total = jnp.float32(local_rows * lax.axis_size("dom") * lax.axis_size("sub"))
    x_local = block_x.astype(jnp.bfloat16).reshape(count, degrees, columns)
    x_rims = extended_2(gather_rims(x_local, send_groups), ((("dom", "sub"), 0),), count)
    image_local = apply_tiles(tile_blocks, neighbours, widen(x_rims, x_local))
    x_image = image_local.reshape(local_rows, columns)
    x_gram, x_cross = lax.psum(
        (
            jnp.dot(block_x.T, block_x, precision=highest),
            jnp.dot(block_x.T, x_image, precision=highest),
        ),
        ("dom", "sub"),
    )
    factor = jnp.linalg.cholesky(x_gram)
    quotient = jax.scipy.linalg.cho_solve((factor, True), x_cross)
    residual = x_image - jnp.dot(block_x, quotient, precision=highest)
    stacked = (
        jnp.concatenate([residual, block_p], 1)
        .astype(jnp.bfloat16)
        .reshape(count, degrees, 2 * columns)
    )
    stacked_rims = extended_2(gather_rims(stacked, send_groups), ((("dom", "sub"), 0),), count)
    rp_local = apply_tiles(tile_blocks, neighbours, widen(stacked_rims, stacked))
    rp_image = rp_local.reshape(local_rows, 2 * columns)
    search = jnp.concatenate([block_x, residual, block_p], 1)
    search_image = jnp.concatenate([x_image, rp_image], 1)
    width = search.shape[1]
    gram_sum = lax.psum(jnp.dot(search.T, search, precision=highest), ("dom", "sub"))
    lower = jnp.linalg.cholesky(gram_sum / total)
    inverse = jax.scipy.linalg.solve_triangular(
        lower, jnp.eye(width, dtype=jnp.float32), lower=True
    )
    basis = jnp.dot(search, inverse.T, precision=highest)
    basis_image = jnp.dot(search_image, inverse.T, precision=highest)
    projected = lax.psum(jnp.dot(basis.T, basis_image, precision=highest), ("dom", "sub")) / total
    return (basis, basis_image, projected)


def solution(mesh):
    placed = (
        P(("dom", "sub"), None, None, None),
        P(("dom", "sub"), None),
        P(("dom", "sub")),
        P(("dom", "sub"), None),
        P(("dom", "sub"), None),
    )
    return jax.shard_map(
        shards,
        mesh=mesh,
        in_specs=placed,
        out_specs=(P(("dom", "sub"), None), P(("dom", "sub"), None), P()),
        check_vma=False,
    )
```

profile of v0, /device:TPU:1, one launch (start us, length us, event | category | flops | bytes accessed | tf_op | source)
XLA Modules:
  0.0 538.7 jit_solution(1182653515284058217)
XLA Ops:
  9.9 4.7 collective-permute-start
  15.2 1.9 collective-permute-start.1
  21.2 4.7 collective-permute-done.1
  27.3 10.4 %gather_fusion.2 = bf16[288,192,64]{1,2,0:T(8,128)(2,1)} fusion(bf16[48,192,64]{1,2,0:T(8,128)(2,1)S(1)} %pad_maximum_fusion.4, s32[1024]{0:T(1024)S(1)} %pad_clamp_fusion), kind=kCustom, calls=%fused_computation.2 | custom fusion | bytes 14156928 | tf_op jit(solution)/shard_map/gather | solution.py:35
  37.7 15.5 %convolution_bitcast_fusion.1 = f32[16,192,64]{1,2,0:T(8,128)S(1)} fusion(bf16[16,18,192,64]{2,3,1,0:T(8,128)(2,1)} %bitcast.75, bf16[16,18,192,192]{3,2,1,0:T(8,128)(2,1)} %param.5), kind=kOutput, calls=%fused_computation.17 | convolution fusion | flops 1358954496 | bytes 29097984 | tf_op jit(solution)/shard_map/gkij,gkjc->gic/dot_general | solution.py:36
  55.0 70.7 %all-reduce.3 = (f32[64,64]{0,1:T(8,128)S(1)}, f32[64,64]{0,1:T(8,128)S(1)}) all-reduce(f32[64,64]{0,1:T(8,128)S(1)} %convolution_bitcast_fusion.2, f32[64,64]{0,1:T(8,128)S(1)} %copy-done.13), channel_id=1, replica_groups=mesh['dom'=16,'sub'=8] {'dom','sub'}, use_global_device_ids=true, to_apply=%region_3.4 | all-reduce | flops 8192 | bytes 65536 | tf_op jit(solution)/shard_map/psum | solution.py:50
  125.8 5.8 %cholesky.58 = f32[64,64]{1,0:T(8,128)S(1)} custom-call(f32[64,64]{1,0:T(8,128)S(1)} %fusion.21), custom_call_target="Cholesky" | custom-call | tf_op jit(solution)/shard_map/jit(cholesky)/cholesky | solution.py:57
  133.0 4.9 custom-call.25
  138.3 1.7 fusion.25
  141.2 4.2 fusion.6
  151.9 3.4 collective-permute-start.2
  155.3 2.5 collective-permute-start.3
  157.8 128.4 %all-reduce.7.cloned.1.call-done = f32[192,192]{0,1:T(8,128)} async-done(((f32[192,192]{0,1:T(8,128)}), f32[192,192]{0,1:T(8,128)}) %all-reduce.7.cloned.1.call-update) | async-done | bytes 147472 | tf_op jit(solution)/shard_map/psum | solution.py:71
  288.3 11.7 %cholesky.119 = f32[128,128]{1,0:T(8,128)S(1)} custom-call(f32[128,128]{1,0:T(8,128)S(1)} %cholesky.149), custom_call_target="Cholesky" | custom-call | tf_op jit(solution)/shard_map/jit(cholesky)/cholesky | solution.py:72
  300.0 9.8 %custom-call.26 = f32[1,128,128]{1,2,0:T(8,128)S(1)} custom-call(f32[1,128,128]{2,1,0:T(8,128)S(1)} %get-tuple-element.35), custom_call_target="InvertDiagBlocksLowerTriangular" | custom-call | tf_op jit(solution)/shard_map/jit(cholesky)/cholesky | solution.py:72
  311.8 5.8 %cholesky.136 = f32[64,64]{1,0:T(8,128)S(1)} custom-call(f32[64,64]{1,0:T(8,128)S(1)} %convolution_subtract_fusion.1), custom_call_target="Cholesky" | custom-call | tf_op jit(solution)/shard_map/jit(cholesky)/cholesky | solution.py:72
  321.8 21.2 %custom-call.27 = f32[2,128,128]{1,2,0:T(8,128)} custom-call(f32[2,128,128]{2,1,0:T(8,128)} %pad_maximum_fusion.9), custom_call_target="InvertDiagBlocksLowerTriangular" | custom-call | tf_op jit(solution)/shard_map/jit(_solve_triangular)/triangular_solve | solution.py:73
  346.3 3.7 fusion.5
  350.0 1.9 pad_maximum_fusion.1
  351.9 12.2 %gather_fusion.5 = bf16[288,192,128]{2,1,0:T(8,128)(2,1)} fusion(bf16[48,192,128]{2,1,0:T(8,128)(2,1)S(1)} %pad_maximum_fusion.1, s32[1024]{0:T(1024)S(1)} %pad_clamp_fusion), kind=kCustom, calls=%fused_computation.5 | custom fusion | bytes 28312704 | tf_op jit(solution)/shard_map/gather | solution.py:35
  364.1 16.7 %fusion.28 = f32[16,128,192,1]{1,2,3,0:T(8,128)S(1)} fusion(bf16[16,18,192,192]{3,2,1,0:T(8,128)(2,1)} %param.5, bf16[16,18,192,128]{3,2,1,0:T(8,128)(2,1)} %bitcast.76), kind=kOutput, calls=%fused_computation.79 | convolution fusion | flops 2717908992 | bytes 36962304 | tf_op jit(solution)/shard_map/gkij,gkjc->gic/dot_general | solution.py:36
  380.9 3.9 fusion.1
  386.2 2.7 fusion.27
  389.0 140.9 %all-reduce.9.cloned.1.call-done = f32[192,192]{0,1:T(8,128)} async-done(((f32[192,192]{0,1:T(8,128)}), f32[192,192]{0,1:T(8,128)}) %all-reduce.9.cloned.1.call-update) | async-done | bytes 147472 | tf_op jit(solution)/shard_map/psum | solution.py:78
  (94 shorter events, 33.2 us)
Async XLA Ops:
  7.2 2.0 copy-start.16
  7.2 279.0 %all-reduce.7.cloned.1.call-start = ((), (), s32[]{:S(2)}) async-start(), calls=%async_computation | async-start | bytes 393216 | tf_op jit(solution)/shard_map/psum | solution.py:71
  9.0 8.8 %copy-start.14 = (s32[16,18]{1,0:T(8,128)S(1)}, s32[16,18]{1,0:T(8,128)}, u32[]{:S(2)}) copy-start(s32[16,18]{1,0:T(8,128)} %param.6) | copy-start | bytes 3460
  9.0 8.9 %copy-start.7 = (f32[3072,64]{0,1:T(8,128)S(1)}, f32[3072,64]{0,1:T(8,128)}, u32[]{:S(2)}) copy-start(f32[3072,64]{0,1:T(8,128)} %param.9) | copy-start | bytes 2359300
  9.9 9.9 %copy-start = (f32[3072,64]{0,1:T(8,128)S(1)}, f32[3072,64]{0,1:T(8,128)}, u32[]{:S(2)}) copy-start(f32[3072,64]{0,1:T(8,128)} %param.8) | copy-start | bytes 2359300
  9.9 11.3 %collective-permute-start = (bf16[16,192,64]{1,2,0:T(8,128)(2,1)S(1)}, bf16[16,192,64]{1,2,0:T(8,128)(2,1)}, u32[]{:S(2)}, u32[]{:S(2)}) collective-permute-start(bf16[16,192,64]{1,2,0:T(8,128)(2,1)S(1)} %gather_fusion), channel_id=1, source_target_pairs={{0,1},{1,2},{2,3},{3,4},{4,5},{5,6},{6,7},{7,8},{8,9},{9,10},{10,1... | collective-permute-start | bytes 1179656 | tf_op jit(solution)/shard_map/ppermute | solution.py:15
  14.6 2.5 copy-start.15
  15.2 10.6 %collective-permute-start.1 = (bf16[16,192,64]{1,2,0:T(8,128)(2,1)S(1)}, bf16[16,192,64]{1,2,0:T(8,128)(2,1)}, u32[]{:S(2)}, u32[]{:S(2)}) collective-permute-start(bf16[16,192,64]{1,2,0:T(8,128)(2,1)S(1)} %gather_fusion.1), channel_id=1, source_target_pairs={{1,0},{2,1},{3,2},{4,3},{5,4},{6,5},{7,6},{8,7},{9,8},{10,9},{11,1... | collective-permute-start | bytes 1179656 | tf_op jit(solution)/shard_map/ppermute | solution.py:17
  53.2 1.8 copy-start.13
  55.0 86.2 %copy-start.8 = (f32[3072,64]{0,1:T(8,128)S(1)}, f32[3072,64]{0,1:T(8,128)}, u32[]{:S(2)}) copy-start(f32[3072,64]{0,1:T(8,128)} %param.9) | copy-start | bytes 2359300
  140.0 5.5 %copy-start.3 = (bf16[3072,64]{1,0:T(8,128)(2,1)S(1)}, bf16[3072,64]{1,0:T(8,128)(2,1)}, u32[]{:S(2)}) copy-start(bf16[3072,64]{1,0:T(8,128)(2,1)} %copy.38) | copy-start | bytes 1179652
  145.5 384.4 %all-reduce.9.cloned.1.call-start = ((), (), s32[]{:S(2)}) async-start(), calls=%async_computation.1 | async-start | bytes 393216 | tf_op jit(solution)/shard_map/psum | solution.py:78
  150.3 5.0 copy-start.11
  151.9 194.4 %copy-start.9 = (f32[3072,64]{0,1:T(8,128)S(1)}, f32[3072,64]{0,1:T(8,128)}, u32[]{:S(2)}) copy-start(f32[3072,64]{0,1:T(8,128)} %param.9) | copy-start | bytes 2359300
  151.9 194.4 %copy-start.10 = (f32[3072,64]{0,1:T(8,128)S(1)}, f32[3072,64]{0,1:T(8,128)}, u32[]{:S(2)}) copy-start(f32[3072,64]{0,1:T(8,128)} %get-tuple-element.43) | copy-start | bytes 2359300
  151.9 198.0 %collective-permute-start.2 = (bf16[16,192,128]{2,1,0:T(8,128)(2,1)}, bf16[16,192,128]{2,1,0:T(8,128)(2,1)}, u32[]{:S(2)}, u32[]{:S(2)}) collective-permute-start(bf16[16,192,128]{2,1,0:T(8,128)(2,1)} %gather_fusion.3), channel_id=1, source_target_pairs={{0,1},{1,2},{2,3},{3,4},{4,5},{5,6},{6,7},{7,8},{8,9},{9,10},{10,1... | collective-permute-start | bytes 2359304 | tf_op jit(solution)/shard_map/ppermute | solution.py:15
  155.3 194.7 %collective-permute-start.3 = (bf16[16,192,128]{2,1,0:T(8,128)(2,1)S(1)}, bf16[16,192,128]{2,1,0:T(8,128)(2,1)}, u32[]{:S(2)}, u32[]{:S(2)}) collective-permute-start(bf16[16,192,128]{2,1,0:T(8,128)(2,1)S(1)} %copy-done.11), channel_id=1, source_target_pairs={{1,0},{2,1},{3,2},{4,3},{5,4},{6,5},{7,6},{8,7},{9,8},{10,9},{11,1... | collective-permute-start | bytes 2359304 | tf_op jit(solution)/shard_map/ppermute | solution.py:17
  288.2 11.7 %copy-start.12 = (f32[192,192]{1,0:T(8,128)}, f32[192,192]{1,0:T(8,128)S(1)}, u32[]{:S(2)}) copy-start(f32[192,192]{1,0:T(8,128)S(1)} %fusion.7) | copy-start | bytes 442372
  346.3 3.7 copy-start.4
  346.3 3.7 copy-start.5
  364.1 16.7 %copy-start.6 = (f32[3072,64]{1,0:T(8,128)S(1)}, f32[3072,64]{1,0:T(8,128)}, u32[]{:S(2)}) copy-start(f32[3072,64]{1,0:T(8,128)} %copy.40) | copy-start | bytes 2359300
  380.9 5.3 copy-start.1
  384.8 1.4 copy-start.2
Sparse Core Ops, SparseCore 0:
  145.6 140.5 all-reduce.6
  389.1 140.7 all-reduce.8
where the time goes:
time: 546 us; the launch traced here: 539 us
  waiting for transfers between devices  274 us (50%)
  other arithmetic  74.1 us (14%)
  blocking collectives  70.7 us (13%)
  matrix products  56.1 us (10%)
  local copies, waits for them, and re-layouts  35.2 us (6%)
  between operations  16 us (3%)
  starting transfers between devices  12.6 us (2%)
    psum x1, waiting for transfers between devices, shards(): lax.psum(jnp.dot(basis.T, basis_image, precision=highest), ('dom', 'sub'))  141 us
    psum x1, waiting for transfers between devices, shards(): lax.psum(jnp.dot(search.T, search, precision=highest), ('dom', 'sub'))  128 us
    psum x1, blocking collectives, shards(): lax.psum((jnp.dot(block_x.T, block_x, precision=highest), jnp.dot(block_x...  70.7 us
    dot_general x2, matrix products, apply_tiles(): jnp.einsum('gkij,gkjc->gic', tile_blocks, picked, preferred_element_type=...  32.2 us
    another operation x7, other arithmetic, shards(): lower = jnp.linalg.cholesky(gram_sum / total)  28.7 us
    another operation x6, other arithmetic, shards(): jax.scipy.linalg.solve_triangular(lower, jnp.eye(width, dtype=jnp.float32...  23.5 us
    gather x2, local copies, waits for them, and re-layouts, apply_tiles(): picked = extended[neighbours]  22.6 us
  transfers between devices with their start and end apart: 6, of which 3 were waited for; matrix products, arithmetic and copies ran while one was open for 14% of the time, Pallas kernels for 0%

commit v1 on v0

v1 whole, which is shorter than its diff:
```python
import functools

import jax
import jax.numpy as jnp
from jax import lax
from jax.experimental import pallas as pl
from jax.experimental.pallas import tpu as pltpu
from jax.sharding import PartitionSpec as P

AXES = ("dom", "sub")
HIGHEST = lax.Precision.HIGHEST
MIB = 2**20
NT = (((1,), (1,)), ((), ()))
TN = (((0,), (0,)), ((), ()))
NN = (((1,), (0,)), ((), ()))


def dot32(a, b, dims):
    return lax.dot_general(a, b, dims, precision=HIGHEST, preferred_element_type=jnp.float32)


def split(odd, value, mine, theirs):
    half = value.shape[0] // 2
    mine[...] = jnp.where(odd[:1] > 0, value[half:], value[:half])
    theirs[...] = jnp.where(odd[:1] > 0, value[:half], value[half:])


def join(odd, mine, theirs):
    first = jnp.where(odd[:1] > 0, theirs, mine)
    second = jnp.where(odd[:1] > 0, mine, theirs)
    return jnp.concatenate([first, second], 0)


def all_sum(mine, theirs, sub, dom):
    twin = [(i, i ^ 1) for i in range(sub)]
    mine = mine + lax.ppermute(theirs, "sub", twin)
    for axis, count, flip in (
        ("sub", sub, 2), ("sub", sub, 6), ("dom", dom, 1), ("dom", dom, 3), ("dom", dom, 4), ("dom", dom, 12)
    ):
        mine = mine + lax.ppermute(mine, axis, [(i, i ^ flip) for i in range(count)])
    return mine, lax.ppermute(mine, "sub", twin)


def to_both(block, devices):
    before = lax.ppermute(block, AXES, [(i, i + 1) for i in range(devices - 1)])
    after = lax.ppermute(block, AXES, [(i + 1, i) for i in range(devices - 1)])
    return before, after


def load_kernel(odd, tiles_hbm, x, p, tiles, gram, sems):
    parts = sems.shape[0]
    size = tiles.shape[0] // parts
    copies = [
        pltpu.make_async_copy(tiles_hbm.at[pl.ds(i * size, size)], tiles.at[pl.ds(i * size, size)], sems.at[i])
        for i in range(parts)
    ]
    for copy in copies:
        copy.start()
    both = jnp.concatenate([x[...], p[...]], 0)
    gram[...] = dot32(both, both, NT)
    for copy in copies:
        copy.wait()


def load(odd, tiles, x, p):
    cols = x.shape[0]
    vmem = pl.BlockSpec(memory_space=pltpu.VMEM)
    return pl.pallas_call(
        load_kernel,
        out_shape=(
            pltpu.VMEM(tiles.shape, tiles.dtype),
            jax.ShapeDtypeStruct((2 * cols, 2 * cols), jnp.float32),
        ),
        in_specs=[vmem, pl.BlockSpec(memory_space=pl.ANY), vmem, vmem],
        out_specs=(vmem, vmem),
        scratch_shapes=[pltpu.SemaphoreType.DMA((8,))],
        compiler_params=pltpu.CompilerParams(vmem_limit_bytes=16 * MIB),
        cost_estimate=pl.CostEstimate(flops=200000000, bytes_accessed=30000000, transcendentals=0),
    )(odd, tiles, x, p)


def fill_slabs(slabs, blocks, count, size):
    for place, block in enumerate(blocks):
        for pair in range(count // 2):
            both = block[:, pair * 2 * size : (pair + 1) * 2 * size]
            slabs[place * count + 2 * pair] = both[:, :size]
            slabs[place * count + 2 * pair + 1] = both[:, size:]


def multiply_tiles(nb, table, tiles, slabs, image, count, per):
    size = tiles.shape[2]

    def step(pair, carry):
        wide = []
        for half in range(per):
            group = pair * per + half
            total = None
            for k in range(tiles.shape[1]):
                slab = slabs[table[nb[group, k]]]
                part = lax.dot_general(tiles[group, k], slab, NT, preferred_element_type=jnp.float32)
                total = part if total is None else total + part
            wide.append(total.T)
        width = per * size
        image[:, pl.ds(pl.multiple_of(pair * width, width), width)] = jnp.concatenate(wide, 1)
        return carry

    lax.fori_loop(0, count // per, step, 0)


def first_kernel(
    per, nb, table, odd, tiles, own, before, after, x, p, gram, x_image, p_image, mine, theirs, slabs, images
):
    count, size, cols = tiles.shape[0], tiles.shape[2], x.shape[0]
    fill_slabs(slabs, (before, own, after), count, size)
    multiply_tiles(nb, table, tiles, slabs, images, count, per)
    image = images[:cols]
    x_image[...] = image
    p_image[...] = images[cols:]
    cross = dot32(jnp.concatenate([x[...], image, p[...]], 0), image, NT)
    g = gram[...]
    left = jnp.concatenate([g[:cols, :cols], g[cols:, :cols], g[cols:, cols:]], 0)
    split(odd, jnp.concatenate([left, cross], 1), mine, theirs)


def half_of(cols):
    return jax.ShapeDtypeStruct((3 * cols // 2, 2 * cols), jnp.float32)


def first_images(nb, table, odd, tiles, own, before, after, x, p, gram):
    count, size, cols = tiles.shape[0], tiles.shape[2], x.shape[0]
    vmem = pl.BlockSpec(memory_space=pltpu.VMEM)
    smem = pl.BlockSpec(memory_space=pltpu.SMEM)
    return pl.pallas_call(
        functools.partial(first_kernel, 4),
        out_shape=(
            jax.ShapeDtypeStruct(x.shape, jnp.float32),
            jax.ShapeDtypeStruct(x.shape, jnp.float32),
            half_of(cols),
            half_of(cols),
        ),
        in_specs=[smem, smem] + [vmem] * 8,
        out_specs=(vmem,) * 4,
        scratch_shapes=[
            pltpu.VMEM((3 * count, 2 * cols, size), jnp.bfloat16),
            pltpu.VMEM((2 * cols, x.shape[1]), jnp.float32),
        ],
        compiler_params=pltpu.CompilerParams(vmem_limit_bytes=16 * MIB),
        cost_estimate=pl.CostEstimate(flops=10000000000, bytes_accessed=4000000, transcendentals=0),
    )(nb, table, odd, pltpu.with_memory_space_constraint(tiles, pltpu.VMEM), own, before, after, x, p, gram)


def middle_kernel(x, r, p, p_image, packed):
    packed[...] = dot32(jnp.concatenate([x[...], r[...], p[...]], 0), p_image[...], NT)


def middle_products(x, r, p, p_image):
    vmem = pl.BlockSpec(memory_space=pltpu.VMEM)
    return pl.pallas_call(
        middle_kernel,
        out_shape=jax.ShapeDtypeStruct((3 * x.shape[0], x.shape[0]), jnp.float32),
        in_specs=[vmem] * 4,
        out_specs=vmem,
        compiler_params=pltpu.CompilerParams(vmem_limit_bytes=4 * MIB),
        cost_estimate=pl.CostEstimate(flops=1500000000, bytes_accessed=3000000, transcendentals=0),
    )(x, r, p, p_image)


def second_kernel(
    per, nb, table, odd, tiles, own, before, after, x, r, p, middle, r_image, mine, theirs, slabs
):
    count, size = tiles.shape[0], tiles.shape[2]
    fill_slabs(slabs, (before, own, after), count, size)
    multiply_tiles(nb, table, tiles, slabs, r_image, count, per)
    cross = dot32(jnp.concatenate([x[...], r[...], p[...]], 0), r_image[...], NT)
    split(odd, jnp.concatenate([cross, middle[...]], 1), mine, theirs)


def second_images(nb, table, odd, tiles, own, before, after, x, r, p, middle):
    count, size, cols = tiles.shape[0], tiles.shape[2], x.shape[0]
    vmem = pl.BlockSpec(memory_space=pltpu.VMEM)
    smem = pl.BlockSpec(memory_space=pltpu.SMEM)
    return pl.pallas_call(
        functools.partial(second_kernel, 4),
        out_shape=(
            jax.ShapeDtypeStruct(x.shape, jnp.float32),
            half_of(cols),
            half_of(cols),
        ),
        in_specs=[smem, smem] + [vmem] * 9,
        out_specs=(vmem,) * 3,
        scratch_shapes=[pltpu.VMEM((3 * count, cols, size), jnp.bfloat16)],
        compiler_params=pltpu.CompilerParams(vmem_limit_bytes=16 * MIB),
        cost_estimate=pl.CostEstimate(flops=10000000000, bytes_accessed=4000000, transcendentals=0),
    )(nb, table, odd, pltpu.with_memory_space_constraint(tiles, pltpu.VMEM), own, before, after, x, r, p, middle)


def cholesky_inverse(a):
    n, step = a.shape[0], 8
    rows = lax.broadcasted_iota(jnp.int32, (step, 2 * n), 0)
    lanes = lax.broadcasted_iota(jnp.int32, (n, n), 1)
    unit = (lanes == lax.broadcasted_iota(jnp.int32, (n, n), 0)).astype(jnp.float32)
    m = jnp.concatenate([a, unit], 1)
    bands = [m[i : i + step] for i in range(0, n, step)]
    pivots = []
    for at in range(n // step):
        live = range(at, n // step)
        columns = [
            {t: jnp.broadcast_to(bands[t][:, at * step + i : at * step + i + 1], (step, 2 * n)) for t in live}
            for i in range(step)
        ]
        for i in range(step):
            pivot = columns[i][at][i : i + 1]
            pivots.append(pivot)
            over = 1.0 / pivot
            row = bands[at][i : i + 1]
            factor = {t: columns[i][t] * over for t in live}
            factor[at] = jnp.where(rows > i, factor[at], 0.0)
            for later in range(i + 1, step):
                entry = columns[later][at][i : i + 1]
                for t in live:
                    columns[later][t] = columns[later][t] - factor[t] * entry
            for t in live:
                bands[t] = bands[t] - factor[t] * row
    scale = jnp.concatenate(pivots, 0)
    return (jnp.concatenate(bands, 0) * (1.0 / jnp.sqrt(scale)))[:, n:]


def residual_kernel(odd, mine, theirs, x, x_image, packed, quotient, inverse, residual, rounded):
    cols = x.shape[0]
    packed[...] = join(odd, mine[...], theirs[...])
    gram, cross = packed[:cols, :cols], packed[:cols, cols:]
    w = cholesky_inverse(gram)
    inverse[...] = w
    q = dot32(w, dot32(w, cross, NN), TN)
    quotient[...] = q
    r = x_image[...] - dot32(q, x[...], TN)
    residual[...] = r
    rounded[...] = r.astype(jnp.bfloat16)


def residual_of(odd, mine, theirs, x, x_image):
    cols = x.shape[0]
    vmem = pl.BlockSpec(memory_space=pltpu.VMEM)
    square = jax.ShapeDtypeStruct((cols, cols), jnp.float32)
    return pl.pallas_call(
        residual_kernel,
        out_shape=(
            jax.ShapeDtypeStruct((3 * cols, 2 * cols), jnp.float32),
            square,
            square,
            jax.ShapeDtypeStruct(x.shape, jnp.float32),
            jax.ShapeDtypeStruct(x.shape, jnp.bfloat16),
        ),
        in_specs=[vmem] * 5,
        out_specs=(vmem,) * 5,
        compiler_params=pltpu.CompilerParams(vmem_limit_bytes=4 * MIB),
        cost_estimate=pl.CostEstimate(flops=3000000000, bytes_accessed=3000000, transcendentals=0),
    )(odd, mine, theirs, x, x_image)


def factor_kernel(total, packed, quotient, x_inverse, inverse, r_cross):
    c = quotient.shape[0]
    q = quotient[...]
    xx, px, pp = packed[:c, :c], packed[c : 2 * c, :c], packed[2 * c :, :c]
    xi, ii, pi = packed[:c, c:], packed[c : 2 * c, c:], packed[2 * c :, c:]
    rx = xi.T - dot32(q, xx, TN)
    ri = ii - dot32(q, xi, TN)
    rr = ri - dot32(rx, q, NN)
    pr = pi - dot32(px, q, NN)
    r_cross[...] = ri
    scale = 1.0 / total
    w1 = x_inverse[...] * (total**0.5)
    l21, l31 = dot32(rx * scale, w1, NT), dot32(px * scale, w1, NT)
    w2 = cholesky_inverse(rr * scale - dot32(l21, l21, NT))
    l32 = dot32(pr * scale - dot32(l31, l21, NT), w2, NT)
    w3 = cholesky_inverse(pp * scale - dot32(l31, l31, NT) - dot32(l32, l32, NT))
    w21 = -dot32(w2, dot32(l21, w1, NN), NN)
    w32 = -dot32(w3, dot32(l32, w2, NN), NN)
    w31 = -dot32(w3, dot32(l31, w1, NN) + dot32(l32, w21, NN), NN)
    zero = jnp.zeros_like(w1)
    inverse[...] = jnp.concatenate(
        [
            jnp.concatenate([w1, zero, zero], 1),
            jnp.concatenate([w21, w2, zero], 1),
            jnp.concatenate([w31, w32, w3], 1),
        ],
        0,
    )


def factor(total, packed, quotient, x_inverse):
    c = quotient.shape[0]
    vmem = pl.BlockSpec(memory_space=pltpu.VMEM)
    return pl.pallas_call(
        functools.partial(factor_kernel, total),
        out_shape=(
            jax.ShapeDtypeStruct((3 * c, 3 * c), jnp.float32),
            jax.ShapeDtypeStruct((c, c), jnp.float32),
        ),
        in_specs=[vmem] * 3,
        out_specs=(vmem,) * 2,
        compiler_params=pltpu.CompilerParams(vmem_limit_bytes=16 * MIB),
        cost_estimate=pl.CostEstimate(flops=3000000000, bytes_accessed=3000000, transcendentals=0),
    )(packed, quotient, x_inverse)


def basis_kernel(inverse, x, r, p, x_image, r_image, p_image, basis, basis_image):
    w = inverse[...]
    basis[...] = dot32(w, jnp.concatenate([x[...], r[...], p[...]], 0), NN)
    basis_image[...] = dot32(w, jnp.concatenate([x_image[...], r_image[...], p_image[...]], 0), NN)


def bases(inverse, *blocks):
    width, rows = inverse.shape[0], blocks[0].shape[1]
    cols = blocks[0].shape[0]
    tile = 512
    block = pl.BlockSpec((cols, tile), lambda i: (0, i))
    out = pl.BlockSpec((width, tile), lambda i: (0, i))
    return pl.pallas_call(
        basis_kernel,
        grid=(rows // tile,),
        out_shape=(jax.ShapeDtypeStruct((width, rows), jnp.float32),) * 2,
        in_specs=[pl.BlockSpec((width, width), lambda i: (0, 0))] + [block] * 6,
        out_specs=(out, out),
        compiler_params=pltpu.CompilerParams(vmem_limit_bytes=16 * MIB),
        cost_estimate=pl.CostEstimate(flops=2700000000, bytes_accessed=10000000, transcendentals=0),
    )(inverse, *blocks)


def project_kernel(total, odd, inverse, packed, r_cross, mine, theirs, projected):
    c = r_cross.shape[0]
    left = jnp.concatenate([packed[:c, c:], r_cross[...], packed[2 * c :, c:]], 0)
    w = inverse[...]
    cross = jnp.concatenate([left, join(odd, mine[...], theirs[...])], 1)
    projected[...] = dot32(dot32(w, cross, NN), w, NT) * (1.0 / total)


def project(total, odd, inverse, packed, r_cross, mine, theirs):
    vmem = pl.BlockSpec(memory_space=pltpu.VMEM)
    return pl.pallas_call(
        functools.partial(project_kernel, total),
        out_shape=jax.ShapeDtypeStruct(inverse.shape, jnp.float32),
        in_specs=[vmem] * 6,
        out_specs=vmem,
        compiler_params=pltpu.CompilerParams(vmem_limit_bytes=16 * MIB),
    )(odd, inverse, packed, r_cross, mine, theirs)


def shards(sub, dom, tile_blocks, neighbours, send_groups, block_x, block_p):
    devices = sub * dom
    count, rows, cols = tile_blocks.shape[0], block_x.shape[0], block_x.shape[1]
    total = float(rows * devices)
    x, p = block_x.T, block_p.T
    lists = jnp.pad(send_groups.astype(jnp.bfloat16)[None], ((0, 2 * cols - 1), (0, 128 - 2 * count)))
    both = jnp.concatenate([jnp.concatenate([x, p], 0).astype(jnp.bfloat16), lists], 1)
    before, after = to_both(both, devices)
    table = jnp.concatenate(
        [
            before[0, rows + count : rows + 2 * count].astype(jnp.int32),
            jnp.arange(count, 2 * count, dtype=jnp.int32),
            after[0, rows : rows + count].astype(jnp.int32) + 2 * count,
        ]
    )
    odd = jnp.broadcast_to(lax.axis_index("sub") % 2, (8, 2 * cols)).astype(jnp.float32)
    tiles, gram = load(odd, tile_blocks, x, p)
    x_image, p_image, *halves = first_images(neighbours, table, odd, tiles, both, before, after, x, p, gram)
    halves = all_sum(*halves, sub, dom)
    packed, quotient, x_inverse, residual, r_round = residual_of(odd, *halves, x, x_image)
    r_before, r_after = to_both(r_round, devices)
    middle = middle_products(x, residual, p, p_image)
    r_image, *halves = second_images(
        neighbours, table, odd, tiles, r_round, r_before, r_after, x, residual, p, middle
    )
    halves = all_sum(*halves, sub, dom)
    inverse, r_cross = factor(total, packed, quotient, x_inverse)
    basis, basis_image = bases(inverse, x, residual, p, x_image, r_image, p_image)
    projected = project(total, odd, inverse, packed, r_cross, *halves)
    return basis.T, basis_image.T, projected


def solution(mesh):
    placed = (
        P(AXES, None, None, None),
        P(AXES, None),
        P(AXES),
        P(AXES, None),
        P(AXES, None),
    )
    return jax.shard_map(
        functools.partial(shards, mesh.shape["sub"], mesh.shape["dom"]),
        mesh=mesh,
        in_specs=placed,
        out_specs=(P(AXES, None), P(AXES, None), P()),
        check_vma=False,
    )
```

time: 546 us -> 145 us (0.27); the launches traced: 539 us -> 145 us
  waiting for transfers between devices: 274 us -> 27.2 us
  other arithmetic: 74.1 us -> 3.23 us
  blocking collectives: 70.7 us -> 0 us
  matrix products: 56.1 us -> 0 us
  Pallas kernels: 0 us -> 51.7 us
  starting transfers between devices: 12.6 us -> 62.2 us
  local copies, waits for them, and re-layouts: 35.2 us -> 0.02 us
  between operations: 16 us -> 0.86 us
    psum x2 -> x0, waiting for transfers between devices: 269 us -> none  [the longest x1 141 us: shards(): lax.psum(jnp.dot(basis.T, basis_image, precision=highest), ('dom', 'sub'))]
    psum x1 -> x0, blocking collectives: 70.7 us -> none  [shards(): lax.psum((jnp.dot(block_x.T, block_x, precision=highest), jnp.dot(block_x...]
    another operation x19 -> x1, other arithmetic: 64.3 us -> 1.58 us  [the longest x7 28.7 us: shards(): lower = jnp.linalg.cholesky(gram_sum / total)]
    pallas_call x0 -> x8, Pallas kernels: none -> 51.7 us  [the longest x1 12.7 us: first_images(): pl.pallas_call(functools.partial(first_kernel, 4), out_shape=(jax.ShapeDt...]
    dot_general x9 -> x0, matrix products: 50.6 us -> none  [the longest x2 32.2 us: apply_tiles(): jnp.einsum('gkij,gkjc->gic', tile_blocks, picked, preferred_element_type=...]
    ppermute x4 -> x20, starting transfers between devices: 12.5 us -> 62.2 us  [the longest x12 37.2 us: all_sum(): lax.ppermute(mine, axis, [(i, i ^ flip) for i in range(count)])]
    gather x6 -> x0, local copies, waits for them, and re-layouts: 26.9 us -> none  [the longest x2 22.6 us: apply_tiles(): picked = extended[neighbours]]
    ppermute x4 -> x20, waiting for transfers between devices: 4.68 us -> 27.2 us  [the longest x12 19.5 us: all_sum(): lax.ppermute(mine, axis, [(i, i ^ flip) for i in range(count)])]
  transfers between devices with their start and end apart: 6 -> 20, of which waited for: 3 -> 16; matrix products, arithmetic and copies ran while one was open for 14% -> 0% of each run, Pallas kernels for 0% -> 16%
where the time goes in v1:
time: 145 us
  starting transfers between devices  62.2 us (43%)
  Pallas kernels  51.7 us (36%)
  waiting for transfers between devices  27.2 us (19%)
  other arithmetic  3.23 us (2%)
    ppermute x12, starting transfers between devices, all_sum(): lax.ppermute(mine, axis, [(i, i ^ flip) for i in range(count)])  37.2 us
    ppermute x12, waiting for transfers between devices, all_sum(): lax.ppermute(mine, axis, [(i, i ^ flip) for i in range(count)])  19.5 us
    ppermute x2, starting transfers between devices, all_sum(): return (mine, lax.ppermute(mine, 'sub', twin))  13.6 us
    pallas_call x1, Pallas kernels, first_images(): pl.pallas_call(functools.partial(first_kernel, 4), out_shape=(jax.ShapeDt...  12.7 us
    pallas_call x1, Pallas kernels, second_images(): pl.pallas_call(functools.partial(second_kernel, 4), out_shape=(jax.ShapeD...  11.6 us
    pallas_call x1, Pallas kernels, load(): pl.pallas_call(load_kernel, out_shape=(pltpu.VMEM(tiles.shape, tiles.dtyp...  9.41 us
    pallas_call x1, Pallas kernels, bases(): pl.pallas_call(basis_kernel, grid=(rows // tile,), out_shape=(jax.ShapeDt...  6.03 us
    ppermute x2, starting transfers between devices, to_both(): after = lax.ppermute(block, AXES, [(i + 1, i) for i in range(devices - 1)])  5.94 us
  transfers between devices with their start and end apart: 20, of which 16 were waited for; matrix products, arithmetic and copies ran while one was open for 0% of the time, Pallas kernels for 16%

profile of v1, /device:TPU:1, one launch (start us, length us, event | category | flops | bytes accessed | tf_op | source)
XLA Modules:
  0.0 145.1 jit_solution(2816215186109712014)
XLA Ops:
  2.9 3.3 %collective-permute-start.1 = (bf16[128,3200]{1,0:T(8,128)(2,1)S(1)}, bf16[128,3200]{1,0:T(8,128)(2,1)S(1)}, u32[]{:S(2)}, u32[]{:S(2)}) collective-permute-start(bf16[128,3200]{1,0:T(8,128)(2,1)S(1)} %fusion.1.own), channel_id=1, source_target_pairs={{1,0},{2,1},{3,2},{4,3},{5,4},{6,5},{7,6},{8,7},{9,8},{10,9},{11,1... | collective-permute-start | bytes 2457608 | tf_op jit(solution)/shard_map/ppermute | solution.py:46
  6.3 3.2 %collective-permute-start = (bf16[128,3200]{1,0:T(8,128)(2,1)S(1)}, bf16[128,3200]{1,0:T(8,128)(2,1)}, u32[]{:S(2)}, u32[]{:S(2)}) collective-permute-start(bf16[128,3200]{1,0:T(8,128)(2,1)S(1)} %fusion.1.own), channel_id=1, source_target_pairs={{0,1},{1,2},{2,3},{3,4},{4,5},{5,6},{6,7},{7,8},{8,9},{9,10},{10,1... | collective-permute-start | bytes 2457608 | tf_op jit(solution)/shard_map/ppermute | solution.py:45
  9.5 9.4 %shard_map.76 = (bf16[16,18,192,192]{3,2,1,0:T(8,128)(2,1)S(1)}, f32[128,128]{1,0:T(8,128)S(1)}) custom-call(f32[8,128]{1,0:T(8,128)S(1)} %broadcast_in_dim.6.odd, bf16[16,18,192,192]{3,2,1,0:T(8,128)(2,1)} %tiles_hbm.1, f32[64,3072]{1,0:T(8,128)S(1)} %bitcast.20, f32[64,3072]{1,0:T(8,128)S(1)} %bitcast.15), custom_call_target="tpu_custom_call" | custom-call | flops 200000000 | bytes 30000000 | tf_op jit(solution)/shard_map/pallas_call | solution.py:68
  19.8 12.7 %shard_map.77 = (f32[64,3072]{1,0:T(8,128)S(1)}, f32[64,3072]{1,0:T(8,128)S(1)}, f32[96,128]{1,0:T(8,128)S(1)}, f32[96,128]{1,0:T(8,128)S(1)}) custom-call(s32[16,18]{1,0:T(8,128)S(1)} %copy-done.2, s32[48]{0:T(128)S(1)} %pad_add_fusion.table, f32[8,128]{1,0:T(8,128)S(1)} %broadcast_in_dim.6.odd, bf16[16,18,192,192]{3,2,1,0:T(8,128)(2,1)S(1)} %get-tuple-element.21.tiles, ...), custom_call_target="tpu_custom_call" | custom-call | flops 10000000000 | bytes 4000000 | tf_op jit(solution)/shard_map/pallas_call | solution.py:133
  33.9 2.1 %collective-permute-start.3 = (f32[96,128]{1,0:T(8,128)S(1)}, f32[96,128]{1,0:T(8,128)S(1)}, u32[]{:S(2)}, u32[]{:S(2)}) collective-permute-start(f32[96,128]{1,0:T(8,128)S(1)} %add.61), channel_id=1, source_target_pairs={{0,2},{1,3},{2,0},{3,1},{4,6},{5,7},{6,4},{7,5},{8,10},{9,11},{10,... | collective-permute-start | bytes 147464 | tf_op jit(solution)/shard_map/ppermute | solution.py:40
  37.5 4.2 %collective-permute-start.4 = (f32[96,128]{1,0:T(8,128)S(1)}, f32[96,128]{1,0:T(8,128)S(1)}, u32[]{:S(2)}, u32[]{:S(2)}) collective-permute-start(f32[96,128]{1,0:T(8,128)S(1)} %add.62), channel_id=1, source_target_pairs={{0,6},{1,7},{2,4},{3,5},{4,2},{5,3},{6,0},{7,1},{8,14},{9,15},{10,... | collective-permute-start | bytes 147464 | tf_op jit(solution)/shard_map/ppermute | solution.py:40
  43.2 4.5 %collective-permute-start.5 = (f32[96,128]{1,0:T(8,128)S(1)}, f32[96,128]{1,0:T(8,128)S(1)}, u32[]{:S(2)}, u32[]{:S(2)}) collective-permute-start(f32[96,128]{1,0:T(8,128)S(1)} %add.63), channel_id=1, source_target_pairs={{0,8},{8,0},{16,24},{24,16},{32,40},{40,32},{48,56},{56,48},{64,72... | collective-permute-start | bytes 147464 | tf_op jit(solution)/shard_map/ppermute | solution.py:40
  49.2 3.1 %collective-permute-start.6 = (f32[96,128]{1,0:T(8,128)S(1)}, f32[96,128]{1,0:T(8,128)S(1)}, u32[]{:S(2)}, u32[]{:S(2)}) collective-permute-start(f32[96,128]{1,0:T(8,128)S(1)} %add.64), channel_id=1, source_target_pairs={{0,24},{8,16},{16,8},{24,0},{32,56},{40,48},{48,40},{56,32},{64,88... | collective-permute-start | bytes 147464 | tf_op jit(solution)/shard_map/ppermute | solution.py:40
  53.8 5.5 %collective-permute-start.7 = (f32[96,128]{1,0:T(8,128)S(1)}, f32[96,128]{1,0:T(8,128)S(1)}, u32[]{:S(2)}, u32[]{:S(2)}) collective-permute-start(f32[96,128]{1,0:T(8,128)S(1)} %add.65), channel_id=1, source_target_pairs={{0,32},{8,40},{16,48},{24,56},{32,0},{40,8},{48,16},{56,24},{64,96... | collective-permute-start | bytes 147464 | tf_op jit(solution)/shard_map/ppermute | solution.py:40
  60.7 3.9 %collective-permute-start.8 = (f32[96,128]{1,0:T(8,128)S(1)}, f32[96,128]{1,0:T(8,128)S(1)}, u32[]{:S(2)}, u32[]{:S(2)}) collective-permute-start(f32[96,128]{1,0:T(8,128)S(1)} %add.66), channel_id=1, source_target_pairs={{0,96},{8,104},{16,112},{24,120},{32,64},{40,72},{48,80},{56,88},{... | collective-permute-start | bytes 147464 | tf_op jit(solution)/shard_map/ppermute | solution.py:40
  66.2 7.1 %collective-permute-start.9 = (f32[96,128]{1,0:T(8,128)S(1)}, f32[96,128]{1,0:T(8,128)S(1)}, u32[]{:S(2)}, u32[]{:S(2)}) collective-permute-start(f32[96,128]{1,0:T(8,128)S(1)} %add.67.mine), channel_id=1, source_target_pairs={{0,1},{1,0},{2,3},{3,2},{4,5},{5,4},{6,7},{7,6},{8,9},{9,8},{10,11... | collective-permute-start | bytes 147464 | tf_op jit(solution)/shard_map/ppermute | solution.py:41
  74.2 3.0 %shard_map.78 = (f32[192,128]{1,0:T(8,128)S(1)}, f32[64,64]{1,0:T(8,128)S(1)}, f32[64,64]{1,0:T(8,128)S(1)}, f32[64,3072]{1,0:T(8,128)S(1)}, bf16[64,3072]{1,0:T(8,128)(2,1)S(1)}) custom-call(f32[8,128]{1,0:T(8,128)S(1)} %broadcast_in_dim.6.odd, f32[96,128]{1,0:T(8,128)S(1)} %add.67.mine, f32[96,128]{1,0:T(8,128)S(1)} %collective-permute-done.9.theirs, ...), custom_call_target="tpu_custom_call" | custom-call | flops 3000000000 | bytes 3000000 | tf_op jit(solution)/shard_map/pallas_call | solution.py:245
  79.1 2.6 %collective-permute-start.11 = (bf16[64,3072]{1,0:T(8,128)(2,1)S(1)}, bf16[64,3072]{1,0:T(8,128)(2,1)S(1)}, u32[]{:S(2)}, u32[]{:S(2)}) collective-permute-start(bf16[64,3072]{1,0:T(8,128)(2,1)S(1)} %get-tuple-element.31.own), channel_id=1, source_target_pairs={{1,0},{2,1},{3,2},{4,3},{5,4},{6,5},{7,6},{8,7},{9,8},{10,9},{11,1... | collective-permute-start | bytes 1179656 | tf_op jit(solution)/shard_map/ppermute | solution.py:46
  81.7 2.0 %shard_map.80.middle = f32[192,64]{1,0:T(8,128)S(1)} custom-call(f32[64,3072]{1,0:T(8,128)S(1)} %bitcast.23, f32[64,3072]{1,0:T(8,128)S(1)} %get-tuple-element.30.r, f32[64,3072]{1,0:T(8,128)S(1)} %bitcast.17, f32[64,3072]{1,0:T(8,128)S(1)} %get-tuple-element.32.p_image), custom_call_target="tpu_custom_call" | custom-call | flops 1500000000 | bytes 3000000 | tf_op jit(solution)/shard_map/pallas_call | solution.py:158
  83.8 4.4 %collective-permute-done.11.after = bf16[64,3072]{1,0:T(8,128)(2,1)S(1)} collective-permute-done((bf16[64,3072]{1,0:T(8,128)(2,1)S(1)}, bf16[64,3072]{1,0:T(8,128)(2,1)S(1)}, u32[]{:S(2)}, u32[]{:S(2)}) %collective-permute-start.11) | collective-permute-done | bytes 393248 | tf_op jit(solution)/shard_map/ppermute | solution.py:46
  88.2 11.6 %shard_map.81 = (f32[64,3072]{1,0:T(8,128)S(1)}, f32[96,128]{1,0:T(8,128)S(1)}, f32[96,128]{1,0:T(8,128)S(1)}) custom-call(s32[16,18]{1,0:T(8,128)S(1)} %copy-done.2, s32[48]{0:T(128)S(1)} %pad_add_fusion.table, f32[8,128]{1,0:T(8,128)S(1)} %broadcast_in_dim.6.odd, bf16[16,18,192,192]{3,2,1,0:T(8,128)(2,1)S(1)} %get-tuple-element.21.tiles, ...), custom_call_target="tpu_custom_call" | custom-call | flops 10000000000 | bytes 4000000 | tf_op jit(solution)/shard_map/pallas_call | solution.py:182
  101.2 2.9 %collective-permute-done.13 = f32[96,128]{1,0:T(8,128)S(1)} collective-permute-done((f32[96,128]{1,0:T(8,128)S(1)}, f32[96,128]{1,0:T(8,128)S(1)}, u32[]{:S(2)}, u32[]{:S(2)}) %collective-permute-start.13) | collective-permute-done | bytes 49184 | tf_op jit(solution)/shard_map/ppermute | solution.py:40
  104.2 3.3 %collective-permute-start.14 = (f32[96,128]{1,0:T(8,128)S(1)}, f32[96,128]{1,0:T(8,128)S(1)}, u32[]{:S(2)}, u32[]{:S(2)}) collective-permute-start(f32[96,128]{1,0:T(8,128)S(1)} %add.69), channel_id=1, source_target_pairs={{0,6},{1,7},{2,4},{3,5},{4,2},{5,3},{6,0},{7,1},{8,14},{9,15},{10,... | collective-permute-start | bytes 147464 | tf_op jit(solution)/shard_map/ppermute | solution.py:40
  109.1 2.9 %collective-permute-done.15 = f32[96,128]{1,0:T(8,128)S(1)} collective-permute-done((f32[96,128]{1,0:T(8,128)S(1)}, f32[96,128]{1,0:T(8,128)S(1)}, u32[]{:S(2)}, u32[]{:S(2)}) %collective-permute-start.15) | collective-permute-done | bytes 49184 | tf_op jit(solution)/shard_map/ppermute | solution.py:40
  112.0 5.4 %collective-permute-start.16 = (f32[96,128]{1,0:T(8,128)S(1)}, f32[96,128]{1,0:T(8,128)S(1)}, u32[]{:S(2)}, u32[]{:S(2)}) collective-permute-start(f32[96,128]{1,0:T(8,128)S(1)} %add.71), channel_id=1, source_target_pairs={{0,24},{8,16},{16,8},{24,0},{32,56},{40,48},{48,40},{56,32},{64,88... | collective-permute-start | bytes 147464 | tf_op jit(solution)/shard_map/ppermute | solution.py:40
  122.4 3.3 %collective-permute-start.18 = (f32[96,128]{1,0:T(8,128)S(1)}, f32[96,128]{1,0:T(8,128)S(1)}, u32[]{:S(2)}, u32[]{:S(2)}) collective-permute-start(f32[96,128]{1,0:T(8,128)S(1)} %add.73), channel_id=1, source_target_pairs={{0,96},{8,104},{16,112},{24,120},{32,64},{40,72},{48,80},{56,88},{... | collective-permute-start | bytes 147464 | tf_op jit(solution)/shard_map/ppermute | solution.py:40
  125.7 5.2 %shard_map.79 = (f32[192,192]{1,0:T(8,128)S(1)}, f32[64,64]{1,0:T(8,128)S(1)}) custom-call(f32[192,128]{1,0:T(8,128)S(1)} %get-tuple-element.26.packed, f32[64,64]{1,0:T(8,128)S(1)} %get-tuple-element.27.quotient, f32[64,64]{1,0:T(8,128)S(1)} %get-tuple-element.28.x_inverse), custom_call_target="tpu_custom_call" | custom-call | flops 3000000000 | bytes 3000000 | tf_op jit(solution)/shard_map/pallas_call | solution.py:294
  130.9 6.5 %collective-permute-start.19 = (f32[96,128]{1,0:T(8,128)S(1)}, f32[96,128]{1,0:T(8,128)S(1)}, u32[]{:S(2)}, u32[]{:S(2)}) collective-permute-start(f32[96,128]{1,0:T(8,128)S(1)} %add.74.mine), channel_id=1, source_target_pairs={{0,1},{1,0},{2,3},{3,2},{4,5},{5,4},{6,7},{7,6},{8,9},{9,8},{10,11... | collective-permute-start | bytes 147464 | tf_op jit(solution)/shard_map/ppermute | solution.py:41
  137.5 6.0 %shard_map.82 = (f32[192,3072]{1,0:T(8,128)}, f32[192,3072]{1,0:T(8,128)}) custom-call(f32[192,192]{1,0:T(8,128)S(1)} %get-tuple-element.29.inverse, f32[64,3072]{1,0:T(8,128)S(1)} %bitcast.25, f32[64,3072]{1,0:T(8,128)S(1)} %get-tuple-element.30.r, f32[64,3072]{1,0:T(8,128)S(1)} %bitcast.19, f32[64,3072]{1,0:T(8,128)S(1)} %get-tuple-element.25.x_image, ...), custom_call_target="tpu_custom_call" | custom-call | flops 2700000000 | bytes 10000000 | tf_op jit(solution)/shard_map/pallas_call | solution.py:319
  (52 shorter events, 25.8 us)
Async XLA Ops:
  1.3 8.2 %copy-start = (f32[3072,64]{0,1:T(8,128)S(1)}, f32[3072,64]{0,1:T(8,128)}, u32[]{:S(2)}) copy-start(f32[3072,64]{0,1:T(8,128)} %param.9) | copy-start | bytes 2359300
  1.3 8.2 %copy-start.1 = (f32[3072,64]{0,1:T(8,128)S(1)}, f32[3072,64]{0,1:T(8,128)}, u32[]{:S(2)}) copy-start(f32[3072,64]{0,1:T(8,128)} %param.8) | copy-start | bytes 2359300
  2.9 16.0 %collective-permute-start.1 = (bf16[128,3200]{1,0:T(8,128)(2,1)S(1)}, bf16[128,3200]{1,0:T(8,128)(2,1)S(1)}, u32[]{:S(2)}, u32[]{:S(2)}) collective-permute-start(bf16[128,3200]{1,0:T(8,128)(2,1)S(1)} %fusion.1.own), channel_id=1, source_target_pairs={{1,0},{2,1},{3,2},{4,3},{5,4},{6,5},{7,6},{8,7},{9,8},{10,9},{11,1... | collective-permute-start | bytes 2457608 | tf_op jit(solution)/shard_map/ppermute | solution.py:46
  6.3 12.7 %collective-permute-start = (bf16[128,3200]{1,0:T(8,128)(2,1)S(1)}, bf16[128,3200]{1,0:T(8,128)(2,1)}, u32[]{:S(2)}, u32[]{:S(2)}) collective-permute-start(bf16[128,3200]{1,0:T(8,128)(2,1)S(1)} %fusion.1.own), channel_id=1, source_target_pairs={{0,1},{1,2},{2,3},{3,4},{4,5},{5,6},{6,7},{7,8},{8,9},{9,10},{10,1... | collective-permute-start | bytes 2457608 | tf_op jit(solution)/shard_map/ppermute | solution.py:45
  9.5 10.3 %copy-start.2 = (s32[16,18]{1,0:T(8,128)S(1)}, s32[16,18]{1,0:T(8,128)}, u32[]{:S(2)}) copy-start(s32[16,18]{1,0:T(8,128)} %nb.3) | copy-start | bytes 3460
  32.6 1.3 collective-permute-start.2
  33.9 3.6 %collective-permute-start.3 = (f32[96,128]{1,0:T(8,128)S(1)}, f32[96,128]{1,0:T(8,128)S(1)}, u32[]{:S(2)}, u32[]{:S(2)}) collective-permute-start(f32[96,128]{1,0:T(8,128)S(1)} %add.61), channel_id=1, source_target_pairs={{0,2},{1,3},{2,0},{3,1},{4,6},{5,7},{6,4},{7,5},{8,10},{9,11},{10,... | collective-permute-start | bytes 147464 | tf_op jit(solution)/shard_map/ppermute | solution.py:40
  37.5 5.7 %collective-permute-start.4 = (f32[96,128]{1,0:T(8,128)S(1)}, f32[96,128]{1,0:T(8,128)S(1)}, u32[]{:S(2)}, u32[]{:S(2)}) collective-permute-start(f32[96,128]{1,0:T(8,128)S(1)} %add.62), channel_id=1, source_target_pairs={{0,6},{1,7},{2,4},{3,5},{4,2},{5,3},{6,0},{7,1},{8,14},{9,15},{10,... | collective-permute-start | bytes 147464 | tf_op jit(solution)/shard_map/ppermute | solution.py:40
  43.2 6.0 %collective-permute-start.5 = (f32[96,128]{1,0:T(8,128)S(1)}, f32[96,128]{1,0:T(8,128)S(1)}, u32[]{:S(2)}, u32[]{:S(2)}) collective-permute-start(f32[96,128]{1,0:T(8,128)S(1)} %add.63), channel_id=1, source_target_pairs={{0,8},{8,0},{16,24},{24,16},{32,40},{40,32},{48,56},{56,48},{64,72... | collective-permute-start | bytes 147464 | tf_op jit(solution)/shard_map/ppermute | solution.py:40
  49.2 4.6 %collective-permute-start.6 = (f32[96,128]{1,0:T(8,128)S(1)}, f32[96,128]{1,0:T(8,128)S(1)}, u32[]{:S(2)}, u32[]{:S(2)}) collective-permute-start(f32[96,128]{1,0:T(8,128)S(1)} %add.64), channel_id=1, source_target_pairs={{0,24},{8,16},{16,8},{24,0},{32,56},{40,48},{48,40},{56,32},{64,88... | collective-permute-start | bytes 147464 | tf_op jit(solution)/shard_map/ppermute | solution.py:40
  53.8 7.0 %collective-permute-start.7 = (f32[96,128]{1,0:T(8,128)S(1)}, f32[96,128]{1,0:T(8,128)S(1)}, u32[]{:S(2)}, u32[]{:S(2)}) collective-permute-start(f32[96,128]{1,0:T(8,128)S(1)} %add.65), channel_id=1, source_target_pairs={{0,32},{8,40},{16,48},{24,56},{32,0},{40,8},{48,16},{56,24},{64,96... | collective-permute-start | bytes 147464 | tf_op jit(solution)/shard_map/ppermute | solution.py:40
  60.7 5.4 %collective-permute-start.8 = (f32[96,128]{1,0:T(8,128)S(1)}, f32[96,128]{1,0:T(8,128)S(1)}, u32[]{:S(2)}, u32[]{:S(2)}) collective-permute-start(f32[96,128]{1,0:T(8,128)S(1)} %add.66), channel_id=1, source_target_pairs={{0,96},{8,104},{16,112},{24,120},{32,64},{40,72},{48,80},{56,88},{... | collective-permute-start | bytes 147464 | tf_op jit(solution)/shard_map/ppermute | solution.py:40
  66.2 8.0 %collective-permute-start.9 = (f32[96,128]{1,0:T(8,128)S(1)}, f32[96,128]{1,0:T(8,128)S(1)}, u32[]{:S(2)}, u32[]{:S(2)}) collective-permute-start(f32[96,128]{1,0:T(8,128)S(1)} %add.67.mine), channel_id=1, source_target_pairs={{0,1},{1,0},{2,3},{3,2},{4,5},{5,4},{6,7},{7,6},{8,9},{9,8},{10,11... | collective-permute-start | bytes 147464 | tf_op jit(solution)/shard_map/ppermute | solution.py:41
  77.2 6.6 %collective-permute-start.10 = (bf16[64,3072]{1,0:T(8,128)(2,1)S(1)}, bf16[64,3072]{1,0:T(8,128)(2,1)S(1)}, u32[]{:S(2)}, u32[]{:S(2)}) collective-permute-start(bf16[64,3072]{1,0:T(8,128)(2,1)S(1)} %get-tuple-element.31.own), channel_id=1, source_target_pairs={{0,1},{1,2},{2,3},{3,4},{4,5},{5,6},{6,7},{7,8},{8,9},{9,10},{10,1... | collective-permute-start | bytes 1179656 | tf_op jit(solution)/shard_map/ppermute | solution.py:45
  79.1 9.1 %collective-permute-start.11 = (bf16[64,3072]{1,0:T(8,128)(2,1)S(1)}, bf16[64,3072]{1,0:T(8,128)(2,1)S(1)}, u32[]{:S(2)}, u32[]{:S(2)}) collective-permute-start(bf16[64,3072]{1,0:T(8,128)(2,1)S(1)} %get-tuple-element.31.own), channel_id=1, source_target_pairs={{1,0},{2,1},{3,2},{4,3},{5,4},{6,5},{7,6},{8,7},{9,8},{10,9},{11,1... | collective-permute-start | bytes 1179656 | tf_op jit(solution)/shard_map/ppermute | solution.py:46
  99.8 1.3 collective-permute-start.12
  101.1 3.0 %collective-permute-start.13 = (f32[96,128]{1,0:T(8,128)S(1)}, f32[96,128]{1,0:T(8,128)S(1)}, u32[]{:S(2)}, u32[]{:S(2)}) collective-permute-start(f32[96,128]{1,0:T(8,128)S(1)} %add.68), channel_id=1, source_target_pairs={{0,2},{1,3},{2,0},{3,1},{4,6},{5,7},{6,4},{7,5},{8,10},{9,11},{10,... | collective-permute-start | bytes 147464 | tf_op jit(solution)/shard_map/ppermute | solution.py:40
  104.2 4.8 %collective-permute-start.14 = (f32[96,128]{1,0:T(8,128)S(1)}, f32[96,128]{1,0:T(8,128)S(1)}, u32[]{:S(2)}, u32[]{:S(2)}) collective-permute-start(f32[96,128]{1,0:T(8,128)S(1)} %add.69), channel_id=1, source_target_pairs={{0,6},{1,7},{2,4},{3,5},{4,2},{5,3},{6,0},{7,1},{8,14},{9,15},{10,... | collective-permute-start | bytes 147464 | tf_op jit(solution)/shard_map/ppermute | solution.py:40
  109.0 3.0 %collective-permute-start.15 = (f32[96,128]{1,0:T(8,128)S(1)}, f32[96,128]{1,0:T(8,128)S(1)}, u32[]{:S(2)}, u32[]{:S(2)}) collective-permute-start(f32[96,128]{1,0:T(8,128)S(1)} %add.70), channel_id=1, source_target_pairs={{0,8},{8,0},{16,24},{24,16},{32,40},{40,32},{48,56},{56,48},{64,72... | collective-permute-start | bytes 147464 | tf_op jit(solution)/shard_map/ppermute | solution.py:40
  112.0 6.9 %collective-permute-start.16 = (f32[96,128]{1,0:T(8,128)S(1)}, f32[96,128]{1,0:T(8,128)S(1)}, u32[]{:S(2)}, u32[]{:S(2)}) collective-permute-start(f32[96,128]{1,0:T(8,128)S(1)} %add.71), channel_id=1, source_target_pairs={{0,24},{8,16},{16,8},{24,0},{32,56},{40,48},{48,40},{56,32},{64,88... | collective-permute-start | bytes 147464 | tf_op jit(solution)/shard_map/ppermute | solution.py:40
  118.9 3.5 %collective-permute-start.17 = (f32[96,128]{1,0:T(8,128)S(1)}, f32[96,128]{1,0:T(8,128)S(1)}, u32[]{:S(2)}, u32[]{:S(2)}) collective-permute-start(f32[96,128]{1,0:T(8,128)S(1)} %add.72), channel_id=1, source_target_pairs={{0,32},{8,40},{16,48},{24,56},{32,0},{40,8},{48,16},{56,24},{64,96... | collective-permute-start | bytes 147464 | tf_op jit(solution)/shard_map/ppermute | solution.py:40
  122.4 8.6 %collective-permute-start.18 = (f32[96,128]{1,0:T(8,128)S(1)}, f32[96,128]{1,0:T(8,128)S(1)}, u32[]{:S(2)}, u32[]{:S(2)}) collective-permute-start(f32[96,128]{1,0:T(8,128)S(1)} %add.73), channel_id=1, source_target_pairs={{0,96},{8,104},{16,112},{24,120},{32,64},{40,72},{48,80},{56,88},{... | collective-permute-start | bytes 147464 | tf_op jit(solution)/shard_map/ppermute | solution.py:40
  130.9 12.6 %collective-permute-start.19 = (f32[96,128]{1,0:T(8,128)S(1)}, f32[96,128]{1,0:T(8,128)S(1)}, u32[]{:S(2)}, u32[]{:S(2)}) collective-permute-start(f32[96,128]{1,0:T(8,128)S(1)} %add.74.mine), channel_id=1, source_target_pairs={{0,1},{1,0},{2,3},{3,2},{4,5},{5,4},{6,7},{7,6},{8,9},{9,8},{10,11... | collective-permute-start | bytes 147464 | tf_op jit(solution)/shard_map/ppermute | solution.py:41

commit v2 on v1

--- a/solution.py
+++ b/solution.py
@@ -13,6 +13,7 @@
 NT = (((1,), (1,)), ((), ()))
 TN = (((0,), (0,)), ((), ()))
 NN = (((1,), (0,)), ((), ()))
+ZEROS = jax.ShapeDtypeStruct((8, 128), jnp.float32)
 
 
 def dot32(a, b, dims):
@@ -31,20 +32,27 @@
     return jnp.concatenate([first, second], 0)
 
 
-def all_sum(mine, theirs, sub, dom):
+def all_sum(mine, theirs, sub, dom, work=()):
     twin = [(i, i ^ 1) for i in range(sub)]
     mine = mine + lax.ppermute(theirs, "sub", twin)
-    for axis, count, flip in (
-        ("sub", sub, 2), ("sub", sub, 6), ("dom", dom, 1), ("dom", dom, 3), ("dom", dom, 4), ("dom", dom, 12)
-    ):
-        mine = mine + lax.ppermute(mine, axis, [(i, i ^ flip) for i in range(count)])
+    steps = [
+        ("dom", dom, 4), ("dom", dom, 12), ("dom", dom, 1), ("dom", dom, 3), ("sub", sub, 2), ("sub", sub, 6)
+    ]
+    for at, (axis, count, flip) in enumerate(steps):
+        got = lax.ppermute(mine, axis, [(i, i ^ flip) for i in range(count)])
+        if at < len(work) and work[at] is not None:
+            zeros = work[at](mine)
+            mine = (mine + got) + zeros[:1]
+        else:
+            mine = mine + got
     return mine, lax.ppermute(mine, "sub", twin)
 
 
-def to_both(block, devices):
-    before = lax.ppermute(block, AXES, [(i, i + 1) for i in range(devices - 1)])
-    after = lax.ppermute(block, AXES, [(i + 1, i) for i in range(devices - 1)])
-    return before, after
+def neighbour_blocks(block, sub, devices):
+    pairs = [(i, i + 1) for i in range(1, devices - 1, 2)]
+    other = lax.ppermute(block, AXES, pairs + [(j, i) for i, j in pairs])
+    twin = lax.ppermute(block, "sub", [(i, i ^ 1) for i in range(sub)])
+    return twin, other
 
 
 def load_kernel(odd, tiles_hbm, x, p, tiles, gram, sems):
@@ -108,10 +116,10 @@
 
 
 def first_kernel(
-    per, nb, table, odd, tiles, own, before, after, x, p, gram, x_image, p_image, mine, theirs, slabs, images
+    per, nb, table, odd, tiles, own, twin, other, x, p, gram, x_image, p_image, mine, theirs, slabs, images
 ):
     count, size, cols = tiles.shape[0], tiles.shape[2], x.shape[0]
-    fill_slabs(slabs, (before, own, after), count, size)
+    fill_slabs(slabs, (own, twin, other), count, size)
     multiply_tiles(nb, table, tiles, slabs, images, count, per)
     image = images[:cols]
     x_image[...] = image
@@ -126,7 +134,7 @@
     return jax.ShapeDtypeStruct((3 * cols // 2, 2 * cols), jnp.float32)
 
 
-def first_images(nb, table, odd, tiles, own, before, after, x, p, gram):
+def first_images(nb, table, odd, tiles, own, twin, other, x, p, gram):
     count, size, cols = tiles.shape[0], tiles.shape[2], x.shape[0]
     vmem = pl.BlockSpec(memory_space=pltpu.VMEM)
     smem = pl.BlockSpec(memory_space=pltpu.SMEM)
@@ -146,36 +154,40 @@
         ],
         compiler_params=pltpu.CompilerParams(vmem_limit_bytes=16 * MIB),
         cost_estimate=pl.CostEstimate(flops=10000000000, bytes_accessed=4000000, transcendentals=0),
-    )(nb, table, odd, pltpu.with_memory_space_constraint(tiles, pltpu.VMEM), own, before, after, x, p, gram)
-
-
-def middle_kernel(x, r, p, p_image, packed):
-    packed[...] = dot32(jnp.concatenate([x[...], r[...], p[...]], 0), p_image[...], NT)
-
-
-def middle_products(x, r, p, p_image):
+    )(nb, table, odd, pltpu.with_memory_space_constraint(tiles, pltpu.VMEM), own, twin, other, x, p, gram)
+
+
+def middle_kernel(sent, x, x_image, p, p_image, packed, zeros):
+    zeros[...] = jnp.zeros_like(zeros)
+    packed[...] = dot32(jnp.concatenate([x[...], x_image[...], p[...]], 0), p_image[...], NT)
+
+
+def middle_products(sent, x, x_image, p, p_image):
     vmem = pl.BlockSpec(memory_space=pltpu.VMEM)
     return pl.pallas_call(
         middle_kernel,
-        out_shape=jax.ShapeDtypeStruct((3 * x.shape[0], x.shape[0]), jnp.float32),
-        in_specs=[vmem] * 4,
-        out_specs=vmem,
+        out_shape=(jax.ShapeDtypeStruct((3 * x.shape[0], x.shape[0]), jnp.float32), ZEROS),
+        in_specs=[pl.BlockSpec(memory_space=pl.ANY)] + [vmem] * 4,
+        out_specs=(vmem, vmem),
         compiler_params=pltpu.CompilerParams(vmem_limit_bytes=4 * MIB),
         cost_estimate=pl.CostEstimate(flops=1500000000, bytes_accessed=3000000, transcendentals=0),
-    )(x, r, p, p_image)
+    )(sent, x, x_image, p, p_image)
 
 
 def second_kernel(
-    per, nb, table, odd, tiles, own, before, after, x, r, p, middle, r_image, mine, theirs, slabs
+    per, nb, table, odd, tiles, own, twin, other, x, r, p, middle, quotient, parts, r_image, mine, theirs, slabs
 ):
     count, size = tiles.shape[0], tiles.shape[2]
-    fill_slabs(slabs, (before, own, after), count, size)
+    fill_slabs(slabs, (own, twin, other), count, size)
     multiply_tiles(nb, table, tiles, slabs, r_image, count, per)
     cross = dot32(jnp.concatenate([x[...], r[...], p[...]], 0), r_image[...], NT)
-    split(odd, jnp.concatenate([cross, middle[...]], 1), mine, theirs)
-
-
-def second_images(nb, table, odd, tiles, own, before, after, x, r, p, middle):
+    c = x.shape[0]
+    xp, ip, pp = middle[:c], middle[c : 2 * c], middle[2 * c :]
+    rp = ip - dot32(quotient[...], xp, TN)
+    split(odd, jnp.concatenate([cross, jnp.concatenate([xp, rp, pp], 0)], 1), mine, theirs)
+
+
+def second_images(nb, table, odd, tiles, own, twin, other, x, r, p, middle, quotient, parts):
     count, size, cols = tiles.shape[0], tiles.shape[2], x.shape[0]
     vmem = pl.BlockSpec(memory_space=pltpu.VMEM)
     smem = pl.BlockSpec(memory_space=pltpu.SMEM)
@@ -186,12 +198,12 @@
             half_of(cols),
             half_of(cols),
         ),
-        in_specs=[smem, smem] + [vmem] * 9,
+        in_specs=[smem, smem] + [vmem] * 10 + [pl.BlockSpec(memory_space=pl.ANY)],
         out_specs=(vmem,) * 3,
         scratch_shapes=[pltpu.VMEM((3 * count, cols, size), jnp.bfloat16)],
         compiler_params=pltpu.CompilerParams(vmem_limit_bytes=16 * MIB),
         cost_estimate=pl.CostEstimate(flops=10000000000, bytes_accessed=4000000, transcendentals=0),
-    )(nb, table, odd, pltpu.with_memory_space_constraint(tiles, pltpu.VMEM), own, before, after, x, r, p, middle)
+    )(nb, table, odd, pltpu.with_memory_space_constraint(tiles, pltpu.VMEM), own, twin, other, x, r, p, middle, quotient, parts)
 
 
 def cholesky_inverse(a):
@@ -258,7 +270,7 @@
     )(odd, mine, theirs, x, x_image)
 
 
-def factor_kernel(total, packed, quotient, x_inverse, inverse, r_cross):
+def factor_kernel(total, packed, quotient, x_inverse, parts):
     c = quotient.shape[0]
     q = quotient[...]
     xx, px, pp = packed[:c, :c], packed[c : 2 * c, :c], packed[2 * c :, :c]
@@ -267,75 +279,99 @@
     ri = ii - dot32(q, xi, TN)
     rr = ri - dot32(rx, q, NN)
     pr = pi - dot32(px, q, NN)
-    r_cross[...] = ri
     scale = 1.0 / total
     w1 = x_inverse[...] * (total**0.5)
     l21, l31 = dot32(rx * scale, w1, NT), dot32(px * scale, w1, NT)
     w2 = cholesky_inverse(rr * scale - dot32(l21, l21, NT))
     l32 = dot32(pr * scale - dot32(l31, l21, NT), w2, NT)
-    w3 = cholesky_inverse(pp * scale - dot32(l31, l31, NT) - dot32(l32, l32, NT))
+    last = pp * scale - dot32(l31, l31, NT) - dot32(l32, l32, NT)
+    for at, part in enumerate((w1, w2, l21, l31, l32, last, ri)):
+        parts[at] = part
+
+
+def factor(total, packed, quotient, x_inverse):
+    c = quotient.shape[0]
+    vmem = pl.BlockSpec(memory_space=pltpu.VMEM)
+    return pl.pallas_call(
+        functools.partial(factor_kernel, total),
+        out_shape=jax.ShapeDtypeStruct((7, c, c), jnp.float32),
+        in_specs=[vmem] * 3,
+        out_specs=vmem,
+        compiler_params=pltpu.CompilerParams(vmem_limit_bytes=4 * MIB),
+        cost_estimate=pl.CostEstimate(flops=2000000000, bytes_accessed=3000000, transcendentals=0),
+    )(packed, quotient, x_inverse)
+
+
+def inverse_kernel(sent, parts, inverse, zeros):
+    zeros[...] = jnp.zeros_like(zeros)
+    w1, w2, l21, l31, l32 = parts[0], parts[1], parts[2], parts[3], parts[4]
     w21 = -dot32(w2, dot32(l21, w1, NN), NN)
-    w32 = -dot32(w3, dot32(l32, w2, NN), NN)
-    w31 = -dot32(w3, dot32(l31, w1, NN) + dot32(l32, w21, NN), NN)
+    below = dot32(l31, w1, NN) + dot32(l32, w21, NN)
+    beside = dot32(l32, w2, NN)
+    w3 = cholesky_inverse(parts[5])
+    w3_below = -dot32(w3, jnp.concatenate([below, beside], 1), NN)
     zero = jnp.zeros_like(w1)
     inverse[...] = jnp.concatenate(
         [
             jnp.concatenate([w1, zero, zero], 1),
             jnp.concatenate([w21, w2, zero], 1),
-            jnp.concatenate([w31, w32, w3], 1),
+            jnp.concatenate([w3_below, w3], 1),
         ],
         0,
     )
 
 
-def factor(total, packed, quotient, x_inverse):
-    c = quotient.shape[0]
-    vmem = pl.BlockSpec(memory_space=pltpu.VMEM)
-    return pl.pallas_call(
-        functools.partial(factor_kernel, total),
-        out_shape=(
-            jax.ShapeDtypeStruct((3 * c, 3 * c), jnp.float32),
-            jax.ShapeDtypeStruct((c, c), jnp.float32),
-        ),
-        in_specs=[vmem] * 3,
-        out_specs=(vmem,) * 2,
-        compiler_params=pltpu.CompilerParams(vmem_limit_bytes=16 * MIB),
-        cost_estimate=pl.CostEstimate(flops=3000000000, bytes_accessed=3000000, transcendentals=0),
-    )(packed, quotient, x_inverse)
-
-
-def basis_kernel(inverse, x, r, p, x_image, r_image, p_image, basis, basis_image):
+def inverse_of(sent, parts):
+    width = 3 * parts.shape[1]
+    vmem = pl.BlockSpec(memory_space=pltpu.VMEM)
+    return pl.pallas_call(
+        inverse_kernel,
+        out_shape=(jax.ShapeDtypeStruct((width, width), jnp.float32), ZEROS),
+        in_specs=[pl.BlockSpec(memory_space=pl.ANY), vmem],
+        out_specs=(vmem, vmem),
+        compiler_params=pltpu.CompilerParams(vmem_limit_bytes=4 * MIB),
+        cost_estimate=pl.CostEstimate(flops=2000000000, bytes_accessed=3000000, transcendentals=0),
+    )(sent, parts)
+
+
+def basis_kernel(extra, sent, inverse, x, r, p, x_image, r_image, p_image, *rest):
+    basis, basis_image, zeros = rest[extra:]
+    zeros[...] = jnp.zeros_like(zeros)
     w = inverse[...]
     basis[...] = dot32(w, jnp.concatenate([x[...], r[...], p[...]], 0), NN)
     basis_image[...] = dot32(w, jnp.concatenate([x_image[...], r_image[...], p_image[...]], 0), NN)
 
 
-def bases(inverse, *blocks):
+def bases(part, parts, sent, inverse, blocks, done):
     width, rows = inverse.shape[0], blocks[0].shape[1]
     cols = blocks[0].shape[0]
-    tile = 512
-    block = pl.BlockSpec((cols, tile), lambda i: (0, i))
-    out = pl.BlockSpec((width, tile), lambda i: (0, i))
-    return pl.pallas_call(
-        basis_kernel,
-        grid=(rows // tile,),
-        out_shape=(jax.ShapeDtypeStruct((width, rows), jnp.float32),) * 2,
-        in_specs=[pl.BlockSpec((width, width), lambda i: (0, 0))] + [block] * 6,
-        out_specs=(out, out),
-        compiler_params=pltpu.CompilerParams(vmem_limit_bytes=16 * MIB),
-        cost_estimate=pl.CostEstimate(flops=2700000000, bytes_accessed=10000000, transcendentals=0),
-    )(inverse, *blocks)
-
-
-def project_kernel(total, odd, inverse, packed, r_cross, mine, theirs, projected):
-    c = r_cross.shape[0]
-    left = jnp.concatenate([packed[:c, c:], r_cross[...], packed[2 * c :, c:]], 0)
+    tile = 384
+    steps = rows // tile // parts
+    first = part * steps
+    whole = pl.BlockSpec(memory_space=pl.ANY)
+    block = pl.BlockSpec((cols, tile), lambda i: (0, first + i))
+    out = pl.BlockSpec((width, tile), lambda i: (0, first + i))
+    return pl.pallas_call(
+        functools.partial(basis_kernel, len(done)),
+        grid=(steps,),
+        out_shape=(jax.ShapeDtypeStruct((width, rows), jnp.float32),) * 2 + (ZEROS,),
+        in_specs=[whole, pl.BlockSpec((width, width), lambda i: (0, 0))] + [block] * 6 + [whole] * len(done),
+        out_specs=(out, out, pl.BlockSpec((8, 128), lambda i: (0, 0))),
+        input_output_aliases={8 + i: i for i in range(len(done))},
+        compiler_params=pltpu.CompilerParams(vmem_limit_bytes=12 * MIB),
+        cost_estimate=pl.CostEstimate(flops=2000000000, bytes_accessed=3000000, transcendentals=0),
+    )(sent, inverse, *blocks, *done)
+
+
+def project_kernel(total, odd, inverse, packed, parts, mine, theirs, projected):
+    c = parts.shape[1]
+    left = jnp.concatenate([packed[:c, c:], parts[6], packed[2 * c :, c:]], 0)
     w = inverse[...]
     cross = jnp.concatenate([left, join(odd, mine[...], theirs[...])], 1)
     projected[...] = dot32(dot32(w, cross, NN), w, NT) * (1.0 / total)
 
 
-def project(total, odd, inverse, packed, r_cross, mine, theirs):
+def project(total, odd, inverse, packed, parts, mine, theirs):
     vmem = pl.BlockSpec(memory_space=pltpu.VMEM)
     return pl.pallas_call(
         functools.partial(project_kernel, total),
@@ -343,7 +379,7 @@
         in_specs=[vmem] * 6,
         out_specs=vmem,
         compiler_params=pltpu.CompilerParams(vmem_limit_bytes=16 * MIB),
-    )(odd, inverse, packed, r_cross, mine, theirs)
+    )(odd, inverse, packed, parts, mine, theirs)
 
 
 def shards(sub, dom, tile_blocks, neighbours, send_groups, block_x, block_p):
@@ -353,28 +389,55 @@
     x, p = block_x.T, block_p.T
     lists = jnp.pad(send_groups.astype(jnp.bfloat16)[None], ((0, 2 * cols - 1), (0, 128 - 2 * count)))
     both = jnp.concatenate([jnp.concatenate([x, p], 0).astype(jnp.bfloat16), lists], 1)
-    before, after = to_both(both, devices)
+    odd = jnp.broadcast_to(lax.axis_index("sub") % 2, (8, 2 * cols)).astype(jnp.float32)
+    twin, other = neighbour_blocks(both, sub, devices)
+    twin_list = twin[0, rows : rows + 2 * count].astype(jnp.int32) + count
+    other_list = other[0, rows : rows + 2 * count].astype(jnp.int32) + 2 * count
+    first_half = odd[0, :count] > 0
     table = jnp.concatenate(
         [
-            before[0, rows + count : rows + 2 * count].astype(jnp.int32),
-            jnp.arange(count, 2 * count, dtype=jnp.int32),
-            after[0, rows : rows + count].astype(jnp.int32) + 2 * count,
+            jnp.where(first_half, twin_list[count:], other_list[count:]),
+            jnp.arange(count, dtype=jnp.int32),
+            jnp.where(first_half, other_list[:count], twin_list[:count]),
         ]
     )
-    odd = jnp.broadcast_to(lax.axis_index("sub") % 2, (8, 2 * cols)).astype(jnp.float32)
     tiles, gram = load(odd, tile_blocks, x, p)
-    x_image, p_image, *halves = first_images(neighbours, table, odd, tiles, both, before, after, x, p, gram)
-    halves = all_sum(*halves, sub, dom)
+    x_image, p_image, *halves = first_images(neighbours, table, odd, tiles, both, twin, other, x, p, gram)
+    made = {}
+
+    def step(name, make):
+        def run(sent):
+            *values, zeros = make(sent)
+            made[name] = values
+            return zeros
+
+        return run
+
+    halves = all_sum(
+        *halves, sub, dom, [step("middle", lambda sent: middle_products(sent, x, x_image, p, p_image))]
+    )
     packed, quotient, x_inverse, residual, r_round = residual_of(odd, *halves, x, x_image)
-    r_before, r_after = to_both(r_round, devices)
-    middle = middle_products(x, residual, p, p_image)
+    r_twin, r_other = neighbour_blocks(r_round, sub, devices)
+    parts = factor(total, packed, quotient, x_inverse)
     r_image, *halves = second_images(
-        neighbours, table, odd, tiles, r_round, r_before, r_after, x, residual, p, middle
-    )
-    halves = all_sum(*halves, sub, dom)
-    inverse, r_cross = factor(total, packed, quotient, x_inverse)
-    basis, basis_image = bases(inverse, x, residual, p, x_image, r_image, p_image)
-    projected = project(total, odd, inverse, packed, r_cross, *halves)
+        neighbours, table, odd, tiles, r_round, r_twin, r_other, x, residual, p, made["middle"][0], quotient, parts
+    )
+    blocks = (x, residual, p, x_image, r_image, p_image)
+    made["bases"] = []
+    pieces = 4
+    work = [
+        step("inverse", lambda sent: inverse_of(sent, parts)),
+    ]
+    for piece in range(pieces):
+        work.append(
+            step(
+                "bases",
+                lambda sent, piece=piece: bases(piece, pieces, sent, made["inverse"][0], blocks, made["bases"]),
+            )
+        )
+    halves = all_sum(*halves, sub, dom, work)
+    basis, basis_image = made["bases"]
+    projected = project(total, odd, made["inverse"][0], packed, parts, *halves)
     return basis.T, basis_image.T, projected
 
 

time: 145 us -> 130 us (0.90)
  starting transfers between devices: 62.2 us -> 42.1 us
  Pallas kernels: 51.7 us -> 55.5 us
    ppermute x16, starting transfers between devices: 48.3 us -> 28.3 us  [the longest x12 21.6 us: all_sum(): got = lax.ppermute(mine, axis, [(i, i ^ flip) for i in range(count)])]
    pallas_call x3 -> x7, Pallas kernels: 13.3 us -> 17 us  [the longest x4 9.74 us: bases(): pl.pallas_call(functools.partial(basis_kernel, len(done)), grid=(steps,),...]
  transfers between devices with their start and end apart: 20 -> 20, of which waited for: 16 -> 15; matrix products, arithmetic and copies ran while one was open for 0% -> 0% of each run, Pallas kernels for 16% -> 20%
where the time goes in v2:
time: 130 us; the launch traced here: 129 us
  Pallas kernels  55.5 us (43%)
  starting transfers between devices  42.1 us (32%)
  waiting for transfers between devices  27.7 us (21%)
  other arithmetic  3.23 us (2%)
    ppermute x12, starting transfers between devices, all_sum(): got = lax.ppermute(mine, axis, [(i, i ^ flip) for i in range(count)])  21.6 us
    ppermute x12, waiting for transfers between devices, all_sum(): got = lax.ppermute(mine, axis, [(i, i ^ flip) for i in range(count)])  19.3 us
    ppermute x2, starting transfers between devices, all_sum(): return (mine, lax.ppermute(mine, 'sub', twin))  13.5 us
    pallas_call x1, Pallas kernels, first_images(): pl.pallas_call(functools.partial(first_kernel, 4), out_shape=(jax.ShapeDt...  12.7 us
    pallas_call x1, Pallas kernels, second_images(): pl.pallas_call(functools.partial(second_kernel, 4), out_shape=(jax.ShapeD...  11.7 us
    pallas_call x4, Pallas kernels, bases(): pl.pallas_call(functools.partial(basis_kernel, len(done)), grid=(steps,),...  9.74 us
    pallas_call x1, Pallas kernels, load(): pl.pallas_call(load_kernel, out_shape=(pltpu.VMEM(tiles.shape, tiles.dtyp...  9.41 us
    ppermute x2, starting transfers between devices, neighbour_blocks(): other = lax.ppermute(block, AXES, pairs + [(j, i) for i, j in pairs])  6.52 us
  transfers between devices with their start and end apart: 20, of which 15 were waited for; matrix products, arithmetic and copies ran while one was open for 0% of the time, Pallas kernels for 20%

profile of v2, /device:TPU:1, one launch (start us, length us, event | category | flops | bytes accessed | tf_op | source)
XLA Modules:
  0.0 129.4 jit_solution(12427488540865768191)
XLA Ops:
  3.0 4.6 %collective-permute-start.1 = (bf16[128,3200]{1,0:T(8,128)(2,1)S(1)}, bf16[128,3200]{1,0:T(8,128)(2,1)S(1)}, u32[]{:S(2)}, u32[]{:S(2)}) collective-permute-start(bf16[128,3200]{1,0:T(8,128)(2,1)S(1)} %fusion.1.own), channel_id=1, source_target_pairs={{1,2},{3,4},{5,6},{7,8},{9,10},{11,12},{13,14},{15,16},{17,18},{19... | collective-permute-start | bytes 2457608 | tf_op jit(solution)/shard_map/ppermute | solution.py:53
  7.7 9.4 %shard_map.76 = (bf16[16,18,192,192]{3,2,1,0:T(8,128)(2,1)S(1)}, f32[128,128]{1,0:T(8,128)S(1)}) custom-call(f32[8,128]{1,0:T(8,128)S(1)} %broadcast_in_dim.7.odd, bf16[16,18,192,192]{3,2,1,0:T(8,128)(2,1)} %tiles_hbm.1, f32[64,3072]{1,0:T(8,128)S(1)} %bitcast.32, f32[64,3072]{1,0:T(8,128)S(1)} %bitcast.24), custom_call_target="tpu_custom_call" | custom-call | flops 200000000 | bytes 30000000 | tf_op jit(solution)/shard_map/pallas_call | solution.py:76
  18.4 12.7 %shard_map.77 = (f32[64,3072]{1,0:T(8,128)S(1)}, f32[64,3072]{1,0:T(8,128)S(1)}, f32[96,128]{1,0:T(8,128)S(1)}, f32[96,128]{1,0:T(8,128)S(1)}) custom-call(s32[16,18]{1,0:T(8,128)S(1)} %copy-done.2, s32[48]{0:T(128)S(1)} %pad_add_fusion.table, f32[8,128]{1,0:T(8,128)S(1)} %broadcast_in_dim.7.odd, bf16[16,18,192,192]{3,2,1,0:T(8,128)(2,1)S(1)} %get-tuple-element.33.tiles, ...), custom_call_target="tpu_custom_call" | custom-call | flops 10000000000 | bytes 4000000 | tf_op jit(solution)/shard_map/pallas_call | solution.py:141
  32.5 6.1 %collective-permute-start.3 = (f32[96,128]{1,0:T(8,128)S(1)}, f32[96,128]{1,0:T(8,128)S(1)}, u32[]{:S(2)}, u32[]{:S(2)}) collective-permute-start(f32[96,128]{1,0:T(8,128)S(1)} %add.127.sent), channel_id=1, source_target_pairs={{0,32},{8,40},{16,48},{24,56},{32,0},{40,8},{48,16},{56,24},{64,96... | collective-permute-start | bytes 147464 | tf_op jit(solution)/shard_map/ppermute | solution.py:42
  38.5 2.0 %shard_map.78 = (f32[192,64]{1,0:T(8,128)S(1)}, f32[8,128]{1,0:T(8,128)S(1)}) custom-call(f32[96,128]{1,0:T(8,128)S(1)} %add.127.sent, f32[64,3072]{1,0:T(8,128)S(1)} %bitcast.34, f32[64,3072]{1,0:T(8,128)S(1)} %get-tuple-element.37.x_image, f32[64,3072]{1,0:T(8,128)S(1)} %bitcast.26, f32[64,3072]{1,0:T(8,128)S(1)} %get-tuple-element.38.p_image), custom_call_target="tpu_custom_call" | custom-call | flops 1500000000 | bytes 3000000 | tf_op jit(solution)/shard_map/pallas_call | solution.py:167
  40.6 3.1 %collective-permute-start.4 = (f32[96,128]{1,0:T(8,128)S(1)}, f32[96,128]{1,0:T(8,128)S(1)}, u32[]{:S(2)}, u32[]{:S(2)}) collective-permute-start(f32[96,128]{1,0:T(8,128)S(1)} %add_add_fusion.5), channel_id=1, source_target_pairs={{0,96},{8,104},{16,112},{24,120},{32,64},{40,72},{48,80},{56,88},{... | collective-permute-start | bytes 147464 | tf_op jit(solution)/shard_map/ppermute | solution.py:42
  45.3 2.9 %collective-permute-done.5 = f32[96,128]{1,0:T(8,128)S(1)} collective-permute-done((f32[96,128]{1,0:T(8,128)S(1)}, f32[96,128]{1,0:T(8,128)S(1)}, u32[]{:S(2)}, u32[]{:S(2)}) %collective-permute-start.5) | collective-permute-done | bytes 49184 | tf_op jit(solution)/shard_map/ppermute | solution.py:42
  48.7 3.8 %collective-permute-done.6 = f32[96,128]{1,0:T(8,128)S(1)} collective-permute-done((f32[96,128]{1,0:T(8,128)S(1)}, f32[96,128]{1,0:T(8,128)S(1)}, u32[]{:S(2)}, u32[]{:S(2)}) %collective-permute-start.6) | collective-permute-done | bytes 49184 | tf_op jit(solution)/shard_map/ppermute | solution.py:42
  52.5 2.9 %collective-permute-done.7 = f32[96,128]{1,0:T(8,128)S(1)} collective-permute-done((f32[96,128]{1,0:T(8,128)S(1)}, f32[96,128]{1,0:T(8,128)S(1)}, u32[]{:S(2)}, u32[]{:S(2)}) %collective-permute-start.7) | collective-permute-done | bytes 49184 | tf_op jit(solution)/shard_map/ppermute | solution.py:42
  55.5 2.3 %collective-permute-start.8 = (f32[96,128]{1,0:T(8,128)S(1)}, f32[96,128]{1,0:T(8,128)S(1)}, u32[]{:S(2)}, u32[]{:S(2)}) collective-permute-start(f32[96,128]{1,0:T(8,128)S(1)} %add.135), channel_id=1, source_target_pairs={{0,6},{1,7},{2,4},{3,5},{4,2},{5,3},{6,0},{7,1},{8,14},{9,15},{10,... | collective-permute-start | bytes 147464 | tf_op jit(solution)/shard_map/ppermute | solution.py:42
  59.7 7.3 %collective-permute-start.9 = (f32[96,128]{1,0:T(8,128)S(1)}, f32[96,128]{1,0:T(8,128)S(1)}, u32[]{:S(2)}, u32[]{:S(2)}) collective-permute-start(f32[96,128]{1,0:T(8,128)S(1)} %add.136.mine), channel_id=1, source_target_pairs={{0,1},{1,0},{2,3},{3,2},{4,5},{5,4},{6,7},{7,6},{8,9},{9,8},{10,11... | collective-permute-start | bytes 147464 | tf_op jit(solution)/shard_map/ppermute | solution.py:48
  67.9 3.0 %shard_map.79 = (f32[192,128]{1,0:T(8,128)S(1)}, f32[64,64]{1,0:T(8,128)S(1)}, f32[64,64]{1,0:T(8,128)S(1)}, f32[64,3072]{1,0:T(8,128)S(1)}, bf16[64,3072]{1,0:T(8,128)(2,1)S(1)}) custom-call(f32[8,128]{1,0:T(8,128)S(1)} %broadcast_in_dim.7.odd, f32[96,128]{1,0:T(8,128)S(1)} %add.136.mine, f32[96,128]{1,0:T(8,128)S(1)} %collective-permute-done.9.theirs, ...), custom_call_target="tpu_custom_call" | custom-call | flops 3000000000 | bytes 3000000 | tf_op jit(solution)/shard_map/pallas_call | solution.py:257
  72.9 3.2 %shard_map.80.parts = f32[7,64,64]{2,1,0:T(8,128)S(1)} custom-call(f32[192,128]{1,0:T(8,128)S(1)} %get-tuple-element.44.packed, f32[64,64]{1,0:T(8,128)S(1)} %get-tuple-element.43.quotient, f32[64,64]{1,0:T(8,128)S(1)} %get-tuple-element.45.x_inverse), custom_call_target="tpu_custom_call" | custom-call | flops 2000000000 | bytes 3000000 | tf_op jit(solution)/shard_map/pallas_call | solution.py:295
  76.1 3.9 %collective-permute-done.11.other = bf16[64,3072]{1,0:T(8,128)(2,1)S(1)} collective-permute-done((bf16[64,3072]{1,0:T(8,128)(2,1)S(1)}, bf16[64,3072]{1,0:T(8,128)(2,1)S(1)}, u32[]{:S(2)}, u32[]{:S(2)}) %collective-permute-start.11) | collective-permute-done | bytes 393248 | tf_op jit(solution)/shard_map/ppermute | solution.py:53
  80.0 11.7 %shard_map.81 = (f32[64,3072]{1,0:T(8,128)S(1)}, f32[96,128]{1,0:T(8,128)S(1)}, f32[96,128]{1,0:T(8,128)S(1)}) custom-call(s32[16,18]{1,0:T(8,128)S(1)} %copy-done.2, s32[48]{0:T(128)S(1)} %pad_add_fusion.table, f32[8,128]{1,0:T(8,128)S(1)} %broadcast_in_dim.7.odd, bf16[16,18,192,192]{3,2,1,0:T(8,128)(2,1)S(1)} %get-tuple-element.33.tiles, ...), custom_call_target="tpu_custom_call" | custom-call | flops 10000000000 | bytes 4000000 | tf_op jit(solution)/shard_map/pallas_call | solution.py:194
  93.0 3.8 %collective-permute-start.13 = (f32[96,128]{1,0:T(8,128)S(1)}, f32[96,128]{1,0:T(8,128)S(1)}, u32[]{:S(2)}, u32[]{:S(2)}) collective-permute-start(f32[96,128]{1,0:T(8,128)S(1)} %add.137.sent), channel_id=1, source_target_pairs={{0,32},{8,40},{16,48},{24,56},{32,0},{40,8},{48,16},{56,24},{64,96... | collective-permute-start | bytes 147464 | tf_op jit(solution)/shard_map/ppermute | solution.py:42
  96.8 2.0 %shard_map.82 = (f32[192,192]{1,0:T(8,128)S(1)}, f32[8,128]{1,0:T(8,128)S(1)}) custom-call(f32[96,128]{1,0:T(8,128)S(1)} %add.137.sent, f32[7,64,64]{2,1,0:T(8,128)S(1)} %shard_map.80.parts), custom_call_target="tpu_custom_call" | custom-call | flops 2000000000 | bytes 3000000 | tf_op jit(solution)/shard_map/pallas_call | solution.py:327
  98.9 4.3 %collective-permute-start.14 = (f32[96,128]{1,0:T(8,128)S(1)}, f32[96,128]{1,0:T(8,128)S(1)}, u32[]{:S(2)}, u32[]{:S(2)}) collective-permute-start(f32[96,128]{1,0:T(8,128)S(1)} %add_add_fusion.4.sent), channel_id=1, source_target_pairs={{0,96},{8,104},{16,112},{24,120},{32,64},{40,72},{48,80},{56,88},{... | collective-permute-start | bytes 147464 | tf_op jit(solution)/shard_map/ppermute | solution.py:42
  103.2 2.4 %shard_map.83 = (f32[192,3072]{1,0:T(8,128)}, f32[192,3072]{1,0:T(8,128)}, f32[8,128]{1,0:T(8,128)S(1)}) custom-call(f32[96,128]{1,0:T(8,128)S(1)} %add_add_fusion.4.sent, f32[192,192]{1,0:T(8,128)S(1)} %get-tuple-element.49.inverse, f32[64,3072]{1,0:T(8,128)S(1)} %bitcast.37, f32[64,3072]{1,0:T(8,128)S(1)} %get-tuple-element.41.r, f32[64,3072]{1,0:T(8,128)S(1)} %bitcast.28, ...), custom_call_target="tpu_custom_call" | custom-call | flops 2000000000 | bytes 3000000 | tf_op jit(solution)/shard_map/pallas_call | solution.py:354
  105.7 2.4 %shard_map.84 = (f32[192,3072]{1,0:T(8,128)}, f32[192,3072]{1,0:T(8,128)}, f32[8,128]{1,0:T(8,128)S(1)}) custom-call(f32[96,128]{1,0:T(8,128)S(1)} %add_add_fusion.3.sent, f32[192,192]{1,0:T(8,128)S(1)} %get-tuple-element.49.inverse, f32[64,3072]{1,0:T(8,128)S(1)} %bitcast.38, ...), custom_call_target="tpu_custom_call", output_to_operand_aliasing={{0}: (8, {}), {1}: (9, {})} | custom-call | flops 2000000000 | bytes 3000000 | tf_op jit(solution)/shard_map/pallas_call | solution.py:354
  109.0 2.4 %shard_map.85 = (f32[192,3072]{1,0:T(8,128)}, f32[192,3072]{1,0:T(8,128)}, f32[8,128]{1,0:T(8,128)S(1)}) custom-call(f32[96,128]{1,0:T(8,128)S(1)} %add_add_fusion.2.sent, f32[192,192]{1,0:T(8,128)S(1)} %get-tuple-element.49.inverse, f32[64,3072]{1,0:T(8,128)S(1)} %bitcast.39, ...), custom_call_target="tpu_custom_call", output_to_operand_aliasing={{0}: (8, {}), {1}: (9, {})} | custom-call | flops 2000000000 | bytes 3000000 | tf_op jit(solution)/shard_map/pallas_call | solution.py:354
  113.2 2.4 %shard_map.86 = (f32[192,3072]{1,0:T(8,128)}, f32[192,3072]{1,0:T(8,128)}, f32[8,128]{1,0:T(8,128)S(1)}) custom-call(f32[96,128]{1,0:T(8,128)S(1)} %add_add_fusion.1.sent, f32[192,192]{1,0:T(8,128)S(1)} %get-tuple-element.49.inverse, f32[64,3072]{1,0:T(8,128)S(1)} %bitcast.40, ...), custom_call_target="tpu_custom_call", output_to_operand_aliasing={{0}: (8, {}), {1}: (9, {})} | custom-call | flops 2000000000 | bytes 3000000 | tf_op jit(solution)/shard_map/pallas_call | solution.py:354
  117.4 3.3 %collective-permute-done.18 = f32[96,128]{1,0:T(8,128)S(1)} collective-permute-done((f32[96,128]{1,0:T(8,128)S(1)}, f32[96,128]{1,0:T(8,128)S(1)}, u32[]{:S(2)}, u32[]{:S(2)}) %collective-permute-start.18) | collective-permute-done | bytes 49184 | tf_op jit(solution)/shard_map/ppermute | solution.py:42
  120.7 6.2 %collective-permute-start.19 = (f32[96,128]{1,0:T(8,128)S(1)}, f32[96,128]{1,0:T(8,128)S(1)}, u32[]{:S(2)}, u32[]{:S(2)}) collective-permute-start(f32[96,128]{1,0:T(8,128)S(1)} %add.158.mine), channel_id=1, source_target_pairs={{0,1},{1,0},{2,3},{3,2},{4,5},{5,4},{6,7},{7,6},{8,9},{9,8},{10,11... | collective-permute-start | bytes 147464 | tf_op jit(solution)/shard_map/ppermute | solution.py:48
  (63 shorter events, 20.1 us)
Async XLA Ops:
  0.6 7.1 %copy-start = (f32[3072,64]{0,1:T(8,128)S(1)}, f32[3072,64]{0,1:T(8,128)}, u32[]{:S(2)}) copy-start(f32[3072,64]{0,1:T(8,128)} %param.9) | copy-start | bytes 2359300
  0.6 7.1 %copy-start.1 = (f32[3072,64]{0,1:T(8,128)S(1)}, f32[3072,64]{0,1:T(8,128)}, u32[]{:S(2)}) copy-start(f32[3072,64]{0,1:T(8,128)} %param.8) | copy-start | bytes 2359300
  3.0 14.6 %collective-permute-start.1 = (bf16[128,3200]{1,0:T(8,128)(2,1)S(1)}, bf16[128,3200]{1,0:T(8,128)(2,1)S(1)}, u32[]{:S(2)}, u32[]{:S(2)}) collective-permute-start(bf16[128,3200]{1,0:T(8,128)(2,1)S(1)} %fusion.1.own), channel_id=1, source_target_pairs={{1,2},{3,4},{5,6},{7,8},{9,10},{11,12},{13,14},{15,16},{17,18},{19... | collective-permute-start | bytes 2457608 | tf_op jit(solution)/shard_map/ppermute | solution.py:53
  7.6 10.0 %collective-permute-start = (bf16[128,3200]{1,0:T(8,128)(2,1)S(1)}, bf16[128,3200]{1,0:T(8,128)(2,1)}, u32[]{:S(2)}, u32[]{:S(2)}) collective-permute-start(bf16[128,3200]{1,0:T(8,128)(2,1)S(1)} %fusion.1.own), channel_id=1, source_target_pairs={{0,1},{1,0},{2,3},{3,2},{4,5},{5,4},{6,7},{7,6},{8,9},{9,8},{10,11... | collective-permute-start | bytes 2457608 | tf_op jit(solution)/shard_map/ppermute | solution.py:54
  7.7 10.7 %copy-start.2 = (s32[16,18]{1,0:T(8,128)S(1)}, s32[16,18]{1,0:T(8,128)}, u32[]{:S(2)}) copy-start(s32[16,18]{1,0:T(8,128)} %nb.3) | copy-start | bytes 3460
  31.2 1.3 %collective-permute-start.2 = (f32[96,128]{1,0:T(8,128)S(1)}, f32[96,128]{1,0:T(8,128)S(1)}, u32[]{:S(2)}, u32[]{:S(2)}) collective-permute-start(f32[96,128]{1,0:T(8,128)S(1)} %get-tuple-element.36), channel_id=1, source_target_pairs={{0,1},{1,0},{2,3},{3,2},{4,5},{5,4},{6,7},{7,6},{8,9},{9,8},{10,11... | collective-permute-start | bytes 147464 | tf_op jit(solution)/shard_map/ppermute | solution.py:37
  32.5 8.1 %collective-permute-start.3 = (f32[96,128]{1,0:T(8,128)S(1)}, f32[96,128]{1,0:T(8,128)S(1)}, u32[]{:S(2)}, u32[]{:S(2)}) collective-permute-start(f32[96,128]{1,0:T(8,128)S(1)} %add.127.sent), channel_id=1, source_target_pairs={{0,32},{8,40},{16,48},{24,56},{32,0},{40,8},{48,16},{56,24},{64,96... | collective-permute-start | bytes 147464 | tf_op jit(solution)/shard_map/ppermute | solution.py:42
  40.6 4.6 %collective-permute-start.4 = (f32[96,128]{1,0:T(8,128)S(1)}, f32[96,128]{1,0:T(8,128)S(1)}, u32[]{:S(2)}, u32[]{:S(2)}) collective-permute-start(f32[96,128]{1,0:T(8,128)S(1)} %add_add_fusion.5), channel_id=1, source_target_pairs={{0,96},{8,104},{16,112},{24,120},{32,64},{40,72},{48,80},{56,88},{... | collective-permute-start | bytes 147464 | tf_op jit(solution)/shard_map/ppermute | solution.py:42
  45.2 3.0 %collective-permute-start.5 = (f32[96,128]{1,0:T(8,128)S(1)}, f32[96,128]{1,0:T(8,128)S(1)}, u32[]{:S(2)}, u32[]{:S(2)}) collective-permute-start(f32[96,128]{1,0:T(8,128)S(1)} %add.132), channel_id=1, source_target_pairs={{0,8},{8,0},{16,24},{24,16},{32,40},{40,32},{48,56},{56,48},{64,72... | collective-permute-start | bytes 147464 | tf_op jit(solution)/shard_map/ppermute | solution.py:42
  48.2 4.2 %collective-permute-start.6 = (f32[96,128]{1,0:T(8,128)S(1)}, f32[96,128]{1,0:T(8,128)S(1)}, u32[]{:S(2)}, u32[]{:S(2)}) collective-permute-start(f32[96,128]{1,0:T(8,128)S(1)} %add.133), channel_id=1, source_target_pairs={{0,24},{8,16},{16,8},{24,0},{32,56},{40,48},{48,40},{56,32},{64,88... | collective-permute-start | bytes 147464 | tf_op jit(solution)/shard_map/ppermute | solution.py:42
  52.4 3.0 %collective-permute-start.7 = (f32[96,128]{1,0:T(8,128)S(1)}, f32[96,128]{1,0:T(8,128)S(1)}, u32[]{:S(2)}, u32[]{:S(2)}) collective-permute-start(f32[96,128]{1,0:T(8,128)S(1)} %add.134), channel_id=1, source_target_pairs={{0,2},{1,3},{2,0},{3,1},{4,6},{5,7},{6,4},{7,5},{8,10},{9,11},{10,... | collective-permute-start | bytes 147464 | tf_op jit(solution)/shard_map/ppermute | solution.py:42
  55.5 4.2 %collective-permute-start.8 = (f32[96,128]{1,0:T(8,128)S(1)}, f32[96,128]{1,0:T(8,128)S(1)}, u32[]{:S(2)}, u32[]{:S(2)}) collective-permute-start(f32[96,128]{1,0:T(8,128)S(1)} %add.135), channel_id=1, source_target_pairs={{0,6},{1,7},{2,4},{3,5},{4,2},{5,3},{6,0},{7,1},{8,14},{9,15},{10,... | collective-permute-start | bytes 147464 | tf_op jit(solution)/shard_map/ppermute | solution.py:42
  59.7 8.2 %collective-permute-start.9 = (f32[96,128]{1,0:T(8,128)S(1)}, f32[96,128]{1,0:T(8,128)S(1)}, u32[]{:S(2)}, u32[]{:S(2)}) collective-permute-start(f32[96,128]{1,0:T(8,128)S(1)} %add.136.mine), channel_id=1, source_target_pairs={{0,1},{1,0},{2,3},{3,2},{4,5},{5,4},{6,7},{7,6},{8,9},{9,8},{10,11... | collective-permute-start | bytes 147464 | tf_op jit(solution)/shard_map/ppermute | solution.py:48
  70.9 9.1 %collective-permute-start.11 = (bf16[64,3072]{1,0:T(8,128)(2,1)S(1)}, bf16[64,3072]{1,0:T(8,128)(2,1)S(1)}, u32[]{:S(2)}, u32[]{:S(2)}) collective-permute-start(bf16[64,3072]{1,0:T(8,128)(2,1)S(1)} %get-tuple-element.40.own), channel_id=1, source_target_pairs={{1,2},{3,4},{5,6},{7,8},{9,10},{11,12},{13,14},{15,16},{17,18},{19... | collective-permute-start | bytes 1179656 | tf_op jit(solution)/shard_map/ppermute | solution.py:53
  72.8 7.2 %collective-permute-start.10 = (bf16[64,3072]{1,0:T(8,128)(2,1)S(1)}, bf16[64,3072]{1,0:T(8,128)(2,1)S(1)}, u32[]{:S(2)}, u32[]{:S(2)}) collective-permute-start(bf16[64,3072]{1,0:T(8,128)(2,1)S(1)} %get-tuple-element.40.own), channel_id=1, source_target_pairs={{0,1},{1,0},{2,3},{3,2},{4,5},{5,4},{6,7},{7,6},{8,9},{9,8},{10,11... | collective-permute-start | bytes 1179656 | tf_op jit(solution)/shard_map/ppermute | solution.py:54
  91.7 1.3 %collective-permute-start.12 = (f32[96,128]{1,0:T(8,128)S(1)}, f32[96,128]{1,0:T(8,128)S(1)}, u32[]{:S(2)}, u32[]{:S(2)}) collective-permute-start(f32[96,128]{1,0:T(8,128)S(1)} %get-tuple-element.47), channel_id=1, source_target_pairs={{0,1},{1,0},{2,3},{3,2},{4,5},{5,4},{6,7},{7,6},{8,9},{9,8},{10,11... | collective-permute-start | bytes 147464 | tf_op jit(solution)/shard_map/ppermute | solution.py:37
  93.0 5.9 %collective-permute-start.13 = (f32[96,128]{1,0:T(8,128)S(1)}, f32[96,128]{1,0:T(8,128)S(1)}, u32[]{:S(2)}, u32[]{:S(2)}) collective-permute-start(f32[96,128]{1,0:T(8,128)S(1)} %add.137.sent), channel_id=1, source_target_pairs={{0,32},{8,40},{16,48},{24,56},{32,0},{40,8},{48,16},{56,24},{64,96... | collective-permute-start | bytes 147464 | tf_op jit(solution)/shard_map/ppermute | solution.py:42
  98.9 6.7 %collective-permute-start.14 = (f32[96,128]{1,0:T(8,128)S(1)}, f32[96,128]{1,0:T(8,128)S(1)}, u32[]{:S(2)}, u32[]{:S(2)}) collective-permute-start(f32[96,128]{1,0:T(8,128)S(1)} %add_add_fusion.4.sent), channel_id=1, source_target_pairs={{0,96},{8,104},{16,112},{24,120},{32,64},{40,72},{48,80},{56,88},{... | collective-permute-start | bytes 147464 | tf_op jit(solution)/shard_map/ppermute | solution.py:42
  105.6 3.0 %collective-permute-start.15 = (f32[96,128]{1,0:T(8,128)S(1)}, f32[96,128]{1,0:T(8,128)S(1)}, u32[]{:S(2)}, u32[]{:S(2)}) collective-permute-start(f32[96,128]{1,0:T(8,128)S(1)} %add_add_fusion.3.sent), channel_id=1, source_target_pairs={{0,8},{8,0},{16,24},{24,16},{32,40},{40,32},{48,56},{56,48},{64,72... | collective-permute-start | bytes 147464 | tf_op jit(solution)/shard_map/ppermute | solution.py:42
  108.7 4.5 %collective-permute-start.16 = (f32[96,128]{1,0:T(8,128)S(1)}, f32[96,128]{1,0:T(8,128)S(1)}, u32[]{:S(2)}, u32[]{:S(2)}) collective-permute-start(f32[96,128]{1,0:T(8,128)S(1)} %add_add_fusion.2.sent), channel_id=1, source_target_pairs={{0,24},{8,16},{16,8},{24,0},{32,56},{40,48},{48,40},{56,32},{64,88... | collective-permute-start | bytes 147464 | tf_op jit(solution)/shard_map/ppermute | solution.py:42
  113.1 3.3 %collective-permute-start.17 = (f32[96,128]{1,0:T(8,128)S(1)}, f32[96,128]{1,0:T(8,128)S(1)}, u32[]{:S(2)}, u32[]{:S(2)}) collective-permute-start(f32[96,128]{1,0:T(8,128)S(1)} %add_add_fusion.1.sent), channel_id=1, source_target_pairs={{0,2},{1,3},{2,0},{3,1},{4,6},{5,7},{6,4},{7,5},{8,10},{9,11},{10,... | collective-permute-start | bytes 147464 | tf_op jit(solution)/shard_map/ppermute | solution.py:42
  116.5 4.2 %collective-permute-start.18 = (f32[96,128]{1,0:T(8,128)S(1)}, f32[96,128]{1,0:T(8,128)S(1)}, u32[]{:S(2)}, u32[]{:S(2)}) collective-permute-start(f32[96,128]{1,0:T(8,128)S(1)} %add_add_fusion), channel_id=1, source_target_pairs={{0,6},{1,7},{2,4},{3,5},{4,2},{5,3},{6,0},{7,1},{8,14},{9,15},{10,... | collective-permute-start | bytes 147464 | tf_op jit(solution)/shard_map/ppermute | solution.py:42
  120.7 7.1 %collective-permute-start.19 = (f32[96,128]{1,0:T(8,128)S(1)}, f32[96,128]{1,0:T(8,128)S(1)}, u32[]{:S(2)}, u32[]{:S(2)}) collective-permute-start(f32[96,128]{1,0:T(8,128)S(1)} %add.158.mine), channel_id=1, source_target_pairs={{0,1},{1,0},{2,3},{3,2},{4,5},{5,4},{6,7},{7,6},{8,9},{9,8},{10,11... | collective-permute-start | bytes 147464 | tf_op jit(solution)/shard_map/ppermute | solution.py:48

commit v3 on v2

--- a/solution.py
+++ b/solution.py
@@ -20,6 +20,17 @@
     return lax.dot_general(a, b, dims, precision=HIGHEST, preferred_element_type=jnp.float32)
 
 
+def halves_of(a):
+    high = a.astype(jnp.bfloat16)
+    return high, (a - high.astype(jnp.float32)).astype(jnp.bfloat16)
+
+
+def dot16(a, b, dims):
+    (a_high, a_low), (b_high, b_low) = halves_of(a), halves_of(b)
+    dot = functools.partial(lax.dot_general, dimension_numbers=dims, preferred_element_type=jnp.float32)
+    return dot(a_high, b_high) + (dot(a_high, b_low) + dot(a_low, b_high))
+
+
 def split(odd, value, mine, theirs):
     half = value.shape[0] // 2
     mine[...] = jnp.where(odd[:1] > 0, value[half:], value[:half])
@@ -35,11 +46,9 @@
 def all_sum(mine, theirs, sub, dom, work=()):
     twin = [(i, i ^ 1) for i in range(sub)]
     mine = mine + lax.ppermute(theirs, "sub", twin)
-    steps = [
-        ("dom", dom, 4), ("dom", dom, 12), ("dom", dom, 1), ("dom", dom, 3), ("sub", sub, 2), ("sub", sub, 6)
-    ]
-    for at, (axis, count, flip) in enumerate(steps):
-        got = lax.ppermute(mine, axis, [(i, i ^ flip) for i in range(count)])
+    y, x, z = (2, 6), (sub, 3 * sub), (4 * sub, 12 * sub)
+    for at, (even, odd) in enumerate(zip(z + x + y, x + y + z)):
+        got = lax.ppermute(mine, AXES, [(i, i ^ (odd if i % 2 else even)) for i in range(sub * dom)])
         if at < len(work) and work[at] is not None:
             zeros = work[at](mine)
             mine = (mine + got) + zeros[:1]
@@ -124,7 +133,7 @@
     image = images[:cols]
     x_image[...] = image
     p_image[...] = images[cols:]
-    cross = dot32(jnp.concatenate([x[...], image, p[...]], 0), image, NT)
+    cross = dot16(jnp.concatenate([x[...], image, p[...]], 0), image, NT)
     g = gram[...]
     left = jnp.concatenate([g[:cols, :cols], g[cols:, :cols], g[cols:, cols:]], 0)
     split(odd, jnp.concatenate([left, cross], 1), mine, theirs)
@@ -159,7 +168,7 @@
 
 def middle_kernel(sent, x, x_image, p, p_image, packed, zeros):
     zeros[...] = jnp.zeros_like(zeros)
-    packed[...] = dot32(jnp.concatenate([x[...], x_image[...], p[...]], 0), p_image[...], NT)
+    packed[...] = dot16(jnp.concatenate([x[...], x_image[...], p[...]], 0), p_image[...], NT)
 
 
 def middle_products(sent, x, x_image, p, p_image):
@@ -180,7 +189,7 @@
     count, size = tiles.shape[0], tiles.shape[2]
     fill_slabs(slabs, (own, twin, other), count, size)
     multiply_tiles(nb, table, tiles, slabs, r_image, count, per)
-    cross = dot32(jnp.concatenate([x[...], r[...], p[...]], 0), r_image[...], NT)
+    cross = dot16(jnp.concatenate([x[...], r[...], p[...]], 0), r_image[...], NT)
     c = x.shape[0]
     xp, ip, pp = middle[:c], middle[c : 2 * c], middle[2 * c :]
     rp = ip - dot32(quotient[...], xp, TN)
@@ -338,14 +347,14 @@
     basis, basis_image, zeros = rest[extra:]
     zeros[...] = jnp.zeros_like(zeros)
     w = inverse[...]
-    basis[...] = dot32(w, jnp.concatenate([x[...], r[...], p[...]], 0), NN)
-    basis_image[...] = dot32(w, jnp.concatenate([x_image[...], r_image[...], p_image[...]], 0), NN)
+    basis[...] = dot16(w, jnp.concatenate([x[...], r[...], p[...]], 0), NN)
+    basis_image[...] = dot16(w, jnp.concatenate([x_image[...], r_image[...], p_image[...]], 0), NN)
 
 
 def bases(part, parts, sent, inverse, blocks, done):
     width, rows = inverse.shape[0], blocks[0].shape[1]
     cols = blocks[0].shape[0]
-    tile = 384
+    tile = 768
     steps = rows // tile // parts
     first = part * steps
     whole = pl.BlockSpec(memory_space=pl.ANY)
@@ -368,7 +377,7 @@
     left = jnp.concatenate([packed[:c, c:], parts[6], packed[2 * c :, c:]], 0)
     w = inverse[...]
     cross = jnp.concatenate([left, join(odd, mine[...], theirs[...])], 1)
-    projected[...] = dot32(dot32(w, cross, NN), w, NT) * (1.0 / total)
+    projected[...] = dot16(dot16(w, cross, NN), w, NT) * (1.0 / total)
 
 
 def project(total, odd, inverse, packed, parts, mine, theirs):

time: 130 us -> 127 us (0.977)
  starting transfers between devices: 42.1 us -> 51.7 us
  Pallas kernels: 55.5 us -> 49.2 us
  waiting for transfers between devices: 27.7 us -> 21.5 us
    ppermute x12, starting transfers between devices: 21.6 us -> 30.4 us  [all_sum(): lax.ppermute(mine, AXES, [(i, i ^ (odd if i % 2 else even)) for i in rang...]
    ppermute x12, waiting for transfers between devices: 19.3 us -> 13.2 us  [all_sum(): lax.ppermute(mine, AXES, [(i, i ^ (odd if i % 2 else even)) for i in rang...]
    pallas_call x4, Pallas kernels: 9.74 us -> 6.6 us  [bases(): pl.pallas_call(functools.partial(basis_kernel, len(done)), grid=(steps,),...]
  transfers between devices with their start and end apart: 20 -> 20, of which waited for: 15 -> 16; matrix products, arithmetic and copies ran while one was open for 0% -> 0% of each run, Pallas kernels for 20% -> 18%
where the time goes in v3:
time: 127 us
  starting transfers between devices  51.7 us (41%)
  Pallas kernels  49.2 us (39%)
  waiting for transfers between devices  21.5 us (17%)
  other arithmetic  3.23 us (3%)
    ppermute x12, starting transfers between devices, all_sum(): lax.ppermute(mine, AXES, [(i, i ^ (odd if i % 2 else even)) for i in rang...  30.4 us
    ppermute x2, starting transfers between devices, all_sum(): return (mine, lax.ppermute(mine, 'sub', twin))  14.2 us
    ppermute x12, waiting for transfers between devices, all_sum(): lax.ppermute(mine, AXES, [(i, i ^ (odd if i % 2 else even)) for i in rang...  13.2 us
    pallas_call x1, Pallas kernels, first_images(): pl.pallas_call(functools.partial(first_kernel, 4), out_shape=(jax.ShapeDt...  11.8 us
    pallas_call x1, Pallas kernels, second_images(): pl.pallas_call(functools.partial(second_kernel, 4), out_shape=(jax.ShapeD...  10.8 us
    pallas_call x1, Pallas kernels, load(): pl.pallas_call(load_kernel, out_shape=(pltpu.VMEM(tiles.shape, tiles.dtyp...  9.41 us
    pallas_call x4, Pallas kernels, bases(): pl.pallas_call(functools.partial(basis_kernel, len(done)), grid=(steps,),...  6.6 us
    ppermute x2, starting transfers between devices, neighbour_blocks(): other = lax.ppermute(block, AXES, pairs + [(j, i) for i, j in pairs])  6.52 us
  transfers between devices with their start and end apart: 20, of which 16 were waited for; matrix products, arithmetic and copies ran while one was open for 0% of the time, Pallas kernels for 18%

profile of v3, /device:TPU:1, one launch (start us, length us, event | category | flops | bytes accessed | tf_op | source)
XLA Modules:
  0.0 126.5 jit_solution(6284179895046530854)
XLA Ops:
  3.0 4.6 %collective-permute-start.1 = (bf16[128,3200]{1,0:T(8,128)(2,1)S(1)}, bf16[128,3200]{1,0:T(8,128)(2,1)S(1)}, u32[]{:S(2)}, u32[]{:S(2)}) collective-permute-start(bf16[128,3200]{1,0:T(8,128)(2,1)S(1)} %fusion.1.own), channel_id=1, source_target_pairs={{1,2},{3,4},{5,6},{7,8},{9,10},{11,12},{13,14},{15,16},{17,18},{19... | collective-permute-start | bytes 2457608 | tf_op jit(solution)/shard_map/ppermute | solution.py:62
  7.7 9.4 %shard_map.76 = (bf16[16,18,192,192]{3,2,1,0:T(8,128)(2,1)S(1)}, f32[128,128]{1,0:T(8,128)S(1)}) custom-call(f32[8,128]{1,0:T(8,128)S(1)} %broadcast_in_dim.7.odd, bf16[16,18,192,192]{3,2,1,0:T(8,128)(2,1)} %tiles_hbm.1, f32[64,3072]{1,0:T(8,128)S(1)} %bitcast.32, f32[64,3072]{1,0:T(8,128)S(1)} %bitcast.24), custom_call_target="tpu_custom_call" | custom-call | flops 200000000 | bytes 30000000 | tf_op jit(solution)/shard_map/pallas_call | solution.py:85
  18.4 11.8 %shard_map.77 = (f32[64,3072]{1,0:T(8,128)S(1)}, f32[64,3072]{1,0:T(8,128)S(1)}, f32[96,128]{1,0:T(8,128)S(1)}, f32[96,128]{1,0:T(8,128)S(1)}) custom-call(s32[16,18]{1,0:T(8,128)S(1)} %copy-done.2, s32[48]{0:T(128)S(1)} %pad_add_fusion.table, f32[8,128]{1,0:T(8,128)S(1)} %broadcast_in_dim.7.odd, bf16[16,18,192,192]{3,2,1,0:T(8,128)(2,1)S(1)} %get-tuple-element.33.tiles, ...), custom_call_target="tpu_custom_call" | custom-call | flops 10000000000 | bytes 4000000 | tf_op jit(solution)/shard_map/pallas_call | solution.py:150
  31.6 3.5 %collective-permute-start.3 = (f32[96,128]{1,0:T(8,128)S(1)}, f32[96,128]{1,0:T(8,128)S(1)}, u32[]{:S(2)}, u32[]{:S(2)}) collective-permute-start(f32[96,128]{1,0:T(8,128)S(1)} %add.127.sent), channel_id=1, source_target_pairs={{0,32},{1,9},{2,34},{3,11},{4,36},{5,13},{6,38},{7,15},{8,40},{9,1... | collective-permute-start | bytes 147464 | tf_op jit(solution)/shard_map/ppermute | solution.py:51
  36.6 2.8 %collective-permute-start.4 = (f32[96,128]{1,0:T(8,128)S(1)}, f32[96,128]{1,0:T(8,128)S(1)}, u32[]{:S(2)}, u32[]{:S(2)}) collective-permute-start(f32[96,128]{1,0:T(8,128)S(1)} %add_add_fusion.5), channel_id=1, source_target_pairs={{0,96},{1,25},{2,98},{3,27},{4,100},{5,29},{6,102},{7,31},{8,104},... | collective-permute-start | bytes 147464 | tf_op jit(solution)/shard_map/ppermute | solution.py:51
  41.0 2.9 %collective-permute-done.5 = f32[96,128]{1,0:T(8,128)S(1)} collective-permute-done((f32[96,128]{1,0:T(8,128)S(1)}, f32[96,128]{1,0:T(8,128)S(1)}, u32[]{:S(2)}, u32[]{:S(2)}) %collective-permute-start.5) | collective-permute-done | bytes 49184 | tf_op jit(solution)/shard_map/ppermute | solution.py:51
  43.9 4.7 %collective-permute-start.6 = (f32[96,128]{1,0:T(8,128)S(1)}, f32[96,128]{1,0:T(8,128)S(1)}, u32[]{:S(2)}, u32[]{:S(2)}) collective-permute-start(f32[96,128]{1,0:T(8,128)S(1)} %add.133), channel_id=1, source_target_pairs={{0,24},{1,7},{2,26},{3,5},{4,28},{5,3},{6,30},{7,1},{8,16},{9,15},... | collective-permute-start | bytes 147464 | tf_op jit(solution)/shard_map/ppermute | solution.py:51
  50.0 2.1 %collective-permute-start.7 = (f32[96,128]{1,0:T(8,128)S(1)}, f32[96,128]{1,0:T(8,128)S(1)}, u32[]{:S(2)}, u32[]{:S(2)}) collective-permute-start(f32[96,128]{1,0:T(8,128)S(1)} %add.134), channel_id=1, source_target_pairs={{0,2},{1,33},{2,0},{3,35},{4,6},{5,37},{6,4},{7,39},{8,10},{9,41},... | collective-permute-start | bytes 147464 | tf_op jit(solution)/shard_map/ppermute | solution.py:51
  53.6 3.7 %collective-permute-start.8 = (f32[96,128]{1,0:T(8,128)S(1)}, f32[96,128]{1,0:T(8,128)S(1)}, u32[]{:S(2)}, u32[]{:S(2)}) collective-permute-start(f32[96,128]{1,0:T(8,128)S(1)} %add.135), channel_id=1, source_target_pairs={{0,6},{1,97},{2,4},{3,99},{4,2},{5,101},{6,0},{7,103},{8,14},{9,10... | collective-permute-start | bytes 147464 | tf_op jit(solution)/shard_map/ppermute | solution.py:51
  58.8 7.1 %collective-permute-start.9 = (f32[96,128]{1,0:T(8,128)S(1)}, f32[96,128]{1,0:T(8,128)S(1)}, u32[]{:S(2)}, u32[]{:S(2)}) collective-permute-start(f32[96,128]{1,0:T(8,128)S(1)} %add.136.mine), channel_id=1, source_target_pairs={{0,1},{1,0},{2,3},{3,2},{4,5},{5,4},{6,7},{7,6},{8,9},{9,8},{10,11... | collective-permute-start | bytes 147464 | tf_op jit(solution)/shard_map/ppermute | solution.py:57
  66.8 3.0 %shard_map.79 = (f32[192,128]{1,0:T(8,128)S(1)}, f32[64,64]{1,0:T(8,128)S(1)}, f32[64,64]{1,0:T(8,128)S(1)}, f32[64,3072]{1,0:T(8,128)S(1)}, bf16[64,3072]{1,0:T(8,128)(2,1)S(1)}) custom-call(f32[8,128]{1,0:T(8,128)S(1)} %broadcast_in_dim.7.odd, f32[96,128]{1,0:T(8,128)S(1)} %add.136.mine, f32[96,128]{1,0:T(8,128)S(1)} %collective-permute-done.9.theirs, ...), custom_call_target="tpu_custom_call" | custom-call | flops 3000000000 | bytes 3000000 | tf_op jit(solution)/shard_map/pallas_call | solution.py:266
  69.8 1.9 %collective-permute-start.11 = (bf16[64,3072]{1,0:T(8,128)(2,1)S(1)}, bf16[64,3072]{1,0:T(8,128)(2,1)S(1)}, u32[]{:S(2)}, u32[]{:S(2)}) collective-permute-start(bf16[64,3072]{1,0:T(8,128)(2,1)S(1)} %get-tuple-element.40.own), channel_id=1, source_target_pairs={{1,2},{3,4},{5,6},{7,8},{9,10},{11,12},{13,14},{15,16},{17,18},{19... | collective-permute-start | bytes 1179656 | tf_op jit(solution)/shard_map/ppermute | solution.py:62
  72.0 3.2 %shard_map.80.parts = f32[7,64,64]{2,1,0:T(8,128)S(1)} custom-call(f32[192,128]{1,0:T(8,128)S(1)} %get-tuple-element.44.packed, f32[64,64]{1,0:T(8,128)S(1)} %get-tuple-element.43.quotient, f32[64,64]{1,0:T(8,128)S(1)} %get-tuple-element.45.x_inverse), custom_call_target="tpu_custom_call" | custom-call | flops 2000000000 | bytes 3000000 | tf_op jit(solution)/shard_map/pallas_call | solution.py:304
  75.2 3.7 %collective-permute-done.11.other = bf16[64,3072]{1,0:T(8,128)(2,1)S(1)} collective-permute-done((bf16[64,3072]{1,0:T(8,128)(2,1)S(1)}, bf16[64,3072]{1,0:T(8,128)(2,1)S(1)}, u32[]{:S(2)}, u32[]{:S(2)}) %collective-permute-start.11) | collective-permute-done | bytes 393248 | tf_op jit(solution)/shard_map/ppermute | solution.py:62
  78.9 10.8 %shard_map.81 = (f32[64,3072]{1,0:T(8,128)S(1)}, f32[96,128]{1,0:T(8,128)S(1)}, f32[96,128]{1,0:T(8,128)S(1)}) custom-call(s32[16,18]{1,0:T(8,128)S(1)} %copy-done.2, s32[48]{0:T(128)S(1)} %pad_add_fusion.table, f32[8,128]{1,0:T(8,128)S(1)} %broadcast_in_dim.7.odd, bf16[16,18,192,192]{3,2,1,0:T(8,128)(2,1)S(1)} %get-tuple-element.33.tiles, ...), custom_call_target="tpu_custom_call" | custom-call | flops 10000000000 | bytes 4000000 | tf_op jit(solution)/shard_map/pallas_call | solution.py:203
  91.6 2.0 %shard_map.82 = (f32[192,192]{1,0:T(8,128)S(1)}, f32[8,128]{1,0:T(8,128)S(1)}) custom-call(f32[96,128]{1,0:T(8,128)S(1)} %add.137.sent, f32[7,64,64]{2,1,0:T(8,128)S(1)} %shard_map.80.parts), custom_call_target="tpu_custom_call" | custom-call | flops 2000000000 | bytes 3000000 | tf_op jit(solution)/shard_map/pallas_call | solution.py:336
  94.0 3.0 %collective-permute-start.14 = (f32[96,128]{1,0:T(8,128)S(1)}, f32[96,128]{1,0:T(8,128)S(1)}, u32[]{:S(2)}, u32[]{:S(2)}) collective-permute-start(f32[96,128]{1,0:T(8,128)S(1)} %add_add_fusion.4.sent), channel_id=1, source_target_pairs={{0,96},{1,25},{2,98},{3,27},{4,100},{5,29},{6,102},{7,31},{8,104},... | collective-permute-start | bytes 147464 | tf_op jit(solution)/shard_map/ppermute | solution.py:51
  97.0 1.6 %shard_map.83 = (f32[192,3072]{1,0:T(8,128)}, f32[192,3072]{1,0:T(8,128)}, f32[8,128]{1,0:T(8,128)S(1)}) custom-call(f32[96,128]{1,0:T(8,128)S(1)} %add_add_fusion.4.sent, f32[192,192]{1,0:T(8,128)S(1)} %get-tuple-element.49.inverse, f32[64,3072]{1,0:T(8,128)S(1)} %bitcast.37, f32[64,3072]{1,0:T(8,128)S(1)} %get-tuple-element.41.r, f32[64,3072]{1,0:T(8,128)S(1)} %bitcast.28, ...), custom_call_target="tpu_custom_call" | custom-call | flops 2000000000 | bytes 3000000 | tf_op jit(solution)/shard_map/pallas_call | solution.py:363
  98.7 1.7 %shard_map.84 = (f32[192,3072]{1,0:T(8,128)}, f32[192,3072]{1,0:T(8,128)}, f32[8,128]{1,0:T(8,128)S(1)}) custom-call(f32[96,128]{1,0:T(8,128)S(1)} %add_add_fusion.3.sent, f32[192,192]{1,0:T(8,128)S(1)} %get-tuple-element.49.inverse, f32[64,3072]{1,0:T(8,128)S(1)} %bitcast.38, ...), custom_call_target="tpu_custom_call", output_to_operand_aliasing={{0}: (8, {}), {1}: (9, {})} | custom-call | flops 2000000000 | bytes 3000000 | tf_op jit(solution)/shard_map/pallas_call | solution.py:363
  101.7 5.5 %collective-permute-start.16 = (f32[96,128]{1,0:T(8,128)S(1)}, f32[96,128]{1,0:T(8,128)S(1)}, u32[]{:S(2)}, u32[]{:S(2)}) collective-permute-start(f32[96,128]{1,0:T(8,128)S(1)} %add_add_fusion.2.sent), channel_id=1, source_target_pairs={{0,24},{1,7},{2,26},{3,5},{4,28},{5,3},{6,30},{7,1},{8,16},{9,15},... | collective-permute-start | bytes 147464 | tf_op jit(solution)/shard_map/ppermute | solution.py:51
  107.2 1.6 %shard_map.85 = (f32[192,3072]{1,0:T(8,128)}, f32[192,3072]{1,0:T(8,128)}, f32[8,128]{1,0:T(8,128)S(1)}) custom-call(f32[96,128]{1,0:T(8,128)S(1)} %add_add_fusion.2.sent, f32[192,192]{1,0:T(8,128)S(1)} %get-tuple-element.49.inverse, f32[64,3072]{1,0:T(8,128)S(1)} %bitcast.39, ...), custom_call_target="tpu_custom_call", output_to_operand_aliasing={{0}: (8, {}), {1}: (9, {})} | custom-call | flops 2000000000 | bytes 3000000 | tf_op jit(solution)/shard_map/pallas_call | solution.py:363
  109.3 1.7 %shard_map.86 = (f32[192,3072]{1,0:T(8,128)}, f32[192,3072]{1,0:T(8,128)}, f32[8,128]{1,0:T(8,128)S(1)}) custom-call(f32[96,128]{1,0:T(8,128)S(1)} %add_add_fusion.1.sent, f32[192,192]{1,0:T(8,128)S(1)} %get-tuple-element.49.inverse, f32[64,3072]{1,0:T(8,128)S(1)} %bitcast.40, ...), custom_call_target="tpu_custom_call", output_to_operand_aliasing={{0}: (8, {}), {1}: (9, {})} | custom-call | flops 2000000000 | bytes 3000000 | tf_op jit(solution)/shard_map/pallas_call | solution.py:363
  111.9 3.8 %collective-permute-start.18 = (f32[96,128]{1,0:T(8,128)S(1)}, f32[96,128]{1,0:T(8,128)S(1)}, u32[]{:S(2)}, u32[]{:S(2)}) collective-permute-start(f32[96,128]{1,0:T(8,128)S(1)} %add_add_fusion), channel_id=1, source_target_pairs={{0,6},{1,97},{2,4},{3,99},{4,2},{5,101},{6,0},{7,103},{8,14},{9,10... | collective-permute-start | bytes 147464 | tf_op jit(solution)/shard_map/ppermute | solution.py:51
  117.2 7.1 %collective-permute-start.19 = (f32[96,128]{1,0:T(8,128)S(1)}, f32[96,128]{1,0:T(8,128)S(1)}, u32[]{:S(2)}, u32[]{:S(2)}) collective-permute-start(f32[96,128]{1,0:T(8,128)S(1)} %add.158.mine), channel_id=1, source_target_pairs={{0,1},{1,0},{2,3},{3,2},{4,5},{5,4},{6,7},{7,6},{8,9},{9,8},{10,11... | collective-permute-start | bytes 147464 | tf_op jit(solution)/shard_map/ppermute | solution.py:57
  (63 shorter events, 22.4 us)
Async XLA Ops:
  0.6 7.1 %copy-start = (f32[3072,64]{0,1:T(8,128)S(1)}, f32[3072,64]{0,1:T(8,128)}, u32[]{:S(2)}) copy-start(f32[3072,64]{0,1:T(8,128)} %param.9) | copy-start | bytes 2359300
  0.6 7.1 %copy-start.1 = (f32[3072,64]{0,1:T(8,128)S(1)}, f32[3072,64]{0,1:T(8,128)}, u32[]{:S(2)}) copy-start(f32[3072,64]{0,1:T(8,128)} %param.8) | copy-start | bytes 2359300
  3.0 14.6 %collective-permute-start.1 = (bf16[128,3200]{1,0:T(8,128)(2,1)S(1)}, bf16[128,3200]{1,0:T(8,128)(2,1)S(1)}, u32[]{:S(2)}, u32[]{:S(2)}) collective-permute-start(bf16[128,3200]{1,0:T(8,128)(2,1)S(1)} %fusion.1.own), channel_id=1, source_target_pairs={{1,2},{3,4},{5,6},{7,8},{9,10},{11,12},{13,14},{15,16},{17,18},{19... | collective-permute-start | bytes 2457608 | tf_op jit(solution)/shard_map/ppermute | solution.py:62
  7.6 10.0 %collective-permute-start = (bf16[128,3200]{1,0:T(8,128)(2,1)S(1)}, bf16[128,3200]{1,0:T(8,128)(2,1)}, u32[]{:S(2)}, u32[]{:S(2)}) collective-permute-start(bf16[128,3200]{1,0:T(8,128)(2,1)S(1)} %fusion.1.own), channel_id=1, source_target_pairs={{0,1},{1,0},{2,3},{3,2},{4,5},{5,4},{6,7},{7,6},{8,9},{9,8},{10,11... | collective-permute-start | bytes 2457608 | tf_op jit(solution)/shard_map/ppermute | solution.py:63
  7.7 10.7 %copy-start.2 = (s32[16,18]{1,0:T(8,128)S(1)}, s32[16,18]{1,0:T(8,128)}, u32[]{:S(2)}) copy-start(s32[16,18]{1,0:T(8,128)} %nb.3) | copy-start | bytes 3460
  30.2 1.3 %collective-permute-start.2 = (f32[96,128]{1,0:T(8,128)S(1)}, f32[96,128]{1,0:T(8,128)S(1)}, u32[]{:S(2)}, u32[]{:S(2)}) collective-permute-start(f32[96,128]{1,0:T(8,128)S(1)} %get-tuple-element.36), channel_id=1, source_target_pairs={{0,1},{1,0},{2,3},{3,2},{4,5},{5,4},{6,7},{7,6},{8,9},{9,8},{10,11... | collective-permute-start | bytes 147464 | tf_op jit(solution)/shard_map/ppermute | solution.py:48
  31.6 5.0 %collective-permute-start.3 = (f32[96,128]{1,0:T(8,128)S(1)}, f32[96,128]{1,0:T(8,128)S(1)}, u32[]{:S(2)}, u32[]{:S(2)}) collective-permute-start(f32[96,128]{1,0:T(8,128)S(1)} %add.127.sent), channel_id=1, source_target_pairs={{0,32},{1,9},{2,34},{3,11},{4,36},{5,13},{6,38},{7,15},{8,40},{9,1... | collective-permute-start | bytes 147464 | tf_op jit(solution)/shard_map/ppermute | solution.py:51
  36.6 4.3 %collective-permute-start.4 = (f32[96,128]{1,0:T(8,128)S(1)}, f32[96,128]{1,0:T(8,128)S(1)}, u32[]{:S(2)}, u32[]{:S(2)}) collective-permute-start(f32[96,128]{1,0:T(8,128)S(1)} %add_add_fusion.5), channel_id=1, source_target_pairs={{0,96},{1,25},{2,98},{3,27},{4,100},{5,29},{6,102},{7,31},{8,104},... | collective-permute-start | bytes 147464 | tf_op jit(solution)/shard_map/ppermute | solution.py:51
  40.9 3.0 %collective-permute-start.5 = (f32[96,128]{1,0:T(8,128)S(1)}, f32[96,128]{1,0:T(8,128)S(1)}, u32[]{:S(2)}, u32[]{:S(2)}) collective-permute-start(f32[96,128]{1,0:T(8,128)S(1)} %add.132), channel_id=1, source_target_pairs={{0,8},{1,3},{2,10},{3,1},{4,12},{5,7},{6,14},{7,5},{8,0},{9,11},{1... | collective-permute-start | bytes 147464 | tf_op jit(solution)/shard_map/ppermute | solution.py:51
  43.9 6.1 %collective-permute-start.6 = (f32[96,128]{1,0:T(8,128)S(1)}, f32[96,128]{1,0:T(8,128)S(1)}, u32[]{:S(2)}, u32[]{:S(2)}) collective-permute-start(f32[96,128]{1,0:T(8,128)S(1)} %add.133), channel_id=1, source_target_pairs={{0,24},{1,7},{2,26},{3,5},{4,28},{5,3},{6,30},{7,1},{8,16},{9,15},... | collective-permute-start | bytes 147464 | tf_op jit(solution)/shard_map/ppermute | solution.py:51
  50.0 3.6 %collective-permute-start.7 = (f32[96,128]{1,0:T(8,128)S(1)}, f32[96,128]{1,0:T(8,128)S(1)}, u32[]{:S(2)}, u32[]{:S(2)}) collective-permute-start(f32[96,128]{1,0:T(8,128)S(1)} %add.134), channel_id=1, source_target_pairs={{0,2},{1,33},{2,0},{3,35},{4,6},{5,37},{6,4},{7,39},{8,10},{9,41},... | collective-permute-start | bytes 147464 | tf_op jit(solution)/shard_map/ppermute | solution.py:51
  53.6 5.1 %collective-permute-start.8 = (f32[96,128]{1,0:T(8,128)S(1)}, f32[96,128]{1,0:T(8,128)S(1)}, u32[]{:S(2)}, u32[]{:S(2)}) collective-permute-start(f32[96,128]{1,0:T(8,128)S(1)} %add.135), channel_id=1, source_target_pairs={{0,6},{1,97},{2,4},{3,99},{4,2},{5,101},{6,0},{7,103},{8,14},{9,10... | collective-permute-start | bytes 147464 | tf_op jit(solution)/shard_map/ppermute | solution.py:51
  58.8 8.0 %collective-permute-start.9 = (f32[96,128]{1,0:T(8,128)S(1)}, f32[96,128]{1,0:T(8,128)S(1)}, u32[]{:S(2)}, u32[]{:S(2)}) collective-permute-start(f32[96,128]{1,0:T(8,128)S(1)} %add.136.mine), channel_id=1, source_target_pairs={{0,1},{1,0},{2,3},{3,2},{4,5},{5,4},{6,7},{7,6},{8,9},{9,8},{10,11... | collective-permute-start | bytes 147464 | tf_op jit(solution)/shard_map/ppermute | solution.py:57
  69.8 9.1 %collective-permute-start.11 = (bf16[64,3072]{1,0:T(8,128)(2,1)S(1)}, bf16[64,3072]{1,0:T(8,128)(2,1)S(1)}, u32[]{:S(2)}, u32[]{:S(2)}) collective-permute-start(bf16[64,3072]{1,0:T(8,128)(2,1)S(1)} %get-tuple-element.40.own), channel_id=1, source_target_pairs={{1,2},{3,4},{5,6},{7,8},{9,10},{11,12},{13,14},{15,16},{17,18},{19... | collective-permute-start | bytes 1179656 | tf_op jit(solution)/shard_map/ppermute | solution.py:62
  71.7 7.2 %collective-permute-start.10 = (bf16[64,3072]{1,0:T(8,128)(2,1)S(1)}, bf16[64,3072]{1,0:T(8,128)(2,1)S(1)}, u32[]{:S(2)}, u32[]{:S(2)}) collective-permute-start(bf16[64,3072]{1,0:T(8,128)(2,1)S(1)} %get-tuple-element.40.own), channel_id=1, source_target_pairs={{0,1},{1,0},{2,3},{3,2},{4,5},{5,4},{6,7},{7,6},{8,9},{9,8},{10,11... | collective-permute-start | bytes 1179656 | tf_op jit(solution)/shard_map/ppermute | solution.py:63
  89.6 1.3 %collective-permute-start.12 = (f32[96,128]{1,0:T(8,128)S(1)}, f32[96,128]{1,0:T(8,128)S(1)}, u32[]{:S(2)}, u32[]{:S(2)}) collective-permute-start(f32[96,128]{1,0:T(8,128)S(1)} %get-tuple-element.47), channel_id=1, source_target_pairs={{0,1},{1,0},{2,3},{3,2},{4,5},{5,4},{6,7},{7,6},{8,9},{9,8},{10,11... | collective-permute-start | bytes 147464 | tf_op jit(solution)/shard_map/ppermute | solution.py:48
  91.0 3.0 %collective-permute-start.13 = (f32[96,128]{1,0:T(8,128)S(1)}, f32[96,128]{1,0:T(8,128)S(1)}, u32[]{:S(2)}, u32[]{:S(2)}) collective-permute-start(f32[96,128]{1,0:T(8,128)S(1)} %add.137.sent), channel_id=1, source_target_pairs={{0,32},{1,9},{2,34},{3,11},{4,36},{5,13},{6,38},{7,15},{8,40},{9,1... | collective-permute-start | bytes 147464 | tf_op jit(solution)/shard_map/ppermute | solution.py:51
  94.0 4.6 %collective-permute-start.14 = (f32[96,128]{1,0:T(8,128)S(1)}, f32[96,128]{1,0:T(8,128)S(1)}, u32[]{:S(2)}, u32[]{:S(2)}) collective-permute-start(f32[96,128]{1,0:T(8,128)S(1)} %add_add_fusion.4.sent), channel_id=1, source_target_pairs={{0,96},{1,25},{2,98},{3,27},{4,100},{5,29},{6,102},{7,31},{8,104},... | collective-permute-start | bytes 147464 | tf_op jit(solution)/shard_map/ppermute | solution.py:51
  98.6 3.0 %collective-permute-start.15 = (f32[96,128]{1,0:T(8,128)S(1)}, f32[96,128]{1,0:T(8,128)S(1)}, u32[]{:S(2)}, u32[]{:S(2)}) collective-permute-start(f32[96,128]{1,0:T(8,128)S(1)} %add_add_fusion.3.sent), channel_id=1, source_target_pairs={{0,8},{1,3},{2,10},{3,1},{4,12},{5,7},{6,14},{7,5},{8,0},{9,11},{1... | collective-permute-start | bytes 147464 | tf_op jit(solution)/shard_map/ppermute | solution.py:51
  101.7 7.2 %collective-permute-start.16 = (f32[96,128]{1,0:T(8,128)S(1)}, f32[96,128]{1,0:T(8,128)S(1)}, u32[]{:S(2)}, u32[]{:S(2)}) collective-permute-start(f32[96,128]{1,0:T(8,128)S(1)} %add_add_fusion.2.sent), channel_id=1, source_target_pairs={{0,24},{1,7},{2,26},{3,5},{4,28},{5,3},{6,30},{7,1},{8,16},{9,15},... | collective-permute-start | bytes 147464 | tf_op jit(solution)/shard_map/ppermute | solution.py:51
  108.8 3.0 %collective-permute-start.17 = (f32[96,128]{1,0:T(8,128)S(1)}, f32[96,128]{1,0:T(8,128)S(1)}, u32[]{:S(2)}, u32[]{:S(2)}) collective-permute-start(f32[96,128]{1,0:T(8,128)S(1)} %add_add_fusion.1.sent), channel_id=1, source_target_pairs={{0,2},{1,33},{2,0},{3,35},{4,6},{5,37},{6,4},{7,39},{8,10},{9,41},... | collective-permute-start | bytes 147464 | tf_op jit(solution)/shard_map/ppermute | solution.py:51
  111.9 5.3 %collective-permute-start.18 = (f32[96,128]{1,0:T(8,128)S(1)}, f32[96,128]{1,0:T(8,128)S(1)}, u32[]{:S(2)}, u32[]{:S(2)}) collective-permute-start(f32[96,128]{1,0:T(8,128)S(1)} %add_add_fusion), channel_id=1, source_target_pairs={{0,6},{1,97},{2,4},{3,99},{4,2},{5,101},{6,0},{7,103},{8,14},{9,10... | collective-permute-start | bytes 147464 | tf_op jit(solution)/shard_map/ppermute | solution.py:51
  117.2 8.0 %collective-permute-start.19 = (f32[96,128]{1,0:T(8,128)S(1)}, f32[96,128]{1,0:T(8,128)S(1)}, u32[]{:S(2)}, u32[]{:S(2)}) collective-permute-start(f32[96,128]{1,0:T(8,128)S(1)} %add.158.mine), channel_id=1, source_target_pairs={{0,1},{1,0},{2,3},{3,2},{4,5},{5,4},{6,7},{7,6},{8,9},{9,8},{10,11... | collective-permute-start | bytes 147464 | tf_op jit(solution)/shard_map/ppermute | solution.py:57

commit v4 on v3

--- a/solution.py
+++ b/solution.py
@@ -10,6 +10,7 @@
 AXES = ("dom", "sub")
 HIGHEST = lax.Precision.HIGHEST
 MIB = 2**20
+PER = 8
 NT = (((1,), (1,)), ((), ()))
 TN = (((0,), (0,)), ((), ()))
 NN = (((1,), (0,)), ((), ()))
@@ -64,72 +65,105 @@
     return twin, other
 
 
-def load_kernel(odd, tiles_hbm, x, p, tiles, gram, sems):
-    parts = sems.shape[0]
-    size = tiles.shape[0] // parts
-    copies = [
-        pltpu.make_async_copy(tiles_hbm.at[pl.ds(i * size, size)], tiles.at[pl.ds(i * size, size)], sems.at[i])
-        for i in range(parts)
-    ]
-    for copy in copies:
-        copy.start()
+def load_kernel(odd, tiles_hbm, x, p, packed, gram, arrived, sems):
+    count, degree, _, size = tiles_hbm.shape
+    depth = arrived.shape[0]
+
+    def copy(group, slot):
+        return pltpu.make_async_copy(tiles_hbm.at[group], arrived.at[slot], sems.at[slot])
+
+    for slot in range(depth):
+        copy(slot, slot).start()
     both = jnp.concatenate([x[...], p[...]], 0)
     gram[...] = dot32(both, both, NT)
-    for copy in copies:
-        copy.wait()
+
+    def step(group, carry):
+        slot = lax.rem(group, depth)
+        copy(group, slot).wait()
+        for pair in range(degree // 2):
+            packed[group, :, 2 * pair * size : 2 * (pair + 1) * size] = jnp.concatenate(
+                [arrived[slot, 2 * pair], arrived[slot, 2 * pair + 1]], 1
+            )
+
+        @pl.when(group + depth < count)
+        def _():
+            copy(group + depth, slot).start()
+
+        return carry
+
+    lax.fori_loop(0, count, step, 0)
 
 
 def load(odd, tiles, x, p):
     cols = x.shape[0]
+    count, degree, size = tiles.shape[:3]
+    depth = 4
     vmem = pl.BlockSpec(memory_space=pltpu.VMEM)
     return pl.pallas_call(
         load_kernel,
         out_shape=(
-            pltpu.VMEM(tiles.shape, tiles.dtype),
+            pltpu.VMEM((count, size, degree * size), tiles.dtype),
             jax.ShapeDtypeStruct((2 * cols, 2 * cols), jnp.float32),
         ),
         in_specs=[vmem, pl.BlockSpec(memory_space=pl.ANY), vmem, vmem],
         out_specs=(vmem, vmem),
-        scratch_shapes=[pltpu.SemaphoreType.DMA((8,))],
-        compiler_params=pltpu.CompilerParams(vmem_limit_bytes=16 * MIB),
+        scratch_shapes=[
+            pltpu.VMEM((depth,) + tiles.shape[1:], tiles.dtype),
+            pltpu.SemaphoreType.DMA((depth,)),
+        ],
+        compiler_params=pltpu.CompilerParams(vmem_limit_bytes=20 * MIB),
         cost_estimate=pl.CostEstimate(flops=200000000, bytes_accessed=30000000, transcendentals=0),
     )(odd, tiles, x, p)
 
 
-def fill_slabs(slabs, blocks, count, size):
+def fill_slabs(low, high, blocks, count, size):
+    cols, lanes = low.shape[1:]
+    gap = jnp.zeros((cols, lanes - size), low.dtype)
     for place, block in enumerate(blocks):
         for pair in range(count // 2):
             both = block[:, pair * 2 * size : (pair + 1) * 2 * size]
-            slabs[place * count + 2 * pair] = both[:, :size]
-            slabs[place * count + 2 * pair + 1] = both[:, size:]
-
-
-def multiply_tiles(nb, table, tiles, slabs, image, count, per):
-    size = tiles.shape[2]
-
-    def step(pair, carry):
+            for half, slab in enumerate((both[:, :size], both[:, size:])):
+                low[place * count + 2 * pair + half] = jnp.concatenate([slab, gap], 1)
+                high[place * count + 2 * pair + half] = jnp.concatenate([gap, slab], 1)
+
+
+def multiply_tiles(nb, table, tiles, low, high, ends, image):
+    count, size, depth = tiles.shape
+    per, lanes = ends.shape[0], low.shape[2]
+    rest = 2 * size - lanes
+
+    def step(turn, carry):
         wide = []
-        for half in range(per):
-            group = pair * per + half
-            total = None
-            for k in range(tiles.shape[1]):
-                slab = slabs[table[nb[group, k]]]
-                part = lax.dot_general(tiles[group, k], slab, NT, preferred_element_type=jnp.float32)
-                total = part if total is None else total + part
+        for part in range(per):
+            group = turn * per + part
+            for pair in range(depth // (2 * size)):
+                first = low[table[nb[group, 2 * pair]]]
+                second = high[table[nb[group, 2 * pair + 1]]]
+                at = 2 * pair * size
+                ends[part, :, at : at + rest] = first[:, :rest]
+                ends[part, :, at + rest : at + lanes] = first[:, rest:] + second[:, : lanes - rest]
+                ends[part, :, at + lanes : at + 2 * size] = second[:, lanes - rest :]
+            total = lax.dot_general(tiles[group], ends[part], NT, preferred_element_type=jnp.float32)
             wide.append(total.T)
         width = per * size
-        image[:, pl.ds(pl.multiple_of(pair * width, width), width)] = jnp.concatenate(wide, 1)
+        image[:, pl.ds(pl.multiple_of(turn * width, width), width)] = jnp.concatenate(wide, 1)
         return carry
 
     lax.fori_loop(0, count // per, step, 0)
 
 
+def slab_scratch(count, cols, size, depth, per):
+    lanes = -(-size // 128) * 128
+    slabs = pltpu.VMEM((3 * count, cols, lanes), jnp.bfloat16)
+    return [slabs, slabs, pltpu.VMEM((per, cols, depth), jnp.bfloat16)]
+
+
 def first_kernel(
-    per, nb, table, odd, tiles, own, twin, other, x, p, gram, x_image, p_image, mine, theirs, slabs, images
+    nb, table, odd, tiles, own, twin, other, x, p, gram, x_image, p_image, mine, theirs, low, high, ends, images
 ):
-    count, size, cols = tiles.shape[0], tiles.shape[2], x.shape[0]
-    fill_slabs(slabs, (own, twin, other), count, size)
-    multiply_tiles(nb, table, tiles, slabs, images, count, per)
+    count, size, cols = tiles.shape[0], tiles.shape[1], x.shape[0]
+    fill_slabs(low, high, (own, twin, other), count, size)
+    multiply_tiles(nb, table, tiles, low, high, ends, images)
     image = images[:cols]
     x_image[...] = image
     p_image[...] = images[cols:]
@@ -144,11 +178,11 @@
 
 
 def first_images(nb, table, odd, tiles, own, twin, other, x, p, gram):
-    count, size, cols = tiles.shape[0], tiles.shape[2], x.shape[0]
+    (count, size, depth), cols = tiles.shape, x.shape[0]
     vmem = pl.BlockSpec(memory_space=pltpu.VMEM)
     smem = pl.BlockSpec(memory_space=pltpu.SMEM)
     return pl.pallas_call(
-        functools.partial(first_kernel, 4),
+        first_kernel,
         out_shape=(
             jax.ShapeDtypeStruct(x.shape, jnp.float32),
             jax.ShapeDtypeStruct(x.shape, jnp.float32),
@@ -158,10 +192,10 @@
         in_specs=[smem, smem] + [vmem] * 8,
         out_specs=(vmem,) * 4,
         scratch_shapes=[
-            pltpu.VMEM((3 * count, 2 * cols, size), jnp.bfloat16),
+            *slab_scratch(count, 2 * cols, size, depth, PER),
             pltpu.VMEM((2 * cols, x.shape[1]), jnp.float32),
         ],
-        compiler_params=pltpu.CompilerParams(vmem_limit_bytes=16 * MIB),
+        compiler_params=pltpu.CompilerParams(vmem_limit_bytes=20 * MIB),
         cost_estimate=pl.CostEstimate(flops=10000000000, bytes_accessed=4000000, transcendentals=0),
     )(nb, table, odd, pltpu.with_memory_space_constraint(tiles, pltpu.VMEM), own, twin, other, x, p, gram)
 
@@ -184,11 +218,11 @@
 
 
 def second_kernel(
-    per, nb, table, odd, tiles, own, twin, other, x, r, p, middle, quotient, parts, r_image, mine, theirs, slabs
+    nb, table, odd, tiles, own, twin, other, x, r, p, middle, quotient, parts, r_image, mine, theirs, low, high, ends
 ):
-    count, size = tiles.shape[0], tiles.shape[2]
-    fill_slabs(slabs, (own, twin, other), count, size)
-    multiply_tiles(nb, table, tiles, slabs, r_image, count, per)
+    count, size = tiles.shape[0], tiles.shape[1]
+    fill_slabs(low, high, (own, twin, other), count, size)
+    multiply_tiles(nb, table, tiles, low, high, ends, r_image)
     cross = dot16(jnp.concatenate([x[...], r[...], p[...]], 0), r_image[...], NT)
     c = x.shape[0]
     xp, ip, pp = middle[:c], middle[c : 2 * c], middle[2 * c :]
@@ -197,11 +231,11 @@
 
 
 def second_images(nb, table, odd, tiles, own, twin, other, x, r, p, middle, quotient, parts):
-    count, size, cols = tiles.shape[0], tiles.shape[2], x.shape[0]
+    (count, size, depth), cols = tiles.shape, x.shape[0]
     vmem = pl.BlockSpec(memory_space=pltpu.VMEM)
     smem = pl.BlockSpec(memory_space=pltpu.SMEM)
     return pl.pallas_call(
-        functools.partial(second_kernel, 4),
+        second_kernel,
         out_shape=(
             jax.ShapeDtypeStruct(x.shape, jnp.float32),
             half_of(cols),
@@ -209,8 +243,8 @@
         ),
         in_specs=[smem, smem] + [vmem] * 10 + [pl.BlockSpec(memory_space=pl.ANY)],
         out_specs=(vmem,) * 3,
-        scratch_shapes=[pltpu.VMEM((3 * count, cols, size), jnp.bfloat16)],
-        compiler_params=pltpu.CompilerParams(vmem_limit_bytes=16 * MIB),
+        scratch_shapes=slab_scratch(count, cols, size, depth, PER),
+        compiler_params=pltpu.CompilerParams(vmem_limit_bytes=20 * MIB),
         cost_estimate=pl.CostEstimate(flops=10000000000, bytes_accessed=4000000, transcendentals=0),
     )(nb, table, odd, pltpu.with_memory_space_constraint(tiles, pltpu.VMEM), own, twin, other, x, r, p, middle, quotient, parts)
 
@@ -387,7 +421,7 @@
         out_shape=jax.ShapeDtypeStruct(inverse.shape, jnp.float32),
         in_specs=[vmem] * 6,
         out_specs=vmem,
-        compiler_params=pltpu.CompilerParams(vmem_limit_bytes=16 * MIB),
+        compiler_params=pltpu.CompilerParams(vmem_limit_bytes=20 * MIB),
     )(odd, inverse, packed, parts, mine, theirs)
 
 

time: 127 us -> 123 us (0.969)
  Pallas kernels: 49.2 us -> 46.5 us
    pallas_call x3, Pallas kernels: 32 us -> 29.2 us  [the longest x1 10.8 us: load(): pl.pallas_call(load_kernel, out_shape=(pltpu.VMEM((count, size, degree *...]
  transfers between devices with their start and end apart: 20 -> 20, of which waited for: 16 -> 15; matrix products, arithmetic and copies ran while one was open for 0% -> 0% of each run, Pallas kernels for 18% -> 19%
where the time goes in v4:
time: 123 us
  starting transfers between devices  51 us (41%)
  Pallas kernels  46.5 us (38%)
  waiting for transfers between devices  20.9 us (17%)
  other arithmetic  3.24 us (3%)
    ppermute x12, starting transfers between devices, all_sum(): lax.ppermute(mine, AXES, [(i, i ^ (odd if i % 2 else even)) for i in rang...  29.3 us
    ppermute x2, starting transfers between devices, all_sum(): return (mine, lax.ppermute(mine, 'sub', twin))  14.2 us
    ppermute x12, waiting for transfers between devices, all_sum(): lax.ppermute(mine, AXES, [(i, i ^ (odd if i % 2 else even)) for i in rang...  13.1 us
    pallas_call x1, Pallas kernels, load(): pl.pallas_call(load_kernel, out_shape=(pltpu.VMEM((count, size, degree *...  10.8 us
    pallas_call x1, Pallas kernels, first_images(): pl.pallas_call(first_kernel, out_shape=(jax.ShapeDtypeStruct(x.shape, jnp...  9.87 us
    pallas_call x1, Pallas kernels, second_images(): pl.pallas_call(second_kernel, out_shape=(jax.ShapeDtypeStruct(x.shape, jn...  8.53 us
    ppermute x2, starting transfers between devices, neighbour_blocks(): other = lax.ppermute(block, AXES, pairs + [(j, i) for i, j in pairs])  6.7 us
    pallas_call x4, Pallas kernels, bases(): pl.pallas_call(functools.partial(basis_kernel, len(done)), grid=(steps,),...  6.64 us
  transfers between devices with their start and end apart: 20, of which 15 were waited for; matrix products, arithmetic and copies ran while one was open for 0% of the time, Pallas kernels for 19%

profile of v4, /device:TPU:1, one launch (start us, length us, event | category | flops | bytes accessed | tf_op | source)
XLA Modules:
  0.0 122.5 jit_solution(2068141807008985972)
XLA Ops:
  3.0 4.6 %collective-permute-start.1 = (bf16[128,3200]{1,0:T(8,128)(2,1)S(1)}, bf16[128,3200]{1,0:T(8,128)(2,1)S(1)}, u32[]{:S(2)}, u32[]{:S(2)}) collective-permute-start(bf16[128,3200]{1,0:T(8,128)(2,1)S(1)} %fusion.1.own), channel_id=1, source_target_pairs={{1,2},{3,4},{5,6},{7,8},{9,10},{11,12},{13,14},{15,16},{17,18},{19... | collective-permute-start | bytes 2457608 | tf_op jit(solution)/shard_map/ppermute | solution.py:63
  7.7 10.8 %shard_map.76 = (bf16[16,192,3456]{2,1,0:T(8,128)(2,1)S(1)}, f32[128,128]{1,0:T(8,128)S(1)}) custom-call(f32[8,128]{1,0:T(8,128)S(1)} %broadcast_in_dim.7.odd, bf16[16,18,192,192]{3,2,1,0:T(8,128)(2,1)} %tiles_hbm.1, f32[64,3072]{1,0:T(8,128)S(1)} %bitcast.32, f32[64,3072]{1,0:T(8,128)S(1)} %bitcast.24), custom_call_target="tpu_custom_call" | custom-call | flops 200000000 | bytes 30000000 | tf_op jit(solution)/shard_map/pallas_call | solution.py:102
  19.4 9.9 %shard_map.77 = (f32[64,3072]{1,0:T(8,128)S(1)}, f32[64,3072]{1,0:T(8,128)S(1)}, f32[96,128]{1,0:T(8,128)S(1)}, f32[96,128]{1,0:T(8,128)S(1)}) custom-call(s32[16,18]{1,0:T(8,128)S(1)} %copy-done.2, s32[48]{0:T(128)S(1)} %pad_add_fusion.table, f32[8,128]{1,0:T(8,128)S(1)} %broadcast_in_dim.7.odd, bf16[16,192,3456]{2,1,0:T(8,128)(2,1)S(1)} %get-tuple-element.33.tiles, ...), custom_call_target="tpu_custom_call" | custom-call | flops 10000000000 | bytes 4000000 | tf_op jit(solution)/shard_map/pallas_call | solution.py:184
  30.7 2.5 %collective-permute-start.3 = (f32[96,128]{1,0:T(8,128)S(1)}, f32[96,128]{1,0:T(8,128)S(1)}, u32[]{:S(2)}, u32[]{:S(2)}) collective-permute-start(f32[96,128]{1,0:T(8,128)S(1)} %add.127.sent), channel_id=1, source_target_pairs={{0,32},{1,9},{2,34},{3,11},{4,36},{5,13},{6,38},{7,15},{8,40},{9,1... | collective-permute-start | bytes 147464 | tf_op jit(solution)/shard_map/ppermute | solution.py:52
  34.6 3.0 %collective-permute-start.4 = (f32[96,128]{1,0:T(8,128)S(1)}, f32[96,128]{1,0:T(8,128)S(1)}, u32[]{:S(2)}, u32[]{:S(2)}) collective-permute-start(f32[96,128]{1,0:T(8,128)S(1)} %add_add_fusion.5), channel_id=1, source_target_pairs={{0,96},{1,25},{2,98},{3,27},{4,100},{5,29},{6,102},{7,31},{8,104},... | collective-permute-start | bytes 147464 | tf_op jit(solution)/shard_map/ppermute | solution.py:52
  39.3 2.9 %collective-permute-done.5 = f32[96,128]{1,0:T(8,128)S(1)} collective-permute-done((f32[96,128]{1,0:T(8,128)S(1)}, f32[96,128]{1,0:T(8,128)S(1)}, u32[]{:S(2)}, u32[]{:S(2)}) %collective-permute-start.5) | collective-permute-done | bytes 49184 | tf_op jit(solution)/shard_map/ppermute | solution.py:52
  42.2 4.5 %collective-permute-start.6 = (f32[96,128]{1,0:T(8,128)S(1)}, f32[96,128]{1,0:T(8,128)S(1)}, u32[]{:S(2)}, u32[]{:S(2)}) collective-permute-start(f32[96,128]{1,0:T(8,128)S(1)} %add.133), channel_id=1, source_target_pairs={{0,24},{1,7},{2,26},{3,5},{4,28},{5,3},{6,30},{7,1},{8,16},{9,15},... | collective-permute-start | bytes 147464 | tf_op jit(solution)/shard_map/ppermute | solution.py:52
  48.1 2.1 %collective-permute-start.7 = (f32[96,128]{1,0:T(8,128)S(1)}, f32[96,128]{1,0:T(8,128)S(1)}, u32[]{:S(2)}, u32[]{:S(2)}) collective-permute-start(f32[96,128]{1,0:T(8,128)S(1)} %add.134), channel_id=1, source_target_pairs={{0,2},{1,33},{2,0},{3,35},{4,6},{5,37},{6,4},{7,39},{8,10},{9,41},... | collective-permute-start | bytes 147464 | tf_op jit(solution)/shard_map/ppermute | solution.py:52
  51.7 3.7 %collective-permute-start.8 = (f32[96,128]{1,0:T(8,128)S(1)}, f32[96,128]{1,0:T(8,128)S(1)}, u32[]{:S(2)}, u32[]{:S(2)}) collective-permute-start(f32[96,128]{1,0:T(8,128)S(1)} %add.135), channel_id=1, source_target_pairs={{0,6},{1,97},{2,4},{3,99},{4,2},{5,101},{6,0},{7,103},{8,14},{9,10... | collective-permute-start | bytes 147464 | tf_op jit(solution)/shard_map/ppermute | solution.py:52
  56.8 7.1 %collective-permute-start.9 = (f32[96,128]{1,0:T(8,128)S(1)}, f32[96,128]{1,0:T(8,128)S(1)}, u32[]{:S(2)}, u32[]{:S(2)}) collective-permute-start(f32[96,128]{1,0:T(8,128)S(1)} %add.136.mine), channel_id=1, source_target_pairs={{0,1},{1,0},{2,3},{3,2},{4,5},{5,4},{6,7},{7,6},{8,9},{9,8},{10,11... | collective-permute-start | bytes 147464 | tf_op jit(solution)/shard_map/ppermute | solution.py:58
  64.8 3.0 %shard_map.79 = (f32[192,128]{1,0:T(8,128)S(1)}, f32[64,64]{1,0:T(8,128)S(1)}, f32[64,64]{1,0:T(8,128)S(1)}, f32[64,3072]{1,0:T(8,128)S(1)}, bf16[64,3072]{1,0:T(8,128)(2,1)S(1)}) custom-call(f32[8,128]{1,0:T(8,128)S(1)} %broadcast_in_dim.7.odd, f32[96,128]{1,0:T(8,128)S(1)} %add.136.mine, f32[96,128]{1,0:T(8,128)S(1)} %collective-permute-done.9.theirs, ...), custom_call_target="tpu_custom_call" | custom-call | flops 3000000000 | bytes 3000000 | tf_op jit(solution)/shard_map/pallas_call | solution.py:300
  67.8 2.1 %collective-permute-start.11 = (bf16[64,3072]{1,0:T(8,128)(2,1)S(1)}, bf16[64,3072]{1,0:T(8,128)(2,1)S(1)}, u32[]{:S(2)}, u32[]{:S(2)}) collective-permute-start(bf16[64,3072]{1,0:T(8,128)(2,1)S(1)} %get-tuple-element.40.own), channel_id=1, source_target_pairs={{1,2},{3,4},{5,6},{7,8},{9,10},{11,12},{13,14},{15,16},{17,18},{19... | collective-permute-start | bytes 1179656 | tf_op jit(solution)/shard_map/ppermute | solution.py:63
  70.0 3.2 %shard_map.80.parts = f32[7,64,64]{2,1,0:T(8,128)S(1)} custom-call(f32[192,128]{1,0:T(8,128)S(1)} %get-tuple-element.44.packed, f32[64,64]{1,0:T(8,128)S(1)} %get-tuple-element.43.quotient, f32[64,64]{1,0:T(8,128)S(1)} %get-tuple-element.45.x_inverse), custom_call_target="tpu_custom_call" | custom-call | flops 2000000000 | bytes 3000000 | tf_op jit(solution)/shard_map/pallas_call | solution.py:338
  73.2 3.9 %collective-permute-done.11.other = bf16[64,3072]{1,0:T(8,128)(2,1)S(1)} collective-permute-done((bf16[64,3072]{1,0:T(8,128)(2,1)S(1)}, bf16[64,3072]{1,0:T(8,128)(2,1)S(1)}, u32[]{:S(2)}, u32[]{:S(2)}) %collective-permute-start.11) | collective-permute-done | bytes 393248 | tf_op jit(solution)/shard_map/ppermute | solution.py:63
  77.1 8.5 %shard_map.81 = (f32[64,3072]{1,0:T(8,128)S(1)}, f32[96,128]{1,0:T(8,128)S(1)}, f32[96,128]{1,0:T(8,128)S(1)}) custom-call(s32[16,18]{1,0:T(8,128)S(1)} %copy-done.2, s32[48]{0:T(128)S(1)} %pad_add_fusion.table, f32[8,128]{1,0:T(8,128)S(1)} %broadcast_in_dim.7.odd, bf16[16,192,3456]{2,1,0:T(8,128)(2,1)S(1)} %get-tuple-element.33.tiles, ...), custom_call_target="tpu_custom_call" | custom-call | flops 10000000000 | bytes 4000000 | tf_op jit(solution)/shard_map/pallas_call | solution.py:237
  87.6 2.0 %shard_map.82 = (f32[192,192]{1,0:T(8,128)S(1)}, f32[8,128]{1,0:T(8,128)S(1)}) custom-call(f32[96,128]{1,0:T(8,128)S(1)} %add.137.sent, f32[7,64,64]{2,1,0:T(8,128)S(1)} %shard_map.80.parts), custom_call_target="tpu_custom_call" | custom-call | flops 2000000000 | bytes 3000000 | tf_op jit(solution)/shard_map/pallas_call | solution.py:370
  90.0 3.0 %collective-permute-start.14 = (f32[96,128]{1,0:T(8,128)S(1)}, f32[96,128]{1,0:T(8,128)S(1)}, u32[]{:S(2)}, u32[]{:S(2)}) collective-permute-start(f32[96,128]{1,0:T(8,128)S(1)} %add_add_fusion.4.sent), channel_id=1, source_target_pairs={{0,96},{1,25},{2,98},{3,27},{4,100},{5,29},{6,102},{7,31},{8,104},... | collective-permute-start | bytes 147464 | tf_op jit(solution)/shard_map/ppermute | solution.py:52
  93.0 1.7 %shard_map.83 = (f32[192,3072]{1,0:T(8,128)}, f32[192,3072]{1,0:T(8,128)}, f32[8,128]{1,0:T(8,128)S(1)}) custom-call(f32[96,128]{1,0:T(8,128)S(1)} %add_add_fusion.4.sent, f32[192,192]{1,0:T(8,128)S(1)} %get-tuple-element.49.inverse, f32[64,3072]{1,0:T(8,128)S(1)} %bitcast.37, f32[64,3072]{1,0:T(8,128)S(1)} %get-tuple-element.41.r, f32[64,3072]{1,0:T(8,128)S(1)} %bitcast.28, ...), custom_call_target="tpu_custom_call" | custom-call | flops 2000000000 | bytes 3000000 | tf_op jit(solution)/shard_map/pallas_call | solution.py:397
  94.7 1.7 %shard_map.84 = (f32[192,3072]{1,0:T(8,128)}, f32[192,3072]{1,0:T(8,128)}, f32[8,128]{1,0:T(8,128)S(1)}) custom-call(f32[96,128]{1,0:T(8,128)S(1)} %add_add_fusion.3.sent, f32[192,192]{1,0:T(8,128)S(1)} %get-tuple-element.49.inverse, f32[64,3072]{1,0:T(8,128)S(1)} %bitcast.38, ...), custom_call_target="tpu_custom_call", output_to_operand_aliasing={{0}: (8, {}), {1}: (9, {})} | custom-call | flops 2000000000 | bytes 3000000 | tf_op jit(solution)/shard_map/pallas_call | solution.py:397
  97.7 5.5 %collective-permute-start.16 = (f32[96,128]{1,0:T(8,128)S(1)}, f32[96,128]{1,0:T(8,128)S(1)}, u32[]{:S(2)}, u32[]{:S(2)}) collective-permute-start(f32[96,128]{1,0:T(8,128)S(1)} %add_add_fusion.2.sent), channel_id=1, source_target_pairs={{0,24},{1,7},{2,26},{3,5},{4,28},{5,3},{6,30},{7,1},{8,16},{9,15},... | collective-permute-start | bytes 147464 | tf_op jit(solution)/shard_map/ppermute | solution.py:52
  103.2 1.7 %shard_map.85 = (f32[192,3072]{1,0:T(8,128)}, f32[192,3072]{1,0:T(8,128)}, f32[8,128]{1,0:T(8,128)S(1)}) custom-call(f32[96,128]{1,0:T(8,128)S(1)} %add_add_fusion.2.sent, f32[192,192]{1,0:T(8,128)S(1)} %get-tuple-element.49.inverse, f32[64,3072]{1,0:T(8,128)S(1)} %bitcast.39, ...), custom_call_target="tpu_custom_call", output_to_operand_aliasing={{0}: (8, {}), {1}: (9, {})} | custom-call | flops 2000000000 | bytes 3000000 | tf_op jit(solution)/shard_map/pallas_call | solution.py:397
  105.3 1.7 %shard_map.86 = (f32[192,3072]{1,0:T(8,128)}, f32[192,3072]{1,0:T(8,128)}, f32[8,128]{1,0:T(8,128)S(1)}) custom-call(f32[96,128]{1,0:T(8,128)S(1)} %add_add_fusion.1.sent, f32[192,192]{1,0:T(8,128)S(1)} %get-tuple-element.49.inverse, f32[64,3072]{1,0:T(8,128)S(1)} %bitcast.40, ...), custom_call_target="tpu_custom_call", output_to_operand_aliasing={{0}: (8, {}), {1}: (9, {})} | custom-call | flops 2000000000 | bytes 3000000 | tf_op jit(solution)/shard_map/pallas_call | solution.py:397
  107.9 3.8 %collective-permute-start.18 = (f32[96,128]{1,0:T(8,128)S(1)}, f32[96,128]{1,0:T(8,128)S(1)}, u32[]{:S(2)}, u32[]{:S(2)}) collective-permute-start(f32[96,128]{1,0:T(8,128)S(1)} %add_add_fusion), channel_id=1, source_target_pairs={{0,6},{1,97},{2,4},{3,99},{4,2},{5,101},{6,0},{7,103},{8,14},{9,10... | collective-permute-start | bytes 147464 | tf_op jit(solution)/shard_map/ppermute | solution.py:52
  113.2 7.1 %collective-permute-start.19 = (f32[96,128]{1,0:T(8,128)S(1)}, f32[96,128]{1,0:T(8,128)S(1)}, u32[]{:S(2)}, u32[]{:S(2)}) collective-permute-start(f32[96,128]{1,0:T(8,128)S(1)} %add.158.mine), channel_id=1, source_target_pairs={{0,1},{1,0},{2,3},{3,2},{4,5},{5,4},{6,7},{7,6},{8,9},{9,8},{10,11... | collective-permute-start | bytes 147464 | tf_op jit(solution)/shard_map/ppermute | solution.py:58
  (63 shorter events, 21.9 us)
Async XLA Ops:
  0.6 7.1 %copy-start = (f32[3072,64]{0,1:T(8,128)S(1)}, f32[3072,64]{0,1:T(8,128)}, u32[]{:S(2)}) copy-start(f32[3072,64]{0,1:T(8,128)} %param.9) | copy-start | bytes 2359300
  0.6 7.1 %copy-start.1 = (f32[3072,64]{0,1:T(8,128)S(1)}, f32[3072,64]{0,1:T(8,128)}, u32[]{:S(2)}) copy-start(f32[3072,64]{0,1:T(8,128)} %param.8) | copy-start | bytes 2359300
  3.0 15.6 %collective-permute-start.1 = (bf16[128,3200]{1,0:T(8,128)(2,1)S(1)}, bf16[128,3200]{1,0:T(8,128)(2,1)S(1)}, u32[]{:S(2)}, u32[]{:S(2)}) collective-permute-start(bf16[128,3200]{1,0:T(8,128)(2,1)S(1)} %fusion.1.own), channel_id=1, source_target_pairs={{1,2},{3,4},{5,6},{7,8},{9,10},{11,12},{13,14},{15,16},{17,18},{19... | collective-permute-start | bytes 2457608 | tf_op jit(solution)/shard_map/ppermute | solution.py:63
  7.6 11.0 %collective-permute-start = (bf16[128,3200]{1,0:T(8,128)(2,1)S(1)}, bf16[128,3200]{1,0:T(8,128)(2,1)}, u32[]{:S(2)}, u32[]{:S(2)}) collective-permute-start(bf16[128,3200]{1,0:T(8,128)(2,1)S(1)} %fusion.1.own), channel_id=1, source_target_pairs={{0,1},{1,0},{2,3},{3,2},{4,5},{5,4},{6,7},{7,6},{8,9},{9,8},{10,11... | collective-permute-start | bytes 2457608 | tf_op jit(solution)/shard_map/ppermute | solution.py:64
  7.7 11.7 %copy-start.2 = (s32[16,18]{1,0:T(8,128)S(1)}, s32[16,18]{1,0:T(8,128)}, u32[]{:S(2)}) copy-start(s32[16,18]{1,0:T(8,128)} %nb.3) | copy-start | bytes 3460
  29.3 1.4 %collective-permute-start.2 = (f32[96,128]{1,0:T(8,128)S(1)}, f32[96,128]{1,0:T(8,128)S(1)}, u32[]{:S(2)}, u32[]{:S(2)}) collective-permute-start(f32[96,128]{1,0:T(8,128)S(1)} %get-tuple-element.36), channel_id=1, source_target_pairs={{0,1},{1,0},{2,3},{3,2},{4,5},{5,4},{6,7},{7,6},{8,9},{9,8},{10,11... | collective-permute-start | bytes 147464 | tf_op jit(solution)/shard_map/ppermute | solution.py:49
  30.7 3.9 %collective-permute-start.3 = (f32[96,128]{1,0:T(8,128)S(1)}, f32[96,128]{1,0:T(8,128)S(1)}, u32[]{:S(2)}, u32[]{:S(2)}) collective-permute-start(f32[96,128]{1,0:T(8,128)S(1)} %add.127.sent), channel_id=1, source_target_pairs={{0,32},{1,9},{2,34},{3,11},{4,36},{5,13},{6,38},{7,15},{8,40},{9,1... | collective-permute-start | bytes 147464 | tf_op jit(solution)/shard_map/ppermute | solution.py:52
  34.6 4.5 %collective-permute-start.4 = (f32[96,128]{1,0:T(8,128)S(1)}, f32[96,128]{1,0:T(8,128)S(1)}, u32[]{:S(2)}, u32[]{:S(2)}) collective-permute-start(f32[96,128]{1,0:T(8,128)S(1)} %add_add_fusion.5), channel_id=1, source_target_pairs={{0,96},{1,25},{2,98},{3,27},{4,100},{5,29},{6,102},{7,31},{8,104},... | collective-permute-start | bytes 147464 | tf_op jit(solution)/shard_map/ppermute | solution.py:52
  39.1 3.0 %collective-permute-start.5 = (f32[96,128]{1,0:T(8,128)S(1)}, f32[96,128]{1,0:T(8,128)S(1)}, u32[]{:S(2)}, u32[]{:S(2)}) collective-permute-start(f32[96,128]{1,0:T(8,128)S(1)} %add.132), channel_id=1, source_target_pairs={{0,8},{1,3},{2,10},{3,1},{4,12},{5,7},{6,14},{7,5},{8,0},{9,11},{1... | collective-permute-start | bytes 147464 | tf_op jit(solution)/shard_map/ppermute | solution.py:52
  42.2 5.9 %collective-permute-start.6 = (f32[96,128]{1,0:T(8,128)S(1)}, f32[96,128]{1,0:T(8,128)S(1)}, u32[]{:S(2)}, u32[]{:S(2)}) collective-permute-start(f32[96,128]{1,0:T(8,128)S(1)} %add.133), channel_id=1, source_target_pairs={{0,24},{1,7},{2,26},{3,5},{4,28},{5,3},{6,30},{7,1},{8,16},{9,15},... | collective-permute-start | bytes 147464 | tf_op jit(solution)/shard_map/ppermute | solution.py:52
  48.1 3.6 %collective-permute-start.7 = (f32[96,128]{1,0:T(8,128)S(1)}, f32[96,128]{1,0:T(8,128)S(1)}, u32[]{:S(2)}, u32[]{:S(2)}) collective-permute-start(f32[96,128]{1,0:T(8,128)S(1)} %add.134), channel_id=1, source_target_pairs={{0,2},{1,33},{2,0},{3,35},{4,6},{5,37},{6,4},{7,39},{8,10},{9,41},... | collective-permute-start | bytes 147464 | tf_op jit(solution)/shard_map/ppermute | solution.py:52
  51.7 5.1 %collective-permute-start.8 = (f32[96,128]{1,0:T(8,128)S(1)}, f32[96,128]{1,0:T(8,128)S(1)}, u32[]{:S(2)}, u32[]{:S(2)}) collective-permute-start(f32[96,128]{1,0:T(8,128)S(1)} %add.135), channel_id=1, source_target_pairs={{0,6},{1,97},{2,4},{3,99},{4,2},{5,101},{6,0},{7,103},{8,14},{9,10... | collective-permute-start | bytes 147464 | tf_op jit(solution)/shard_map/ppermute | solution.py:52
  56.8 8.0 %collective-permute-start.9 = (f32[96,128]{1,0:T(8,128)S(1)}, f32[96,128]{1,0:T(8,128)S(1)}, u32[]{:S(2)}, u32[]{:S(2)}) collective-permute-start(f32[96,128]{1,0:T(8,128)S(1)} %add.136.mine), channel_id=1, source_target_pairs={{0,1},{1,0},{2,3},{3,2},{4,5},{5,4},{6,7},{7,6},{8,9},{9,8},{10,11... | collective-permute-start | bytes 147464 | tf_op jit(solution)/shard_map/ppermute | solution.py:58
  67.8 9.3 %collective-permute-start.11 = (bf16[64,3072]{1,0:T(8,128)(2,1)S(1)}, bf16[64,3072]{1,0:T(8,128)(2,1)S(1)}, u32[]{:S(2)}, u32[]{:S(2)}) collective-permute-start(bf16[64,3072]{1,0:T(8,128)(2,1)S(1)} %get-tuple-element.40.own), channel_id=1, source_target_pairs={{1,2},{3,4},{5,6},{7,8},{9,10},{11,12},{13,14},{15,16},{17,18},{19... | collective-permute-start | bytes 1179656 | tf_op jit(solution)/shard_map/ppermute | solution.py:63
  69.9 7.2 %collective-permute-start.10 = (bf16[64,3072]{1,0:T(8,128)(2,1)S(1)}, bf16[64,3072]{1,0:T(8,128)(2,1)S(1)}, u32[]{:S(2)}, u32[]{:S(2)}) collective-permute-start(bf16[64,3072]{1,0:T(8,128)(2,1)S(1)} %get-tuple-element.40.own), channel_id=1, source_target_pairs={{0,1},{1,0},{2,3},{3,2},{4,5},{5,4},{6,7},{7,6},{8,9},{9,8},{10,11... | collective-permute-start | bytes 1179656 | tf_op jit(solution)/shard_map/ppermute | solution.py:64
  85.6 1.3 %collective-permute-start.12 = (f32[96,128]{1,0:T(8,128)S(1)}, f32[96,128]{1,0:T(8,128)S(1)}, u32[]{:S(2)}, u32[]{:S(2)}) collective-permute-start(f32[96,128]{1,0:T(8,128)S(1)} %get-tuple-element.47), channel_id=1, source_target_pairs={{0,1},{1,0},{2,3},{3,2},{4,5},{5,4},{6,7},{7,6},{8,9},{9,8},{10,11... | collective-permute-start | bytes 147464 | tf_op jit(solution)/shard_map/ppermute | solution.py:49
  87.0 3.0 %collective-permute-start.13 = (f32[96,128]{1,0:T(8,128)S(1)}, f32[96,128]{1,0:T(8,128)S(1)}, u32[]{:S(2)}, u32[]{:S(2)}) collective-permute-start(f32[96,128]{1,0:T(8,128)S(1)} %add.137.sent), channel_id=1, source_target_pairs={{0,32},{1,9},{2,34},{3,11},{4,36},{5,13},{6,38},{7,15},{8,40},{9,1... | collective-permute-start | bytes 147464 | tf_op jit(solution)/shard_map/ppermute | solution.py:52
  90.0 4.6 %collective-permute-start.14 = (f32[96,128]{1,0:T(8,128)S(1)}, f32[96,128]{1,0:T(8,128)S(1)}, u32[]{:S(2)}, u32[]{:S(2)}) collective-permute-start(f32[96,128]{1,0:T(8,128)S(1)} %add_add_fusion.4.sent), channel_id=1, source_target_pairs={{0,96},{1,25},{2,98},{3,27},{4,100},{5,29},{6,102},{7,31},{8,104},... | collective-permute-start | bytes 147464 | tf_op jit(solution)/shard_map/ppermute | solution.py:52
  94.6 3.0 %collective-permute-start.15 = (f32[96,128]{1,0:T(8,128)S(1)}, f32[96,128]{1,0:T(8,128)S(1)}, u32[]{:S(2)}, u32[]{:S(2)}) collective-permute-start(f32[96,128]{1,0:T(8,128)S(1)} %add_add_fusion.3.sent), channel_id=1, source_target_pairs={{0,8},{1,3},{2,10},{3,1},{4,12},{5,7},{6,14},{7,5},{8,0},{9,11},{1... | collective-permute-start | bytes 147464 | tf_op jit(solution)/shard_map/ppermute | solution.py:52
  97.7 7.2 %collective-permute-start.16 = (f32[96,128]{1,0:T(8,128)S(1)}, f32[96,128]{1,0:T(8,128)S(1)}, u32[]{:S(2)}, u32[]{:S(2)}) collective-permute-start(f32[96,128]{1,0:T(8,128)S(1)} %add_add_fusion.2.sent), channel_id=1, source_target_pairs={{0,24},{1,7},{2,26},{3,5},{4,28},{5,3},{6,30},{7,1},{8,16},{9,15},... | collective-permute-start | bytes 147464 | tf_op jit(solution)/shard_map/ppermute | solution.py:52
  104.9 3.0 %collective-permute-start.17 = (f32[96,128]{1,0:T(8,128)S(1)}, f32[96,128]{1,0:T(8,128)S(1)}, u32[]{:S(2)}, u32[]{:S(2)}) collective-permute-start(f32[96,128]{1,0:T(8,128)S(1)} %add_add_fusion.1.sent), channel_id=1, source_target_pairs={{0,2},{1,33},{2,0},{3,35},{4,6},{5,37},{6,4},{7,39},{8,10},{9,41},... | collective-permute-start | bytes 147464 | tf_op jit(solution)/shard_map/ppermute | solution.py:52
  107.9 5.3 %collective-permute-start.18 = (f32[96,128]{1,0:T(8,128)S(1)}, f32[96,128]{1,0:T(8,128)S(1)}, u32[]{:S(2)}, u32[]{:S(2)}) collective-permute-start(f32[96,128]{1,0:T(8,128)S(1)} %add_add_fusion), channel_id=1, source_target_pairs={{0,6},{1,97},{2,4},{3,99},{4,2},{5,101},{6,0},{7,103},{8,14},{9,10... | collective-permute-start | bytes 147464 | tf_op jit(solution)/shard_map/ppermute | solution.py:52
  113.2 8.0 %collective-permute-start.19 = (f32[96,128]{1,0:T(8,128)S(1)}, f32[96,128]{1,0:T(8,128)S(1)}, u32[]{:S(2)}, u32[]{:S(2)}) collective-permute-start(f32[96,128]{1,0:T(8,128)S(1)} %add.158.mine), channel_id=1, source_target_pairs={{0,1},{1,0},{2,3},{3,2},{4,5},{5,4},{6,7},{7,6},{8,9},{9,8},{10,11... | collective-permute-start | bytes 147464 | tf_op jit(solution)/shard_map/ppermute | solution.py:58

commit v5 on v4

--- a/solution.py
+++ b/solution.py
@@ -48,7 +48,7 @@
     twin = [(i, i ^ 1) for i in range(sub)]
     mine = mine + lax.ppermute(theirs, "sub", twin)
     y, x, z = (2, 6), (sub, 3 * sub), (4 * sub, 12 * sub)
-    for at, (even, odd) in enumerate(zip(z + x + y, x + y + z)):
+    for at, (even, odd) in enumerate(zip(z + x + y, x + z + y)):
         got = lax.ppermute(mine, AXES, [(i, i ^ (odd if i % 2 else even)) for i in range(sub * dom)])
         if at < len(work) and work[at] is not None:
             zeros = work[at](mine)
@@ -75,7 +75,7 @@
     for slot in range(depth):
         copy(slot, slot).start()
     both = jnp.concatenate([x[...], p[...]], 0)
-    gram[...] = dot32(both, both, NT)
+    gram[...] = dot16(both, both, NT)
 
     def step(group, carry):
         slot = lax.rem(group, depth)

time: 123 us -> 123 us (level)
    ppermute x12, waiting for transfers between devices: 13.1 us -> 14.5 us  [all_sum(): lax.ppermute(mine, AXES, [(i, i ^ (odd if i % 2 else even)) for i in rang...]
  transfers between devices with their start and end apart: 20 -> 20, of which waited for: 15 -> 14; matrix products, arithmetic and copies ran while one was open for 0% -> 0% of each run, Pallas kernels for 19% -> 19%
where the time goes in v5:
time: 123 us; the launch traced here: 122 us
  starting transfers between devices  50.6 us (41%)
  Pallas kernels  45.6 us (37%)
  waiting for transfers between devices  22 us (18%)
  other arithmetic  3.24 us (3%)
    ppermute x12, starting transfers between devices, all_sum(): lax.ppermute(mine, AXES, [(i, i ^ (odd if i % 2 else even)) for i in rang...  29.1 us
    ppermute x12, waiting for transfers between devices, all_sum(): lax.ppermute(mine, AXES, [(i, i ^ (odd if i % 2 else even)) for i in rang...  14.5 us
    ppermute x2, starting transfers between devices, all_sum(): return (mine, lax.ppermute(mine, 'sub', twin))  14 us
    pallas_call x1, Pallas kernels, load(): pl.pallas_call(load_kernel, out_shape=(pltpu.VMEM((count, size, degree *...  9.92 us
    pallas_call x1, Pallas kernels, first_images(): pl.pallas_call(first_kernel, out_shape=(jax.ShapeDtypeStruct(x.shape, jnp...  9.87 us
    pallas_call x1, Pallas kernels, second_images(): pl.pallas_call(second_kernel, out_shape=(jax.ShapeDtypeStruct(x.shape, jn...  8.53 us
    pallas_call x4, Pallas kernels, bases(): pl.pallas_call(functools.partial(basis_kernel, len(done)), grid=(steps,),...  6.63 us
    ppermute x2, starting transfers between devices, neighbour_blocks(): other = lax.ppermute(block, AXES, pairs + [(j, i) for i, j in pairs])  6.52 us
  transfers between devices with their start and end apart: 20, of which 14 were waited for; matrix products, arithmetic and copies ran while one was open for 0% of the time, Pallas kernels for 19%

profile of v5, /device:TPU:1, one launch (start us, length us, event | category | flops | bytes accessed | tf_op | source)
XLA Modules:
  0.0 122.3 jit_solution(17005776974307859737)
XLA Ops:
  3.0 4.6 %collective-permute-start.1 = (bf16[128,3200]{1,0:T(8,128)(2,1)S(1)}, bf16[128,3200]{1,0:T(8,128)(2,1)S(1)}, u32[]{:S(2)}, u32[]{:S(2)}) collective-permute-start(bf16[128,3200]{1,0:T(8,128)(2,1)S(1)} %fusion.1.own), channel_id=1, source_target_pairs={{1,2},{3,4},{5,6},{7,8},{9,10},{11,12},{13,14},{15,16},{17,18},{19... | collective-permute-start | bytes 2457608 | tf_op jit(solution)/shard_map/ppermute | solution.py:63
  7.7 9.9 %shard_map.76 = (bf16[16,192,3456]{2,1,0:T(8,128)(2,1)S(1)}, f32[128,128]{1,0:T(8,128)S(1)}) custom-call(f32[8,128]{1,0:T(8,128)S(1)} %broadcast_in_dim.7.odd, bf16[16,18,192,192]{3,2,1,0:T(8,128)(2,1)} %tiles_hbm.1, f32[64,3072]{1,0:T(8,128)S(1)} %bitcast.32, f32[64,3072]{1,0:T(8,128)S(1)} %bitcast.24), custom_call_target="tpu_custom_call" | custom-call | flops 200000000 | bytes 30000000 | tf_op jit(solution)/shard_map/pallas_call | solution.py:102
  18.5 9.9 %shard_map.77 = (f32[64,3072]{1,0:T(8,128)S(1)}, f32[64,3072]{1,0:T(8,128)S(1)}, f32[96,128]{1,0:T(8,128)S(1)}, f32[96,128]{1,0:T(8,128)S(1)}) custom-call(s32[16,18]{1,0:T(8,128)S(1)} %copy-done.2, s32[48]{0:T(128)S(1)} %pad_add_fusion.table, f32[8,128]{1,0:T(8,128)S(1)} %broadcast_in_dim.7.odd, bf16[16,192,3456]{2,1,0:T(8,128)(2,1)S(1)} %get-tuple-element.33.tiles, ...), custom_call_target="tpu_custom_call" | custom-call | flops 10000000000 | bytes 4000000 | tf_op jit(solution)/shard_map/pallas_call | solution.py:184
  29.8 3.3 %collective-permute-start.3 = (f32[96,128]{1,0:T(8,128)S(1)}, f32[96,128]{1,0:T(8,128)S(1)}, u32[]{:S(2)}, u32[]{:S(2)}) collective-permute-start(f32[96,128]{1,0:T(8,128)S(1)} %add.127.sent), channel_id=1, source_target_pairs={{0,32},{1,9},{2,34},{3,11},{4,36},{5,13},{6,38},{7,15},{8,40},{9,1... | collective-permute-start | bytes 147464 | tf_op jit(solution)/shard_map/ppermute | solution.py:52
  34.6 2.8 %collective-permute-start.4 = (f32[96,128]{1,0:T(8,128)S(1)}, f32[96,128]{1,0:T(8,128)S(1)}, u32[]{:S(2)}, u32[]{:S(2)}) collective-permute-start(f32[96,128]{1,0:T(8,128)S(1)} %add_add_fusion.5), channel_id=1, source_target_pairs={{0,96},{1,25},{2,98},{3,27},{4,100},{5,29},{6,102},{7,31},{8,104},... | collective-permute-start | bytes 147464 | tf_op jit(solution)/shard_map/ppermute | solution.py:52
  38.9 4.0 %collective-permute-start.5 = (f32[96,128]{1,0:T(8,128)S(1)}, f32[96,128]{1,0:T(8,128)S(1)}, u32[]{:S(2)}, u32[]{:S(2)}) collective-permute-start(f32[96,128]{1,0:T(8,128)S(1)} %add.132), channel_id=1, source_target_pairs={{0,8},{1,33},{2,10},{3,35},{4,12},{5,37},{6,14},{7,39},{8,0},{9,41... | collective-permute-start | bytes 147464 | tf_op jit(solution)/shard_map/ppermute | solution.py:52
  44.4 3.7 %collective-permute-start.6 = (f32[96,128]{1,0:T(8,128)S(1)}, f32[96,128]{1,0:T(8,128)S(1)}, u32[]{:S(2)}, u32[]{:S(2)}) collective-permute-start(f32[96,128]{1,0:T(8,128)S(1)} %add.133), channel_id=1, source_target_pairs={{0,24},{1,97},{2,26},{3,99},{4,28},{5,101},{6,30},{7,103},{8,16},{... | collective-permute-start | bytes 147464 | tf_op jit(solution)/shard_map/ppermute | solution.py:52
  49.7 2.9 %collective-permute-done.7 = f32[96,128]{1,0:T(8,128)S(1)} collective-permute-done((f32[96,128]{1,0:T(8,128)S(1)}, f32[96,128]{1,0:T(8,128)S(1)}, u32[]{:S(2)}, u32[]{:S(2)}) %collective-permute-start.7) | collective-permute-done | bytes 49184 | tf_op jit(solution)/shard_map/ppermute | solution.py:52
  52.6 1.7 %collective-permute-start.8 = (f32[96,128]{1,0:T(8,128)S(1)}, f32[96,128]{1,0:T(8,128)S(1)}, u32[]{:S(2)}, u32[]{:S(2)}) collective-permute-start(f32[96,128]{1,0:T(8,128)S(1)} %add.135), channel_id=1, source_target_pairs={{0,6},{1,7},{2,4},{3,5},{4,2},{5,3},{6,0},{7,1},{8,14},{9,15},{10,... | collective-permute-start | bytes 147464 | tf_op jit(solution)/shard_map/ppermute | solution.py:52
  54.3 2.5 %collective-permute-done.8 = f32[96,128]{1,0:T(8,128)S(1)} collective-permute-done((f32[96,128]{1,0:T(8,128)S(1)}, f32[96,128]{1,0:T(8,128)S(1)}, u32[]{:S(2)}, u32[]{:S(2)}) %collective-permute-start.8) | collective-permute-done | bytes 49184 | tf_op jit(solution)/shard_map/ppermute | solution.py:52
  56.8 7.1 %collective-permute-start.9 = (f32[96,128]{1,0:T(8,128)S(1)}, f32[96,128]{1,0:T(8,128)S(1)}, u32[]{:S(2)}, u32[]{:S(2)}) collective-permute-start(f32[96,128]{1,0:T(8,128)S(1)} %add.136.mine), channel_id=1, source_target_pairs={{0,1},{1,0},{2,3},{3,2},{4,5},{5,4},{6,7},{7,6},{8,9},{9,8},{10,11... | collective-permute-start | bytes 147464 | tf_op jit(solution)/shard_map/ppermute | solution.py:58
  64.8 3.0 %shard_map.79 = (f32[192,128]{1,0:T(8,128)S(1)}, f32[64,64]{1,0:T(8,128)S(1)}, f32[64,64]{1,0:T(8,128)S(1)}, f32[64,3072]{1,0:T(8,128)S(1)}, bf16[64,3072]{1,0:T(8,128)(2,1)S(1)}) custom-call(f32[8,128]{1,0:T(8,128)S(1)} %broadcast_in_dim.7.odd, f32[96,128]{1,0:T(8,128)S(1)} %add.136.mine, f32[96,128]{1,0:T(8,128)S(1)} %collective-permute-done.9.theirs, ...), custom_call_target="tpu_custom_call" | custom-call | flops 3000000000 | bytes 3000000 | tf_op jit(solution)/shard_map/pallas_call | solution.py:300
  67.8 1.9 %collective-permute-start.11 = (bf16[64,3072]{1,0:T(8,128)(2,1)S(1)}, bf16[64,3072]{1,0:T(8,128)(2,1)S(1)}, u32[]{:S(2)}, u32[]{:S(2)}) collective-permute-start(bf16[64,3072]{1,0:T(8,128)(2,1)S(1)} %get-tuple-element.40.own), channel_id=1, source_target_pairs={{1,2},{3,4},{5,6},{7,8},{9,10},{11,12},{13,14},{15,16},{17,18},{19... | collective-permute-start | bytes 1179656 | tf_op jit(solution)/shard_map/ppermute | solution.py:63
  70.0 3.2 %shard_map.80.parts = f32[7,64,64]{2,1,0:T(8,128)S(1)} custom-call(f32[192,128]{1,0:T(8,128)S(1)} %get-tuple-element.44.packed, f32[64,64]{1,0:T(8,128)S(1)} %get-tuple-element.43.quotient, f32[64,64]{1,0:T(8,128)S(1)} %get-tuple-element.45.x_inverse), custom_call_target="tpu_custom_call" | custom-call | flops 2000000000 | bytes 3000000 | tf_op jit(solution)/shard_map/pallas_call | solution.py:338
  73.2 3.7 %collective-permute-done.11.other = bf16[64,3072]{1,0:T(8,128)(2,1)S(1)} collective-permute-done((bf16[64,3072]{1,0:T(8,128)(2,1)S(1)}, bf16[64,3072]{1,0:T(8,128)(2,1)S(1)}, u32[]{:S(2)}, u32[]{:S(2)}) %collective-permute-start.11) | collective-permute-done | bytes 393248 | tf_op jit(solution)/shard_map/ppermute | solution.py:63
  76.9 8.5 %shard_map.81 = (f32[64,3072]{1,0:T(8,128)S(1)}, f32[96,128]{1,0:T(8,128)S(1)}, f32[96,128]{1,0:T(8,128)S(1)}) custom-call(s32[16,18]{1,0:T(8,128)S(1)} %copy-done.2, s32[48]{0:T(128)S(1)} %pad_add_fusion.table, f32[8,128]{1,0:T(8,128)S(1)} %broadcast_in_dim.7.odd, bf16[16,192,3456]{2,1,0:T(8,128)(2,1)S(1)} %get-tuple-element.33.tiles, ...), custom_call_target="tpu_custom_call" | custom-call | flops 10000000000 | bytes 4000000 | tf_op jit(solution)/shard_map/pallas_call | solution.py:237
  87.4 2.0 %shard_map.82 = (f32[192,192]{1,0:T(8,128)S(1)}, f32[8,128]{1,0:T(8,128)S(1)}) custom-call(f32[96,128]{1,0:T(8,128)S(1)} %add.137.sent, f32[7,64,64]{2,1,0:T(8,128)S(1)} %shard_map.80.parts), custom_call_target="tpu_custom_call" | custom-call | flops 2000000000 | bytes 3000000 | tf_op jit(solution)/shard_map/pallas_call | solution.py:370
  89.8 3.0 %collective-permute-start.14 = (f32[96,128]{1,0:T(8,128)S(1)}, f32[96,128]{1,0:T(8,128)S(1)}, u32[]{:S(2)}, u32[]{:S(2)}) collective-permute-start(f32[96,128]{1,0:T(8,128)S(1)} %add_add_fusion.4.sent), channel_id=1, source_target_pairs={{0,96},{1,25},{2,98},{3,27},{4,100},{5,29},{6,102},{7,31},{8,104},... | collective-permute-start | bytes 147464 | tf_op jit(solution)/shard_map/ppermute | solution.py:52
  94.5 3.4 %collective-permute-start.15 = (f32[96,128]{1,0:T(8,128)S(1)}, f32[96,128]{1,0:T(8,128)S(1)}, u32[]{:S(2)}, u32[]{:S(2)}) collective-permute-start(f32[96,128]{1,0:T(8,128)S(1)} %add_add_fusion.3.sent), channel_id=1, source_target_pairs={{0,8},{1,33},{2,10},{3,35},{4,12},{5,37},{6,14},{7,39},{8,0},{9,41... | collective-permute-start | bytes 147464 | tf_op jit(solution)/shard_map/ppermute | solution.py:52
  97.9 1.7 %shard_map.84 = (f32[192,3072]{1,0:T(8,128)}, f32[192,3072]{1,0:T(8,128)}, f32[8,128]{1,0:T(8,128)S(1)}) custom-call(f32[96,128]{1,0:T(8,128)S(1)} %add_add_fusion.3.sent, f32[192,192]{1,0:T(8,128)S(1)} %get-tuple-element.49.inverse, f32[64,3072]{1,0:T(8,128)S(1)} %bitcast.38, ...), custom_call_target="tpu_custom_call", output_to_operand_aliasing={{0}: (8, {}), {1}: (9, {})} | custom-call | flops 2000000000 | bytes 3000000 | tf_op jit(solution)/shard_map/pallas_call | solution.py:397
  99.6 4.7 %collective-permute-start.16 = (f32[96,128]{1,0:T(8,128)S(1)}, f32[96,128]{1,0:T(8,128)S(1)}, u32[]{:S(2)}, u32[]{:S(2)}) collective-permute-start(f32[96,128]{1,0:T(8,128)S(1)} %add_add_fusion.2.sent), channel_id=1, source_target_pairs={{0,24},{1,97},{2,26},{3,99},{4,28},{5,101},{6,30},{7,103},{8,16},{... | collective-permute-start | bytes 147464 | tf_op jit(solution)/shard_map/ppermute | solution.py:52
  106.0 1.7 %shard_map.86 = (f32[192,3072]{1,0:T(8,128)}, f32[192,3072]{1,0:T(8,128)}, f32[8,128]{1,0:T(8,128)S(1)}) custom-call(f32[96,128]{1,0:T(8,128)S(1)} %add_add_fusion.1.sent, f32[192,192]{1,0:T(8,128)S(1)} %get-tuple-element.49.inverse, f32[64,3072]{1,0:T(8,128)S(1)} %bitcast.40, ...), custom_call_target="tpu_custom_call", output_to_operand_aliasing={{0}: (8, {}), {1}: (9, {})} | custom-call | flops 2000000000 | bytes 3000000 | tf_op jit(solution)/shard_map/pallas_call | solution.py:397
  110.6 2.6 %collective-permute-done.18 = f32[96,128]{1,0:T(8,128)S(1)} collective-permute-done((f32[96,128]{1,0:T(8,128)S(1)}, f32[96,128]{1,0:T(8,128)S(1)}, u32[]{:S(2)}, u32[]{:S(2)}) %collective-permute-start.18) | collective-permute-done | bytes 49184 | tf_op jit(solution)/shard_map/ppermute | solution.py:52
  113.2 6.9 %collective-permute-start.19 = (f32[96,128]{1,0:T(8,128)S(1)}, f32[96,128]{1,0:T(8,128)S(1)}, u32[]{:S(2)}, u32[]{:S(2)}) collective-permute-start(f32[96,128]{1,0:T(8,128)S(1)} %add.158.mine), channel_id=1, source_target_pairs={{0,1},{1,0},{2,3},{3,2},{4,5},{5,4},{6,7},{7,6},{8,9},{9,8},{10,11... | collective-permute-start | bytes 147464 | tf_op jit(solution)/shard_map/ppermute | solution.py:58
  (63 shorter events, 22.7 us)
Async XLA Ops:
  0.6 7.1 %copy-start = (f32[3072,64]{0,1:T(8,128)S(1)}, f32[3072,64]{0,1:T(8,128)}, u32[]{:S(2)}) copy-start(f32[3072,64]{0,1:T(8,128)} %param.9) | copy-start | bytes 2359300
  0.6 7.1 %copy-start.1 = (f32[3072,64]{0,1:T(8,128)S(1)}, f32[3072,64]{0,1:T(8,128)}, u32[]{:S(2)}) copy-start(f32[3072,64]{0,1:T(8,128)} %param.8) | copy-start | bytes 2359300
  3.0 14.7 %collective-permute-start.1 = (bf16[128,3200]{1,0:T(8,128)(2,1)S(1)}, bf16[128,3200]{1,0:T(8,128)(2,1)S(1)}, u32[]{:S(2)}, u32[]{:S(2)}) collective-permute-start(bf16[128,3200]{1,0:T(8,128)(2,1)S(1)} %fusion.1.own), channel_id=1, source_target_pairs={{1,2},{3,4},{5,6},{7,8},{9,10},{11,12},{13,14},{15,16},{17,18},{19... | collective-permute-start | bytes 2457608 | tf_op jit(solution)/shard_map/ppermute | solution.py:63
  7.6 10.1 %collective-permute-start = (bf16[128,3200]{1,0:T(8,128)(2,1)S(1)}, bf16[128,3200]{1,0:T(8,128)(2,1)}, u32[]{:S(2)}, u32[]{:S(2)}) collective-permute-start(bf16[128,3200]{1,0:T(8,128)(2,1)S(1)} %fusion.1.own), channel_id=1, source_target_pairs={{0,1},{1,0},{2,3},{3,2},{4,5},{5,4},{6,7},{7,6},{8,9},{9,8},{10,11... | collective-permute-start | bytes 2457608 | tf_op jit(solution)/shard_map/ppermute | solution.py:64
  7.7 10.8 %copy-start.2 = (s32[16,18]{1,0:T(8,128)S(1)}, s32[16,18]{1,0:T(8,128)}, u32[]{:S(2)}) copy-start(s32[16,18]{1,0:T(8,128)} %nb.3) | copy-start | bytes 3460
  28.4 1.4 %collective-permute-start.2 = (f32[96,128]{1,0:T(8,128)S(1)}, f32[96,128]{1,0:T(8,128)S(1)}, u32[]{:S(2)}, u32[]{:S(2)}) collective-permute-start(f32[96,128]{1,0:T(8,128)S(1)} %get-tuple-element.36), channel_id=1, source_target_pairs={{0,1},{1,0},{2,3},{3,2},{4,5},{5,4},{6,7},{7,6},{8,9},{9,8},{10,11... | collective-permute-start | bytes 147464 | tf_op jit(solution)/shard_map/ppermute | solution.py:49
  29.8 4.8 %collective-permute-start.3 = (f32[96,128]{1,0:T(8,128)S(1)}, f32[96,128]{1,0:T(8,128)S(1)}, u32[]{:S(2)}, u32[]{:S(2)}) collective-permute-start(f32[96,128]{1,0:T(8,128)S(1)} %add.127.sent), channel_id=1, source_target_pairs={{0,32},{1,9},{2,34},{3,11},{4,36},{5,13},{6,38},{7,15},{8,40},{9,1... | collective-permute-start | bytes 147464 | tf_op jit(solution)/shard_map/ppermute | solution.py:52
  34.6 4.3 %collective-permute-start.4 = (f32[96,128]{1,0:T(8,128)S(1)}, f32[96,128]{1,0:T(8,128)S(1)}, u32[]{:S(2)}, u32[]{:S(2)}) collective-permute-start(f32[96,128]{1,0:T(8,128)S(1)} %add_add_fusion.5), channel_id=1, source_target_pairs={{0,96},{1,25},{2,98},{3,27},{4,100},{5,29},{6,102},{7,31},{8,104},... | collective-permute-start | bytes 147464 | tf_op jit(solution)/shard_map/ppermute | solution.py:52
  38.9 5.5 %collective-permute-start.5 = (f32[96,128]{1,0:T(8,128)S(1)}, f32[96,128]{1,0:T(8,128)S(1)}, u32[]{:S(2)}, u32[]{:S(2)}) collective-permute-start(f32[96,128]{1,0:T(8,128)S(1)} %add.132), channel_id=1, source_target_pairs={{0,8},{1,33},{2,10},{3,35},{4,12},{5,37},{6,14},{7,39},{8,0},{9,41... | collective-permute-start | bytes 147464 | tf_op jit(solution)/shard_map/ppermute | solution.py:52
  44.4 5.1 %collective-permute-start.6 = (f32[96,128]{1,0:T(8,128)S(1)}, f32[96,128]{1,0:T(8,128)S(1)}, u32[]{:S(2)}, u32[]{:S(2)}) collective-permute-start(f32[96,128]{1,0:T(8,128)S(1)} %add.133), channel_id=1, source_target_pairs={{0,24},{1,97},{2,26},{3,99},{4,28},{5,101},{6,30},{7,103},{8,16},{... | collective-permute-start | bytes 147464 | tf_op jit(solution)/shard_map/ppermute | solution.py:52
  49.6 3.0 %collective-permute-start.7 = (f32[96,128]{1,0:T(8,128)S(1)}, f32[96,128]{1,0:T(8,128)S(1)}, u32[]{:S(2)}, u32[]{:S(2)}) collective-permute-start(f32[96,128]{1,0:T(8,128)S(1)} %add.134), channel_id=1, source_target_pairs={{0,2},{1,3},{2,0},{3,1},{4,6},{5,7},{6,4},{7,5},{8,10},{9,11},{10,... | collective-permute-start | bytes 147464 | tf_op jit(solution)/shard_map/ppermute | solution.py:52
  52.6 4.2 %collective-permute-start.8 = (f32[96,128]{1,0:T(8,128)S(1)}, f32[96,128]{1,0:T(8,128)S(1)}, u32[]{:S(2)}, u32[]{:S(2)}) collective-permute-start(f32[96,128]{1,0:T(8,128)S(1)} %add.135), channel_id=1, source_target_pairs={{0,6},{1,7},{2,4},{3,5},{4,2},{5,3},{6,0},{7,1},{8,14},{9,15},{10,... | collective-permute-start | bytes 147464 | tf_op jit(solution)/shard_map/ppermute | solution.py:52
  56.8 8.0 %collective-permute-start.9 = (f32[96,128]{1,0:T(8,128)S(1)}, f32[96,128]{1,0:T(8,128)S(1)}, u32[]{:S(2)}, u32[]{:S(2)}) collective-permute-start(f32[96,128]{1,0:T(8,128)S(1)} %add.136.mine), channel_id=1, source_target_pairs={{0,1},{1,0},{2,3},{3,2},{4,5},{5,4},{6,7},{7,6},{8,9},{9,8},{10,11... | collective-permute-start | bytes 147464 | tf_op jit(solution)/shard_map/ppermute | solution.py:58
  67.8 9.1 %collective-permute-start.11 = (bf16[64,3072]{1,0:T(8,128)(2,1)S(1)}, bf16[64,3072]{1,0:T(8,128)(2,1)S(1)}, u32[]{:S(2)}, u32[]{:S(2)}) collective-permute-start(bf16[64,3072]{1,0:T(8,128)(2,1)S(1)} %get-tuple-element.40.own), channel_id=1, source_target_pairs={{1,2},{3,4},{5,6},{7,8},{9,10},{11,12},{13,14},{15,16},{17,18},{19... | collective-permute-start | bytes 1179656 | tf_op jit(solution)/shard_map/ppermute | solution.py:63
  69.8 7.2 %collective-permute-start.10 = (bf16[64,3072]{1,0:T(8,128)(2,1)S(1)}, bf16[64,3072]{1,0:T(8,128)(2,1)S(1)}, u32[]{:S(2)}, u32[]{:S(2)}) collective-permute-start(bf16[64,3072]{1,0:T(8,128)(2,1)S(1)} %get-tuple-element.40.own), channel_id=1, source_target_pairs={{0,1},{1,0},{2,3},{3,2},{4,5},{5,4},{6,7},{7,6},{8,9},{9,8},{10,11... | collective-permute-start | bytes 1179656 | tf_op jit(solution)/shard_map/ppermute | solution.py:64
  85.5 1.3 %collective-permute-start.12 = (f32[96,128]{1,0:T(8,128)S(1)}, f32[96,128]{1,0:T(8,128)S(1)}, u32[]{:S(2)}, u32[]{:S(2)}) collective-permute-start(f32[96,128]{1,0:T(8,128)S(1)} %get-tuple-element.47), channel_id=1, source_target_pairs={{0,1},{1,0},{2,3},{3,2},{4,5},{5,4},{6,7},{7,6},{8,9},{9,8},{10,11... | collective-permute-start | bytes 147464 | tf_op jit(solution)/shard_map/ppermute | solution.py:49
  86.8 3.0 %collective-permute-start.13 = (f32[96,128]{1,0:T(8,128)S(1)}, f32[96,128]{1,0:T(8,128)S(1)}, u32[]{:S(2)}, u32[]{:S(2)}) collective-permute-start(f32[96,128]{1,0:T(8,128)S(1)} %add.137.sent), channel_id=1, source_target_pairs={{0,32},{1,9},{2,34},{3,11},{4,36},{5,13},{6,38},{7,15},{8,40},{9,1... | collective-permute-start | bytes 147464 | tf_op jit(solution)/shard_map/ppermute | solution.py:52
  89.8 4.6 %collective-permute-start.14 = (f32[96,128]{1,0:T(8,128)S(1)}, f32[96,128]{1,0:T(8,128)S(1)}, u32[]{:S(2)}, u32[]{:S(2)}) collective-permute-start(f32[96,128]{1,0:T(8,128)S(1)} %add_add_fusion.4.sent), channel_id=1, source_target_pairs={{0,96},{1,25},{2,98},{3,27},{4,100},{5,29},{6,102},{7,31},{8,104},... | collective-permute-start | bytes 147464 | tf_op jit(solution)/shard_map/ppermute | solution.py:52
  94.5 5.1 %collective-permute-start.15 = (f32[96,128]{1,0:T(8,128)S(1)}, f32[96,128]{1,0:T(8,128)S(1)}, u32[]{:S(2)}, u32[]{:S(2)}) collective-permute-start(f32[96,128]{1,0:T(8,128)S(1)} %add_add_fusion.3.sent), channel_id=1, source_target_pairs={{0,8},{1,33},{2,10},{3,35},{4,12},{5,37},{6,14},{7,39},{8,0},{9,41... | collective-permute-start | bytes 147464 | tf_op jit(solution)/shard_map/ppermute | solution.py:52
  99.6 6.3 %collective-permute-start.16 = (f32[96,128]{1,0:T(8,128)S(1)}, f32[96,128]{1,0:T(8,128)S(1)}, u32[]{:S(2)}, u32[]{:S(2)}) collective-permute-start(f32[96,128]{1,0:T(8,128)S(1)} %add_add_fusion.2.sent), channel_id=1, source_target_pairs={{0,24},{1,97},{2,26},{3,99},{4,28},{5,101},{6,30},{7,103},{8,16},{... | collective-permute-start | bytes 147464 | tf_op jit(solution)/shard_map/ppermute | solution.py:52
  105.9 3.0 %collective-permute-start.17 = (f32[96,128]{1,0:T(8,128)S(1)}, f32[96,128]{1,0:T(8,128)S(1)}, u32[]{:S(2)}, u32[]{:S(2)}) collective-permute-start(f32[96,128]{1,0:T(8,128)S(1)} %add_add_fusion.1.sent), channel_id=1, source_target_pairs={{0,2},{1,3},{2,0},{3,1},{4,6},{5,7},{6,4},{7,5},{8,10},{9,11},{10,... | collective-permute-start | bytes 147464 | tf_op jit(solution)/shard_map/ppermute | solution.py:52
  109.0 4.2 %collective-permute-start.18 = (f32[96,128]{1,0:T(8,128)S(1)}, f32[96,128]{1,0:T(8,128)S(1)}, u32[]{:S(2)}, u32[]{:S(2)}) collective-permute-start(f32[96,128]{1,0:T(8,128)S(1)} %add_add_fusion), channel_id=1, source_target_pairs={{0,6},{1,7},{2,4},{3,5},{4,2},{5,3},{6,0},{7,1},{8,14},{9,15},{10,... | collective-permute-start | bytes 147464 | tf_op jit(solution)/shard_map/ppermute | solution.py:52
  113.2 7.8 %collective-permute-start.19 = (f32[96,128]{1,0:T(8,128)S(1)}, f32[96,128]{1,0:T(8,128)S(1)}, u32[]{:S(2)}, u32[]{:S(2)}) collective-permute-start(f32[96,128]{1,0:T(8,128)S(1)} %add.158.mine), channel_id=1, source_target_pairs={{0,1},{1,0},{2,3},{3,2},{4,5},{5,4},{6,7},{7,6},{8,9},{9,8},{10,11... | collective-permute-start | bytes 147464 | tf_op jit(solution)/shard_map/ppermute | solution.py:58
